TPU v7x, 32 devices: a whole 2x2x4 slice. The times are simulated.
32 devices in a mesh: dp: 16 (over z, y, x), chan: 2 (over core).
Axes of the slice: x: 2, y: 2, z: 4, core: 2. Of those that a mesh axis runs over, the one named last changes fastest.
Arguments:
- counts: int32 [16], P('dp'), may hold values from 1 to 2, as said below
- features_in: bfloat16 [32, 16, 16, 512], P('dp', None, None, 'chan'), may hold values from -6 to 6
- rgb_in: float32 [32, 3, 16, 16], P('dp'), may hold values from -6 to 6
- latent: bfloat16 [32, 512], P('dp'), may hold values from -6 to 6
- affine_one: bfloat16 [512, 512], P(None, 'chan'), may hold values from -0.25 to 0.25
- affine_bias_one: float32 [512], P('chan'), may hold values from 0.5 to 1.5
- affine_two: bfloat16 [512, 512], P(None, 'chan'), may hold values from -0.25 to 0.25
- affine_bias_two: float32 [512], P('chan'), may hold values from 0.5 to 1.5
- affine_three: bfloat16 [512, 512], P(None, 'chan'), may hold values from -0.25 to 0.25
- affine_bias_three: float32 [512], P('chan'), may hold values from 0.5 to 1.5
- kernel_one: bfloat16 [3, 3, 512, 512], P(None, None, 'chan'), may hold values from -0.09375 to 0.09375
- bias_one: float32 [512], P('chan'), may hold values from -2 to 2
- kernel_two: bfloat16 [3, 3, 512, 512], P(None, None, 'chan'), may hold values from -0.09375 to 0.09375
- bias_two: float32 [512], P('chan'), may hold values from -2 to 2
- rgb_weight: bfloat16 [3, 512], P(None, 'chan'), may hold values from -0.25 to 0.25
- rgb_bias: float32 [3], replicated, may hold values from -2 to 2
- noise_gain: float32 [2], replicated, may hold values from 0.3 to 1
- noise_one: float32 [32, 32, 32], P('dp'), may hold values from -6 to 6
- noise_two: float32 [32, 32, 32], P('dp'), may hold values from -6 to 6
- grad_features: bfloat16 [32, 32, 32, 512], P('dp', None, None, 'chan'), may hold values from -6 to 6
- grad_rgb: bfloat16 [32, 3, 32, 32], P('dp'), may hold values from -6 to 6
Outputs:
- features_out: bfloat16 [32, 32, 32, 512], P('dp', None, None, 'chan')
- rgb_out: float32 [32, 3, 32, 32], P('dp')
- grad_features_in: float32 [32, 16, 16, 512], P('dp', None, None, 'chan')
- grad_rgb_in: float32 [32, 3, 16, 16], P('dp')
- grad_latent: float32 [32, 512], P('dp')
- grad_affine_one: float32 [512, 512], P(None, 'chan')
- grad_affine_bias_one: float32 [512], P('chan')
- grad_affine_two: float32 [512, 512], P(None, 'chan')
- grad_affine_bias_two: float32 [512], P('chan')
- grad_affine_three: float32 [512, 512], P(None, 'chan')
- grad_affine_bias_three: float32 [512], P('chan')
- grad_kernel_one: float32 [3, 3, 512, 512], P(None, None, 'chan')
- grad_bias_one: float32 [512], P('chan')
- grad_kernel_two: float32 [3, 3, 512, 512], P(None, None, 'chan')
- grad_bias_two: float32 [512], P('chan')
- grad_rgb_weight: float32 [3, 512], P(None, 'chan')
- grad_rgb_bias: float32 [3], replicated
- grad_noise_gain: float32 [2], replicated
- rms_values: float32 [3], replicated
Inputs may be any that keep to these rules, and one draw needn't show every extreme that they name: counts gives each index of dp its number of real images among its 2 slots; in every draw some index holds 2 and some other holds 1.
All inputs are finite; a program needn't handle non-finite values.
Results may differ from a plain program's by a relative error of at most 0.0058.
Values may be sent and summed in bfloat16 or wider, within the bound.
No kernel may reach another device: no remote copies, remote signals or barrier semaphores. Data moves between devices by JAX's collectives and lax.ppermute only.
A program may use at most 128 MiB of HBM per device.

v0:
```python
import functools

import jax
import jax.numpy as jnp
from jax import lax
from jax.experimental import pallas as pl
from jax.experimental.pallas import tpu as pltpu
from jax.sharding import Mesh, PartitionSpec as P

RES = 32
HALF = 16
PLANE = HALF * HALF
SQRT_TWO = 1.4142135623730951
EPSILON = 1e-08
STAGE = 60
DP = ("block", "far", "near", "y", "x")
SWAP = [(0, 1), (1, 0)]
F32 = jnp.float32
BF16 = jnp.bfloat16
VMEM_BYTES = 16 * 2**20
VMEM = pl.BlockSpec(memory_space=pltpu.VMEM)
SMEM = pl.BlockSpec(memory_space=pltpu.SMEM)
UP_TAPS = (((0, 1),), ((0, 0), (1, 2)))


def dot(left, right, left_dim, right_dim):
    return lax.dot_general(
        left, right, (((left_dim,), (right_dim,)), ((), ())), preferred_element_type=F32
    )


def exact(left, right, left_dim, right_dim):
    return lax.dot_general(
        left,
        right,
        (((left_dim,), (right_dim,)), ((), ())),
        precision=lax.Precision.HIGHEST,
        preferred_element_type=F32,
    )


def source(parity, tap):
    return (parity + tap - 1) & 1, (parity + tap - 1) >> 1


def each(count, body):
    lax.fori_loop(0, count, lambda index, carry: (body(index), carry)[1], 0)


def row_of(ref, index):
    return ref[pl.ds(index, 1), :]


def rows_at(index, count):
    return pl.ds(pl.multiple_of(index * count, count), count)


def rows_from(values, shift):
    if shift == 0:
        return values
    blank = jnp.zeros((HALF, values.shape[1]), values.dtype)
    if shift == 1:
        return jnp.concatenate([values[HALF:], blank], 0)
    return jnp.concatenate([blank, values[:-HALF]], 0)


def columns_from(values, shift):
    if shift == 0:
        return values
    moved = pltpu.roll(values, (-shift) % values.shape[0], 0)
    column = lax.broadcasted_iota(jnp.int32, values.shape, 0) % HALF
    return jnp.where(column == (HALF - 1 if shift == 1 else 0), 0.0, moved)


def gather_terms(terms):
    total = None
    for shift, group in terms.items():
        part = None
        for left, right, right_dim in group:
            product = dot(left, right, 1, right_dim)
            part = product if part is None else part + product
        part = columns_from(part, shift)
        total = part if total is None else total + part
    return total


def split_three(values):
    high = values.astype(BF16)
    rest = values - high.astype(F32)
    middle = rest.astype(BF16)
    low = (rest - middle.astype(F32)).astype(BF16)
    return high, middle, low


def fetch(place, kernel, out, sem):
    share = out.shape[2]
    return pltpu.make_async_copy(kernel.at[:, :, rows_at(1 - place[2], share)], out, sem)


def style_kernel(
    place, kernel, latent, a1, b1, a2, b2, a3, b3, features, styles, scaled, send, sem
):
    fetch(place, kernel, send, sem).start()
    for index, (affine, bias) in enumerate(((a1, b1), (a2, b2), (a3, b3))):
        styles[index] = dot(latent[...], affine[...], 1, 0) + bias[...]
    for image in range(features.shape[0]):
        row = styles[0, image : image + 1, :]
        scaled[image] = (features[image].astype(F32) * row).astype(BF16)
    fetch(place, kernel, send, sem).wait()


def pixel_planes(rasters):
    count = len(rasters)
    stacked = jnp.concatenate(rasters, 0)
    lane = lax.broadcasted_iota(jnp.int32, (RES, PLANE), 1)
    line = lax.broadcasted_iota(jnp.int32, (RES, PLANE), 0)
    found = [[None] * 4 for _ in range(count)]
    for qx in range(2):
        choose = jnp.where(line == 2 * (lane % HALF) + qx, 1.0, 0.0).astype(BF16)
        spread_out = dot(stacked, choose, 1, 0)
        for qy in range(2):
            mask = jnp.where(line == 2 * (lane // HALF) + qy, 1.0, 0.0)
            for index in range(count):
                block = spread_out[RES * index : RES * (index + 1)]
                found[index][2 * qy + qx] = jnp.sum(block * mask, axis=0, keepdims=True)
    return found


def planes_kernel(
    place,
    valid,
    gain,
    kernel,
    noise_one,
    noise_two,
    grad_rgb,
    planes_one,
    planes_two,
    colours,
    send,
    sem,
):
    fetch(place, kernel, send, sem).start()
    images = noise_one.shape[0]
    ones = jnp.ones((3, PLANE), F32)
    blank = jnp.zeros((7, PLANE), F32)
    for image in range(images):
        rasters = []
        for index, noise in enumerate((noise_one, noise_two)):
            value = noise[image]
            rasters += list(split_three(value)) + list(split_three(value * gain[:, index : index + 1]))
        keep = valid[image : image + 1, :RES]
        for colour in range(3):
            rasters.append((grad_rgb[image, colour].astype(F32) * keep).astype(BF16))
        found = pixel_planes(rasters)
        for plane in range(4):
            rows = [member[plane] for member in found]
            planes_one[image, plane] = jnp.concatenate(rows[:6] + [ones, blank], 0).astype(BF16)
            planes_two[image, plane] = jnp.concatenate(rows[6:12] + [ones, blank], 0).astype(BF16)
            colours[image, plane] = jnp.concatenate(rows[12:] * 3 + [blank], 0).astype(BF16)
    fetch(place, kernel, send, sem).wait()


def squares_kernel(
    place, styles, kernel, bias, rgb, squares, mine, theirs, add, colour, parts, *, layer
):
    total = None
    for tap in range(kernel.shape[0]):
        value = kernel[tap].astype(F32)
        total = value * value if total is None else total + value * value
    squares[...] = total
    style = styles[layer]
    parts[...] = lax.dot_general(
        style * style,
        total,
        (((1,), (0,)), ((), ())),
        precision=lax.Precision.HIGHEST,
        preferred_element_type=F32,
    )
    share = bias.shape[1]
    mine[...] = parts[:, pl.ds(pl.multiple_of(place[2] * share, share), share)]
    theirs[...] = parts[:, pl.ds(pl.multiple_of((1 - place[2]) * share, share), share)]
    add[...] = jnp.concatenate(
        [jnp.zeros((3, share), F32), jnp.full((3, share), 0.5, F32)]
        + [part.astype(F32) for part in split_three(0.5 * bias[...])]
        + [jnp.zeros((7, share), F32)],
        0,
    ).astype(BF16)
    for image in range(styles.shape[1]):
        weight = rgb[...].astype(F32) * styles[2, image : image + 1, :]
        colour[image] = jnp.concatenate(
            [part.astype(F32) for part in split_three(weight)] + [jnp.zeros((7, share), F32)], 0
        ).astype(BF16)


def scale_half(rows, add, image, plane, demod, weights):
    return rows * (0.5 * demod) + dot(add[image, plane], weights, 0, 0)


def smooth_leaky(half_pre):
    size = jnp.abs(half_pre)
    soft = jnp.maximum(half_pre, 0.0) * 2.0 + jnp.log(1.0 + jnp.exp(-2.0 * size))
    return (0.4 * SQRT_TWO) * half_pre + (0.8 * SQRT_TWO) * soft


def leaky_slope(half_pre):
    return (0.6 * SQRT_TWO) + (0.4 * SQRT_TWO) * jnp.tanh(half_pre)


def column_sum(values):
    return jnp.sum(values, axis=0, keepdims=True)


def square_grad(products, demod):
    return -0.5 * products * demod * demod


def conv_one_kernel(
    place,
    own,
    other,
    k_own,
    k_other,
    sums_own,
    sums_other,
    add,
    weights,
    styles,
    conv,
    scaled,
    demod,
):
    share = own.shape[-1]
    columns = pl.ds(pl.multiple_of(place[2] * share, share), share)
    demod[...] = lax.rsqrt(sums_own[...] + sums_other[...] + EPSILON)
    for qy in range(2):
        for qx in range(2):
            plane = 2 * qy + qx
            terms = {}
            for shift_y, tap_y in UP_TAPS[qy]:
                for shift_x, tap_x in UP_TAPS[qx]:
                    tap = 3 * tap_y + tap_x
                    for source_ref, right in (
                        (own, k_own[tap, :, columns]),
                        (other, k_other[tap]),
                    ):
                        left = jnp.concatenate(
                            [rows_from(source_ref[b], shift_y) for b in range(own.shape[0])], 0
                        )
                        terms.setdefault(shift_x, []).append((left, right, 0))
            total = gather_terms(terms)
            for image in range(own.shape[0]):
                rows = total[image * PLANE : (image + 1) * PLANE]
                conv[image, plane] = rows
                half_pre = scale_half(
                    rows, add, image, plane, demod[image : image + 1, :], weights[...]
                )
                act = smooth_leaky(half_pre)
                scaled[image, plane] = (act * styles[1, image : image + 1, :]).astype(BF16)


def spread(raster, image, wide):
    for block in range(wide.shape[0]):
        lanes = raster[image, :, :, block * 128 : (block + 1) * 128]
        wide[block] = lanes.reshape(wide.shape[1:]).astype(F32)


def read_plane(wide, qy, qx):
    cells = [wide[block, :, qy, pl.ds(qx, HALF, stride=2), :] for block in range(wide.shape[0])]
    return jnp.concatenate([cell.reshape(PLANE, 128) for cell in cells], 1)


def write_plane(wide, qy, qx, values):
    for block in range(wide.shape[0]):
        cell = values[:, block * 128 : (block + 1) * 128].reshape(HALF, HALF, 128)
        wide[block, :, qy, pl.ds(qx, HALF, stride=2), :] = cell


def store_raster(wide, out, image):
    for block in range(wide.shape[0]):
        lanes = wide[block].reshape(RES, RES, 128)
        out[image, :, :, block * 128 : (block + 1) * 128] = lanes.astype(out.dtype)


def conv_two_kernel(
    place,
    own,
    other,
    k_own,
    k_other,
    sums_own,
    sums_other,
    valid,
    add,
    weights,
    colours,
    colour_weights,
    cotangent,
    conv,
    grad_conv,
    demod,
    square,
    wide,
):
    share = own.shape[-1]
    columns = pl.ds(pl.multiple_of(place[2] * share, share), share)
    demod[...] = lax.rsqrt(sums_own[...] + sums_other[...] + EPSILON)

    def one(image):
        spread(cotangent, image, wide)
        products = None
        for qy in range(2):
            for qx in range(2):
                plane = 2 * qy + qx
                terms = {}
                for tap_x in range(3):
                    px, shift_x = source(qx, tap_x)
                    for tap_y in range(3):
                        py, shift_y = source(qy, tap_y)
                        tap = 3 * tap_y + tap_x
                        for source_ref, right in (
                            (own, k_own[tap, :, columns]),
                            (other, k_other[tap]),
                        ):
                            left = rows_from(source_ref[image, 2 * py + px], shift_y)
                            terms.setdefault(shift_x, []).append((left, right, 0))
                rows = gather_terms(terms)
                conv[image, plane] = rows
                half_pre = scale_half(
                    rows, add, image, plane, row_of(demod, image), weights[...]
                )
                grad = read_plane(wide, qy, qx) + dot(colours[image, plane], colour_weights[image], 0, 0)
                row = row_of(demod, image) * row_of(valid, image)
                grad = grad * leaky_slope(half_pre) * row
                grad_conv[image, plane] = grad.astype(BF16)
                product = column_sum(grad * rows)
                products = product if products is None else products + product
        square[pl.ds(image, 1), :] = square_grad(products, row_of(demod, image))

    each(own.shape[0], one)


def add_term(total, place, axis, kernel, tap, column, terms, outs):
    at = tap
    while at >= outs[0].shape[0]:
        at, outs = at - outs[0].shape[0], outs[4:]
    send, keep = outs[2 * axis : 2 * axis + 2]
    half, share = send.shape[1], send.shape[2]
    columns = rows_at(column, share)
    for start, index, out in ((0, 1 - place[axis], send), (half, place[axis], keep)):
        weight = kernel[tap, rows_at(index, half), columns].astype(F32)
        value = total[start : start + half] + weight * terms[start : start + half]
        out[at] = value.astype(out.dtype)


def square_terms(place, axis, squared, grads):
    half = squared.shape[1] // 2
    rows = [squared[:, rows_at(1 - place[axis], half)], squared[:, rows_at(place[axis], half)]]
    return 2.0 * exact(jnp.concatenate(rows, 1), grads[...], 0, 0)


def shifted_kernel(scaled, moved):
    def one(image):
        for plane in range(scaled.shape[1]):
            value = scaled[image, plane].astype(F32)
            moved[image, plane] = columns_from(value, 1 if plane % 2 == 0 else -1).astype(BF16)

    each(scaled.shape[0], one)


def kernel_two_grad(
    place,
    scaled,
    moved,
    g_own,
    g_other,
    kernel,
    styles,
    q_own,
    q_other,
    *refs,
):
    outs, squared = refs[:-1], refs[-1]
    half = scaled.shape[3] // 2
    squared[...] = styles[1] * styles[1]
    for axis, column, grads, squares in (
        (0, place[2], g_own, q_own),
        (1, 1 - place[2], g_other, q_other),
    ):
        terms = square_terms(place, axis, squared, squares)
        lanes = (rows_at(1 - place[axis], half), rows_at(place[axis], half))
        for tap_y in range(3):
            for tap_x in range(3):
                left, right = [], []
                for image in range(scaled.shape[0]):
                    for qy in range(2):
                        for qx in range(2):
                            py, shift_y = source(qy, tap_y)
                            px, shift_x = source(qx, tap_x)
                            ref = scaled if shift_x == 0 else moved
                            value = jnp.concatenate(
                                [ref[image, 2 * py + px, :, at] for at in lanes], 1
                            )
                            left.append(rows_from(value, shift_y))
                            right.append(grads[image, 2 * qy + qx])
                total = dot(jnp.concatenate(left, 0), jnp.concatenate(right, 0), 0, 0)
                tap = 3 * tap_y + tap_x
                add_term(total, place, axis, kernel, tap, column, terms, outs)


def kernel_one_grad(
    place,
    scaled,
    g_own,
    g_other,
    kernel,
    styles,
    q_own,
    q_other,
    *refs,
):
    outs, (moved, squared) = refs[:-2], refs[-2:]
    half = scaled.shape[2] // 2
    images = scaled.shape[0]
    for image in range(images):
        moved[image] = columns_from(scaled[image].astype(F32), 1).astype(BF16)
    squared[...] = styles[0] * styles[0]
    for axis, column, grads, squares in (
        (0, place[2], g_own, q_own),
        (1, 1 - place[2], g_other, q_other),
    ):
        terms = square_terms(place, axis, squared, squares)
        lanes = (rows_at(1 - place[axis], half), rows_at(place[axis], half))
        for qy in range(2):
            for qx in range(2):
                right = jnp.concatenate([grads[b, 2 * qy + qx] for b in range(images)], 0)
                for shift_y, tap_y in UP_TAPS[qy]:
                    for shift_x, tap_x in UP_TAPS[qx]:
                        ref = moved if shift_x else scaled
                        left = [
                            rows_from(jnp.concatenate([ref[b, :, at] for at in lanes], 1), shift_y)
                            for b in range(images)
                        ]
                        total = dot(jnp.concatenate(left, 0), right, 0, 0)
                        tap = 3 * tap_y + tap_x
                        add_term(total, place, axis, kernel, tap, column, terms, outs)


def input_two_grad(
    place,
    g_own,
    g_other,
    kernel,
    conv,
    demod,
    add,
    weights,
    styles,
    grad_scaled,
    grad_conv,
    square,
):
    share = g_own.shape[3]
    mine = pl.multiple_of(place[2] * share, share)
    theirs = pl.multiple_of((1 - place[2]) * share, share)

    def one(image):
        products = None
        for py in range(2):
            for px in range(2):
                plane = 2 * py + px
                terms = {}
                for tap_x in range(3):
                    qx = (px - tap_x + 1) & 1
                    shift_x = source(qx, tap_x)[1]
                    for tap_y in range(3):
                        qy = (py - tap_y + 1) & 1
                        shift_y = source(qy, tap_y)[1]
                        tap = 3 * tap_y + tap_x
                        for grads, start in ((g_own, mine), (g_other, theirs)):
                            left = rows_from(grads[image, 2 * qy + qx], -shift_y)
                            right = kernel[tap, :, pl.ds(start, share)]
                            terms.setdefault(-shift_x, []).append((left, right, 1))
                rows = gather_terms(terms)
                grad_scaled[image, plane] = rows
                values = conv[image, plane]
                half_pre = scale_half(
                    values,
                    add,
                    image,
                    plane,
                    row_of(demod, image),
                    weights[...],
                )
                row = row_of(demod, image) * row_of(styles.at[1], image)
                grad = rows * leaky_slope(half_pre) * row
                grad_conv[image, plane] = grad.astype(BF16)
                product = column_sum(grad * values)
                products = product if products is None else products + product
        square[pl.ds(image, 1), :] = square_grad(products, row_of(demod, image))

    each(g_own.shape[0], one)


def input_one_grad(
    place, g_own, g_other, kernel, features, styles, grad_features, sums
):
    share = g_own.shape[3]
    mine = pl.multiple_of(place[2] * share, share)
    theirs = pl.multiple_of((1 - place[2]) * share, share)
    images = g_own.shape[0]
    terms = {}
    for qy in range(2):
        for qx in range(2):
            for shift_y, tap_y in UP_TAPS[qy]:
                for shift_x, tap_x in UP_TAPS[qx]:
                    tap = 3 * tap_y + tap_x
                    for grads, start in ((g_own, mine), (g_other, theirs)):
                        left = jnp.concatenate(
                            [rows_from(grads[b, 2 * qy + qx], -shift_y) for b in range(images)], 0
                        )
                        right = kernel[tap, :, pl.ds(start, share)]
                        terms.setdefault(-shift_x, []).append((left, right, 1))
    total = gather_terms(terms)
    for image in range(images):
        rows = total[image * PLANE : (image + 1) * PLANE]
        grad_features[image] = rows * styles[0, image : image + 1, :]
        product = rows * features[image].astype(F32)
        sums[image : image + 1, :] = jnp.sum(product, axis=0, keepdims=True)


def noise_rows(add, image, plane, share):
    pick = lax.broadcasted_iota(jnp.int32, (add.shape[2], share), 0) < 3
    return dot(add[image, plane], jnp.where(pick, 1.0, 0.0).astype(BF16), 0, 0)


def point_sums(image, totals, out):
    for row, total in enumerate(totals):
        out[image, row : row + 1, :] = total
    out[image, len(totals) :, :] = jnp.zeros((8 - len(totals), out.shape[2]), F32)


def outputs_two_kernel(
    conv,
    demod,
    valid,
    add,
    weights,
    colours,
    cotangent,
    styles,
    rgb,
    features_out,
    rgb_rows,
    rgb_grad,
    sums,
    wide,
):
    share = conv.shape[3]
    rgb_grad[...] = jnp.zeros_like(rgb_grad)

    def one(image):
        spread(cotangent, image, wide)
        totals = None
        for plane in range(4):
            qy, qx = plane // 2, plane % 2
            rows = conv[image, plane]
            half_pre = scale_half(rows, add, image, plane, row_of(demod, image), weights[...])
            act = smooth_leaky(half_pre)
            style = row_of(styles.at[2], image)
            keep = row_of(valid, image)
            from_rgb = dot(colours[image, plane], rgb[...], 0, 0)
            grad = (read_plane(wide, qy, qx) + from_rgb * style) * keep * leaky_slope(half_pre)
            write_plane(wide, qy, qx, act * keep)
            to_rgb = (act * style).astype(BF16)
            rgb_rows[image, plane] = dot(rgb[...], to_rgb, 1, 1)[:8]
            rgb_grad[...] += dot(colours[image, plane], to_rgb, 1, 0)
            own = [
                column_sum(grad),
                column_sum(grad * noise_rows(add, image, plane, share)),
                column_sum(from_rgb * act),
                column_sum(act * act) * keep,
            ]
            totals = own if totals is None else [a + b for a, b in zip(totals, own)]
        store_raster(wide, features_out, image)
        point_sums(image, totals, sums)

    each(conv.shape[0], one)


def outputs_one_kernel(
    conv, grad_scaled, demod, valid, add, weights, styles, sums
):
    share = conv.shape[3]

    def one(image):
        totals = None
        for plane in range(4):
            rows = conv[image, plane]
            half_pre = scale_half(rows, add, image, plane, row_of(demod, image), weights[...])
            act = smooth_leaky(half_pre)
            back = grad_scaled[image, plane]
            grad = back * row_of(styles.at[1], image) * leaky_slope(half_pre)
            own = [
                column_sum(grad),
                column_sum(grad * noise_rows(add, image, plane, share)),
                column_sum(back * act),
                column_sum(act * act) * row_of(valid, image),
            ]
            totals = own if totals is None else [a + b for a, b in zip(totals, own)]
        point_sums(image, totals, sums)

    each(conv.shape[0], one)


def upsampling(rows, cols):
    line = lax.broadcasted_iota(jnp.int32, (rows, cols), 0)
    column = lax.broadcasted_iota(jnp.int32, (rows, cols), 1)
    centre, near = line // 2, line // 2 + 2 * (line % 2) - 1
    return jnp.where(column == centre, 0.75, 0.0) + jnp.where(column == near, 0.25, 0.0)


def rgb_kernel(valid, bias, own, other, rgb_in, grad_rgb, rgb_out, grad_in, sums, raster):
    images = rgb_in.shape[0]
    double = upsampling(RES, HALF)
    lane = lax.broadcasted_iota(jnp.int32, (HALF, PLANE), 1)
    line = lax.broadcasted_iota(jnp.int32, (HALF, PLANE), 0)
    mask = jnp.where(lane // HALF == line, 1.0, 0.0)
    for qx in range(2):
        pixel = lax.broadcasted_iota(jnp.int32, (PLANE, 128), 0) % HALF
        column = lax.broadcasted_iota(jnp.int32, (PLANE, 128), 1)
        choose = jnp.where(column == 2 * pixel + qx, 1.0, 0.0)
        for qy in range(2):
            plane = 2 * qy + qx
            rows = []
            for image in range(images):
                both = own[image, plane] + other[image, plane]
                rows += [mask * both[colour : colour + 1] for colour in range(3)]
            found = exact(jnp.concatenate(rows, 0), choose, 1, 0)
            for index in range(3 * images):
                cell = found[HALF * index : HALF * (index + 1)]
                place = (index, pl.ds(qy, HALF, stride=2), slice(None))
                raster[place] = cell if qx == 0 else raster[place] + cell
    squares = jnp.zeros((1, 1), F32)
    biases = [jnp.zeros((1, 1), F32) for _ in range(3)]
    for image in range(images):
        keep = valid[image : image + 1, :RES]
        for colour in range(3):
            skip = exact(exact(double, rgb_in[image, colour], 1, 0), double, 1, 1)
            value = (skip + raster[3 * image + colour, :, :RES]) + bias[:, colour : colour + 1]
            value = value * keep
            rgb_out[image, colour] = value
            squares = squares + jnp.sum(value * value, keepdims=True)
            grad = grad_rgb[image, colour].astype(F32) * keep
            grad_in[image, colour] = exact(exact(double, grad, 0, 0), double, 1, 0)
            biases[colour] = biases[colour] + jnp.sum(grad, keepdims=True)
    sums[...] = jnp.concatenate(
        [jnp.broadcast_to(member, (1, 128)) for member in [squares] + biases]
        + [jnp.zeros((4, 128), F32)],
        0,
    )


def style_grads_kernel(
    place,
    own_one,
    other_one,
    own_two,
    other_two,
    squares_one,
    squares_two,
    styles,
    style_sums,
    sums_one,
    sums_two,
    a1,
    a2,
    a3,
    grads,
    crossing,
):
    images, share = style_sums.shape
    mine, theirs = rows_at(place[2], share), rows_at(1 - place[2], share)
    rows = []
    for layer, (own, other, squares, sums) in enumerate(
        ((own_one, other_one, squares_one, style_sums), (own_two, other_two, squares_two, None))
    ):
        back = exact(own[...], squares[:, mine], 1, 1) + exact(
            other[...], squares[:, theirs], 1, 1
        )
        if sums is None:
            direct = jnp.concatenate([sums_one[b, 2:3, :] for b in range(images)], 0)
        else:
            direct = sums[...]
        rows.append(direct + 2.0 * styles[layer] * back)
    rows.append(jnp.concatenate([sums_two[b, 2:3, :] for b in range(images)], 0))
    grads[...] = jnp.concatenate(rows, 0)
    latent = None
    for row, affine in zip(rows, (a1, a2, a3)):
        part = exact(row, affine[...].astype(F32), 1, 1)
        latent = part if latent is None else latent + part
    lane = lax.broadcasted_iota(jnp.int32, (1, share), 1)
    scalars = jnp.zeros((1, share), F32)
    for index, (sums, row) in enumerate(
        ((sums_one, 3), (sums_two, 3), (sums_one, 1), (sums_two, 1))
    ):
        total = sums[0, row : row + 1, :]
        for image in range(1, images):
            total = total + sums[image, row : row + 1, :]
        scalars = scalars + jnp.where(lane == index, jnp.sum(total, keepdims=True), 0.0)
    pieces = [latent[b : b + 1, h * share : (h + 1) * share] for b in range(images) for h in (0, 1)]
    blank = jnp.zeros((crossing.shape[0] - len(pieces) - 1, share), F32)
    crossing[...] = jnp.concatenate(pieces + [scalars, blank], 0)


def pack_kernel(
    valid,
    own,
    other,
    grads,
    latent,
    sums_one,
    sums_two,
    rgb_grad,
    rgb_sums,
    grad_latent,
    pack,
):
    images, share = latent.shape[0], grads.shape[1]
    total = own[...] + other[...]
    count = 2 * images
    for image in range(images):
        grad_latent[image : image + 1, :] = jnp.concatenate(
            [total[2 * image : 2 * image + 1], total[2 * image + 1 : 2 * image + 2]], 1
        )
    values = latent[...].astype(F32)
    rows = [values[:, :share], values[:, share:], grads[...]]
    for sums in (sums_one, sums_two):
        bias = sums[0, 0:1, :]
        for image in range(1, images):
            bias = bias + sums[image, 0:1, :]
        rows.append(bias)
    rows.append(rgb_grad[:3, :])
    lane = lax.broadcasted_iota(jnp.int32, (1, share), 1)
    scalars = total[count : count + 1]
    wide = jnp.concatenate([rgb_sums[...]] * (share // 128), 1)
    for index in range(4):
        scalars = scalars + jnp.where(lane == 4 + index, wide[index : index + 1], 0.0)
    for image in range(images):
        scalars = scalars + jnp.where(lane == 8, valid[image : image + 1, :], 0.0)
    rows.append(scalars)
    used = sum(member.shape[0] for member in rows)
    if used < pack.shape[0]:
        rows.append(jnp.zeros((pack.shape[0] - used, share), F32))
    pack[...] = jnp.concatenate(rows, 0)


def spread_kernel(place, *refs, images):
    packs, outs, parts = refs[:-14], refs[-14:-1], refs[-1]
    grads, biases, points = outs[0:3], outs[3:6], outs[6:8]
    rgb_grad, gains, rms, rgb_bias, everything = outs[8:]
    if len(packs) == 1:
        everything[...] = packs[0][...]
    else:
        own, got_own, other, got_other = packs
        tap, rows = own.shape[0] - 1, everything.shape[1]
        for index in range(8):
            at = pl.ds(rows * index, rows)
            near, far, second = (index >> 1) & 1, index & 1, index >> 2
            line = 8 * far + 4 * near
            for own_ref, other_ref, first_x, first_y in (
                (own, other, place[0], place[1]),
                (got_own, got_other, 1 - place[0], 1 - place[1]),
            ):
                parts[0, line + 2 * second + first_x] = own_ref[tap, at, :].astype(F32)
                parts[1, line + 2 * first_y + second] = other_ref[tap, at, :].astype(F32)
        everything[...] = parts[0] + parts[1]
    count = everything.shape[0]

    def rows(start, size):
        return jnp.concatenate([everything[d, start : start + size, :] for d in range(count)], 0)

    latent = jnp.concatenate([rows(0, images), rows(images, images)], 1)
    at = 2 * images
    for layer in range(3):
        grad = rows(at, images)
        grads[layer][...] = exact(latent, grad, 0, 0)
        biases[layer][...] = jnp.sum(grad, axis=0, keepdims=True)
        at += images
    total = everything[0]
    for device in range(1, count):
        total = total + everything[device]
    points[0][...] = total[at : at + 1]
    points[1][...] = total[at + 1 : at + 2]
    rgb_grad[...] = total[at + 2 : at + 5]
    scalars = total[at + 5 : at + 6]
    lane = lax.broadcasted_iota(jnp.int32, scalars.shape, 1)

    def scalar(index):
        return jnp.sum(jnp.where(lane == index, scalars, 0.0))

    share = scalars.shape[1]
    real = jnp.sum(jnp.where(lane == 8, scalars, 0.0), keepdims=True)
    entries = jnp.where(lane == 4, 3.0 * RES * RES, 2.0 * share * RES * RES)
    roots = jnp.sqrt(scalars / (real * entries))

    def root(index):
        return jnp.sum(jnp.where(lane == index, roots, 0.0))

    for index, lane_at in enumerate((0, 1, 4)):
        rms[index] = root(lane_at)
    for index in range(2):
        gains[index] = scalar(2 + index)
    for index in range(3):
        rgb_bias[index] = scalar(5 + index)


def second_kernel(
    place, keep_own, got_own, keep_other, got_other, s_own, k_own, s_other, k_other
):
    count = s_own.shape[1]
    for axis, keep, got, send, kept in (
        (1, keep_own, got_own, s_own, k_own),
        (0, keep_other, got_other, s_other, k_other),
    ):
        away, here = rows_at(1 - place[axis], count), rows_at(place[axis], count)

        def one(tap, keep=keep, got=got, send=send, kept=kept, away=away, here=here):
            total = keep[tap, away, :] + got[tap, away, :].astype(F32)
            send[tap] = total.astype(BF16)
            kept[tap] = keep[tap, here, :] + got[tap, here, :].astype(F32)

        each(keep.shape[0], one)


def merge_kernel(place, keep_own, got_own, keep_other, got_other, send, keep):
    count = send.shape[2]
    away, here = rows_at(1 - place[3], count), rows_at(place[3], count)
    for order, (kept, got) in enumerate(((keep_own, got_own), (keep_other, got_other))):

        def one(tap, order=order, kept=kept, got=got):
            total = kept[tap, away, :] + got[tap, away, :].astype(F32)
            send[order, tap] = total.astype(BF16)
            keep[order, tap] = kept[tap, here, :] + got[tap, here, :].astype(F32)

        each(kept.shape[0], one)


def across_kernel(kept, got, out):
    for order in range(kept.shape[0]):

        def one(tap, order=order):
            out[order, tap] = (kept[order, tap] + got[order, tap].astype(F32)).astype(BF16)

        each(kept.shape[1], one)


def total_kernel(place, mine, got, *refs):
    packs, out = refs[:-1], refs[-1]
    for index, pack in enumerate(packs):
        rows = rows_at(place[4] if index == 0 else 1 - place[4], pack.shape[0])
        for order, part in enumerate(split_three(pack[...])[:2]):
            out[order, out.shape[1] - 1, rows, :] = part
    for order in range(mine.shape[0]):

        def one(tap, order=order):
            total = mine[order, tap].astype(F32) + got[order, tap].astype(F32)
            out[order, tap] = total.astype(BF16)

        each(mine.shape[1], one)


def join_near_kernel(place, own, got, *outs):
    count = own.shape[2]
    here, away = rows_at(place[3], count), rows_at(1 - place[3], count)
    for order, out in enumerate(outs):

        def one(tap, order=order, out=out):
            out[tap, here, :] = own[order, tap]
            out[tap, away, :] = got[order, tap]

        each(own.shape[1], one)


def join_pair_kernel(place, own, got_own, other, got_other, half_own, half_other):
    count = own.shape[1]
    for axis, mine, theirs, out in ((1, own, got_own, half_own), (0, other, got_other, half_other)):
        here, away = rows_at(place[axis], count), rows_at(1 - place[axis], count)

        def one(tap, mine=mine, theirs=theirs, out=out, here=here, away=away):
            out[tap, here, :] = mine[tap]
            out[tap, away, :] = theirs[tap]

        each(out.shape[0], one)


def finish_kernel(place, own, other, *refs, away, first):
    out, held, sems = refs[-3:]
    _, taps, half, share = held.shape

    def copy(tap, order):
        column, index = (place[2], place[0]) if order == 0 else (1 - place[2], place[1])
        rows = rows_at(1 - index if away else index, half)
        block = out.at[first + tap, rows, rows_at(column, share)]
        return pltpu.make_async_copy(held.at[order, tap], block, sems.at[order, tap])

    def one(tap):
        for order, part in enumerate((own, other)):
            held[order, tap] = part[tap].astype(F32)
            copy(tap, order).start()

    def last(tap):
        for order in range(2):
            copy(tap, order).wait()

    each(taps, one)
    each(taps, last)


def call(body, outs, scratch=(), smem=0, after=(), hbm=(), scalars=(), plain=(), loose=(), whole=(), micros=0, aliases=None):
    outs = outs if isinstance(outs, tuple) else (outs,)
    any_space = pl.BlockSpec(memory_space=pl.ANY)

    def run(*operands):
        count = len(operands)
        spaces = [pltpu.SMEM] * smem + [pltpu.VMEM] * (count - smem)
        for index in loose + whole:
            spaces[index] = pltpu.HBM
        values = [pltpu.with_memory_space_constraint(*pair) for pair in zip(operands, spaces)]

        def inner(*refs):
            body(*refs[:count], *refs[count + len(after) : -1 - len(scratch)], *refs[len(refs) - len(scratch) :])

        results = pl.pallas_call(
            inner,
            out_shape=tuple(
                member if index in hbm + scalars + plain else pltpu.VMEM(member.shape, member.dtype)
                for index, member in enumerate(outs)
            )
            + (shape(8, 128),),
            in_specs=[SMEM] * smem
            + [any_space if index in whole or index in (aliases or {}) else VMEM for index in range(smem, count)]
            + [any_space] * len(after),
            out_specs=tuple(
                any_space if index in hbm else SMEM if index in scalars else VMEM
                for index in range(len(outs))
            )
            + (any_space,),
            scratch_shapes=scratch,
            input_output_aliases=aliases or {},
            compiler_params=pltpu.CompilerParams(vmem_limit_bytes=VMEM_BYTES),
            cost_estimate=pl.CostEstimate(
                flops=2**10 + int(micros * 1.1e9), bytes_accessed=2**10, transcendentals=0
            ),
        )(*values, *after)
        found, token = results[:-1], results[-1]
        return (found if len(found) > 1 else found[0]), token

    return run


def shape(*dims, kind=F32):
    return jax.ShapeDtypeStruct(dims, kind)


def kernel_shapes(taps, rows, cols):
    return (shape(taps, rows, cols, kind=BF16), shape(taps, rows, cols))


def swap(values, axis_name):
    return lax.ppermute(values, axis_name, SWAP)


def part_of(values, axis, index, size):
    return lax.dynamic_slice_in_dim(values, index * size, size, axis)


def place_pair(index, own, other, axis):
    return jnp.where(
        index == 0,
        jnp.concatenate([own, other], axis=axis),
        jnp.concatenate([other, own], axis=axis),
    )


class Reduction:
    def __init__(self, place, parts, first=0):
        self.place, self.first, self.taps = place, first, parts[0].shape[0]
        self.sent_own, self.keep_own, self.sent_other, self.keep_other = parts
        self.got = swap(self.sent_own, "x"), swap(self.sent_other, "y")

    def second(self, token, micros=0):
        taps, rows, cols = self.keep_own.shape
        parts, token = call(
            second_kernel,
            kernel_shapes(taps, rows // 2, cols) * 2,
            smem=1,
            after=(token,),
            micros=micros,
        )(self.place, self.keep_own, self.got[0], self.keep_other, self.got[1])
        sent_own, self.keep_own, sent_other, self.keep_other = parts
        self.got = swap(sent_own, "y"), swap(sent_other, "x")
        return token

    def near(self, token, micros=0):
        taps, rows, cols = self.keep_own.shape
        piece = (2, taps, rows // 2, cols)
        (send, self.keep), token = call(
            merge_kernel, (shape(*piece, kind=BF16), shape(*piece)), smem=1, after=(token,), micros=micros
        )(self.place, self.keep_own, self.got[0], self.keep_other, self.got[1])
        self.got = swap(send, "near")
        return token

    def across(self, token, micros=0):
        out = shape(*self.keep.shape, kind=BF16)
        self.own, token = call(across_kernel, out, after=(token,), micros=micros)(
            self.keep, self.got
        )
        self.got = swap(self.own, "far")
        return token

    def total(self, token, *packs, micros=0):
        if lax.axis_size("block") > 1:
            self.own = lax.psum(self.own.astype(F32) + self.got.astype(F32), "block").astype(BF16)
            self.got = jnp.zeros_like(self.own)
        orders, taps, rows, cols = self.own.shape
        out = shape(orders, taps + min(len(packs), 1), rows, cols, kind=BF16)
        self.own, token = call(total_kernel, out, smem=1, after=(token,), micros=micros)(
            self.place, self.own, self.got, *packs
        )
        self.got = swap(self.own, "near")
        return token

    def join_near(self, token, micros=0):
        _, taps, rows, cols = self.own.shape
        quarter = shape(taps, 2 * rows, cols, kind=BF16)
        self.own, token = call(
            join_near_kernel, (quarter,) * 2, smem=1, after=(token,), micros=micros
        )(self.place, self.own, self.got)
        self.got = swap(self.own[0], "y"), swap(self.own[1], "x")
        return token

    def join_pair(self, token, micros=0):
        taps, rows, cols = self.own[0].shape
        half = shape(taps, 2 * rows, cols, kind=BF16)
        self.own, token = call(
            join_pair_kernel, (half,) * 2, smem=1, after=(token,), micros=micros
        )(
            self.place, self.own[0], self.got[0], self.own[1], self.got[1]
        )
        self.got = swap(self.own[0], "x"), swap(self.own[1], "y")
        return token

    def finish_half(self, token, parts, out, away):
        taps, (_, half, share) = self.taps, parts[0].shape
        return call(
            functools.partial(finish_kernel, away=away, first=self.first),
            shape(9, 2 * half, 2 * share),
            [pltpu.VMEM((2, taps, half, share), F32), pltpu.SemaphoreType.DMA((2, taps))],
            smem=1,
            after=(token,),
            hbm=(0,),
            loose=(3,) if out else (),
            aliases={3: 0} if out else None,
        )(self.place, *parts, *out)

    def finish_own(self, token, out=()):
        return self.finish_half(token, self.own, out, False)

    def finish(self, token, out):
        return self.finish_half(token, self.got, (out,), True)


def gather_packs(pack):
    for axis_name in DP[::-1]:
        pack = lax.all_gather(pack[None] if pack.ndim == 2 else pack, axis_name, axis=0, tiled=True)
    return pack


def per_device(
    counts,
    features_in,
    rgb_in,
    latent,
    affine_one,
    affine_bias_one,
    affine_two,
    affine_bias_two,
    affine_three,
    affine_bias_three,
    kernel_one,
    bias_one,
    kernel_two,
    bias_two,
    rgb_weight,
    rgb_bias,
    noise_gain,
    noise_one,
    noise_two,
    grad_features,
    grad_rgb,
):
    images, share = features_in.shape[0], features_in.shape[3]
    channels = share * lax.axis_size("chan")
    me = lax.axis_index("chan")
    place = jnp.stack([lax.axis_index(name) for name in ("x", "y", "chan", "near", "far")])
    place = place.astype(jnp.int32)
    valid = (jnp.arange(images, dtype=jnp.int32) < counts[0]).astype(F32)
    valid_rows = jnp.broadcast_to(valid[:, None], (images, share))
    features = features_in.reshape(images, PLANE, share)
    flat_one = kernel_one.reshape(9, share, channels)
    flat_two = kernel_two.reshape(9, share, channels)
    plane_shape = (images, 4, PLANE, share)
    half = share // 2
    wide = pltpu.VMEM((share // 128, HALF, 2, RES, 128), F32)

    send_kind = shape(9, share, share, kind=BF16)
    (styles, scaled_one, send_one), token = call(
        style_kernel,
        (shape(3, images, share), shape(images, PLANE, share, kind=BF16), send_kind),
        [pltpu.SemaphoreType.DMA],
        smem=1,
        loose=tuple(range(2, 10)),
        whole=(1,),
    )(
        place,
        flat_one,
        latent,
        affine_one,
        affine_bias_one.reshape(1, -1),
        affine_two,
        affine_bias_two.reshape(1, -1),
        affine_three,
        affine_bias_three.reshape(1, -1),
        features,
    )
    received_one = swap(send_one, "chan")
    scaled_one_other = swap(scaled_one, "chan")

    def layer_squares(layer, kernel, bias, token):
        (squares, mine, theirs, add, colour), token = call(
            functools.partial(squares_kernel, layer=layer),
            (
                shape(share, channels),
                shape(images, share),
                shape(images, share),
                shape(16, share, kind=BF16),
                shape(images, 16, share, kind=BF16),
            ),
            [pltpu.VMEM((images, channels), F32)],
            smem=1,
            after=(token,),
            loose=(3, 4),
        )(place, styles, kernel, bias.reshape(1, -1), rgb_weight)
        return squares, mine, swap(theirs, "chan"), add, colour, token

    squares_one, mine_one, theirs_one, add_one, _, token = layer_squares(
        0, flat_one, bias_one, token
    )
    (noise_planes_one, noise_planes_two, colours, send_two), token = call(
        planes_kernel,
        (shape(images, 4, 16, PLANE, kind=BF16),) * 3 + (send_kind,),
        [pltpu.SemaphoreType.DMA],
        smem=1,
        after=(token,),
        loose=(2, 4, 5, 6),
        whole=(3,),
    )(place, valid_rows, noise_gain.reshape(1, -1), flat_two, noise_one, noise_two, grad_rgb)
    received_two = swap(send_two, "chan")
    rgb_rows_in = jnp.pad(rgb_weight, ((0, 13), (0, 0)))

    (conv_one, scaled_two, demod_one), token = call(
        conv_one_kernel,
        (shape(*plane_shape), shape(*plane_shape, kind=BF16), shape(images, share)),
        smem=1,
        after=(token,),
        micros=STAGE,
    )(
        place,
        scaled_one,
        scaled_one_other,
        flat_one,
        received_one,
        mine_one,
        theirs_one,
        noise_planes_one,
        add_one,
        styles,
    )
    scaled_two_other = swap(scaled_two, "chan")
    squares_two, mine_two, theirs_two, add_two, colour_weights, token = layer_squares(
        1, flat_two, bias_two, token
    )
    (conv_two, grad_conv_two, demod_two, square_two), token = call(
        conv_two_kernel,
        (
            shape(*plane_shape),
            shape(*plane_shape, kind=BF16),
            shape(images, share),
            shape(images, share),
        ),
        [wide],
        smem=1,
        after=(token,),
    )(
        place,
        scaled_two,
        scaled_two_other,
        flat_two,
        received_two,
        mine_two,
        theirs_two,
        valid_rows,
        noise_planes_two,
        add_two,
        colours,
        colour_weights,
        grad_features,
    )
    grad_conv_two_other = swap(grad_conv_two, "chan")
    square_two_other = swap(square_two, "chan")
    shifted_two, token = call(
        shifted_kernel, shape(*plane_shape, kind=BF16), after=(token,)
    )(scaled_two)
    parts_two, token = call(
        kernel_two_grad,
        kernel_shapes(9, half, share) * 2,
        [pltpu.VMEM((images, share), F32)],
        smem=1,
        after=(token,),
    )(
        place,
        scaled_two,
        shifted_two,
        grad_conv_two,
        grad_conv_two_other,
        flat_two,
        styles,
        square_two,
        square_two_other,
    )
    reduce_two = Reduction(place, parts_two)
    (grad_scaled_two, grad_conv_one, square_one), token = call(
        input_two_grad,
        (shape(*plane_shape), shape(*plane_shape, kind=BF16), shape(images, share)),
        smem=1,
        after=(token,),
    )(
        place,
        grad_conv_two,
        grad_conv_two_other,
        flat_two,
        conv_one,
        demod_one,
        noise_planes_one,
        add_one,
        styles,
    )
    grad_conv_one_other = swap(grad_conv_one, "chan")
    square_one_other = swap(square_one, "chan")
    (features_out, rgb_planes, rgb_grad, sums_two), token = call(
        outputs_two_kernel,
        (
            shape(images, RES, RES, share, kind=BF16),
            shape(images, 4, 8, PLANE),
            shape(16, share),
            shape(images, 8, share),
        ),
        [wide],
        after=(token,),
        plain=(0,),
        loose=(6,),
    )(
        conv_two,
        demod_two,
        valid_rows,
        noise_planes_two,
        add_two,
        colours,
        grad_features,
        styles,
        rgb_rows_in,
    )
    rgb_planes_other = swap(rgb_planes, "chan")
    token = reduce_two.second(token, STAGE)
    parts_one, token = call(
        kernel_one_grad,
        kernel_shapes(9, half, share) * 2,
        [pltpu.VMEM((images, PLANE, share), BF16), pltpu.VMEM((images, share), F32)],
        smem=1,
        after=(token,),
    )(
        place,
        scaled_one,
        grad_conv_one,
        grad_conv_one_other,
        flat_one,
        styles,
        square_one,
        square_one_other,
    )
    reduce_one = Reduction(place, parts_one)
    (rgb_out, grad_rgb_in, rgb_sums), token = call(
        rgb_kernel,
        (shape(*grad_rgb.shape), shape(*rgb_in.shape), shape(8, 128)),
        [pltpu.VMEM((3 * images, RES, 128), F32)],
        after=(token,),
        plain=(0, 1),
        loose=(1, 4, 5),
    )(valid_rows, rgb_bias.reshape(1, -1), rgb_planes, rgb_planes_other, rgb_in, grad_rgb)
    token = reduce_two.near(token, STAGE)
    sums_one, token = call(
        outputs_one_kernel, shape(images, 8, share), after=(token,)
    )(
        conv_one,
        grad_scaled_two,
        demod_one,
        valid_rows,
        noise_planes_one,
        add_one,
        styles,
    )
    (grad_features_in, style_sums), token = call(
        input_one_grad,
        (shape(images, PLANE, share), shape(images, share)),
        smem=1,
        after=(token,),
        plain=(0,),
        loose=(4,),
    )(place, grad_conv_one, grad_conv_one_other, flat_one, features, styles)
    (style_grads, crossing), token = call(
        style_grads_kernel,
        (shape(3 * images, share), shape(-(-(2 * images + 1) // 8) * 8, share)),
        smem=1,
        after=(token,),
        loose=(11, 12, 13),
    )(
        place,
        square_one,
        square_one_other,
        square_two,
        square_two_other,
        squares_one,
        squares_two,
        styles,
        style_sums,
        sums_one,
        sums_two,
        affine_one,
        affine_two,
        affine_three,
    )
    crossing_other = swap(crossing, "chan")
    token = reduce_two.across(token)
    token = reduce_one.second(token)
    (grad_latent, pack), token = call(
        pack_kernel,
        (shape(images, channels), shape(-(-(5 * images + 6) // 8) * 8, share)),
        after=(token,),
        plain=(0,),
    )(
        valid_rows,
        crossing,
        crossing_other,
        style_grads,
        latent,
        sums_one,
        sums_two,
        rgb_grad,
        rgb_sums,
    )
    devices = lax.axis_size(DP)
    alone = lax.axis_size("block") == 1
    packs = [pack, swap(pack, "far")] if alone else []
    token = reduce_two.total(token, *packs, micros=STAGE)
    token = reduce_one.near(token, STAGE)
    token = reduce_two.join_near(token, STAGE)
    token = reduce_one.across(token, STAGE)
    token = reduce_two.join_pair(token, STAGE)
    token = reduce_one.total(token, micros=STAGE)
    sum_two, token = reduce_two.finish_own(token)
    token = reduce_one.join_near(token)
    sum_two, token = reduce_two.finish(token, sum_two)
    if alone:
        packs = [reduce_two.own[0], reduce_two.got[0], reduce_two.own[1], reduce_two.got[1]]
    else:
        packs = [gather_packs(pack)]
    token = reduce_one.join_pair(token, STAGE)
    sum_one, token = reduce_one.finish_own(token)
    spread_out, token = call(
        functools.partial(spread_kernel, images=images),
        (shape(channels, share),) * 3
        + (shape(1, share),) * 5
        + (shape(3, share), shape(2), shape(3), shape(3)),
        [pltpu.VMEM((devices,) + pack.shape, F32), pltpu.VMEM((2, devices) + pack.shape, F32)],
        smem=1,
        after=(token,),
        scalars=(9, 10, 11),
        plain=tuple(range(9)),
    )(place, *packs)
    affine_grads, affine_biases, points = spread_out[0:3], spread_out[3:6], spread_out[6:8]
    rgb_total, gains, rms_values, rgb_bias_grad = spread_out[8:]
    sum_one, token = reduce_one.finish(token, sum_one)
    affine_outs = []
    for grad, bias in zip(affine_grads, affine_biases):
        affine_outs += [grad, bias.reshape(-1)]
    return (
        features_out,
        rgb_out,
        grad_features_in.reshape(features_in.shape),
        grad_rgb_in,
        grad_latent,
        *affine_outs,
        sum_one.reshape(kernel_one.shape),
        points[0].reshape(-1),
        sum_two.reshape(kernel_two.shape),
        points[1].reshape(-1),
        rgb_total,
        rgb_bias_grad,
        gains,
        rms_values,
    )


def solution(mesh):
    blocks = mesh.shape["dp"] // 16
    grid = mesh.devices.reshape(blocks, 2, 2, 2, 2, mesh.shape["chan"])
    split_mesh = Mesh(grid, DP + ("chan",))
    in_specs = (
        P(DP),
        P(DP, None, None, "chan"),
        P(DP, None, None, None),
        P(DP, None),
        P(None, "chan"),
        P("chan"),
        P(None, "chan"),
        P("chan"),
        P(None, "chan"),
        P("chan"),
        P(None, None, "chan", None),
        P("chan"),
        P(None, None, "chan", None),
        P("chan"),
        P(None, "chan"),
        P(),
        P(),
        P(DP, None, None),
        P(DP, None, None),
        P(DP, None, None, "chan"),
        P(DP, None, None, None),
    )
    out_specs = (
        P(DP, None, None, "chan"),
        P(DP, None, None, None),
        P(DP, None, None, "chan"),
        P(DP, None, None, None),
        P(DP, None),
        P(None, "chan"),
        P("chan"),
        P(None, "chan"),
        P("chan"),
        P(None, "chan"),
        P("chan"),
        P(None, None, "chan", None),
        P("chan"),
        P(None, None, "chan", None),
        P("chan"),
        P(None, "chan"),
        P(),
        P(),
        P(),
    )
    return jax.shard_map(
        per_device, mesh=split_mesh, in_specs=in_specs, out_specs=out_specs, check_vma=False
    )
```

profile of v0, /device:TPU:0, one launch (start us, length us, event | category | flops | bytes accessed | tf_op | source)
XLA Modules:
  0.0 158.5 jit_solution(7931890379924571393)
XLA Ops:
  0.8 2.7 %shard_map.348 = (f32[3,2,256]{2,1,0:T(2,128)S(1)}, bf16[2,256,256]{2,1,0:T(8,128)(2,1)S(1)}, bf16[9,256,256]{2,1,0:T(8,128)(2,1)S(1)}, f32[8,128]{1,0:T(8,128)S(1)}) custom-call(s32[5]{0:T(128)S(1)} %stack.23.refs_0_, bf16[9,256,512]{2,1,0:T(8,128)(2,1)} %bitcast.30, bf16[2,512]{1,0:T(2,128)(2,1)} %refs_4_.9, bf16[512,256]{1,0:T(8,128)(2,1)} %refs_11_.1, ...), custom_call_target="tpu_custom_call" | custom-call | flops 1024 | bytes 1024 | tf_op jit(solution)/shard_map/pallas_call | solution.py:934
  3.5 0.5 collective-permute-start.1
  4.1 2.0 %shard_map.349 = (f32[256,512]{1,0:T(8,128)S(1)}, f32[2,256]{1,0:T(2,128)S(1)}, f32[2,256]{1,0:T(2,128)S(1)}, bf16[16,256]{1,0:T(8,128)(2,1)S(1)}, bf16[2,16,256]{2,1,0:T(8,128)(2,1)}, /*index=5*/f32[8,128]{1,0:T(8,128)S(1)}) custom-call(s32[5]{0:T(128)S(1)} %stack.23.refs_0_, ...), custom_call_target="tpu_custom_call" | custom-call | flops 1024 | bytes 1024 | tf_op jit(solution)/shard_map/pallas_call | solution.py:934
  7.2 2.7 %shard_map.350 = (bf16[2,4,16,256]{3,2,1,0:T(8,128)(2,1)S(1)}, bf16[2,4,16,256]{3,2,1,0:T(8,128)(2,1)S(1)}, bf16[2,4,16,256]{3,2,1,0:T(8,128)(2,1)S(1)}, bf16[9,256,256]{2,1,0:T(8,128)(2,1)S(1)}, f32[8,128]{1,0:T(8,128)S(1)}) custom-call(s32[5]{0:T(128)S(1)} %stack.23.refs_0_, f32[2,256]{1,0:T(2,128)S(1)} %broadcast_in_dim.2.refs_1_.refs_7_.refs_2_.refs_0_.refs_3_, ...), custom_call_target="tpu_custom_call" | custom-call | flops 1024 | bytes 1024 | tf_op jit(solution)/shard_map/pallas_call | solution.py:934
  10.1 2.8 %shard_map.351 = (f32[2,4,256,256]{3,2,1,0:T(8,128)S(1)}, bf16[2,4,256,256]{3,2,1,0:T(8,128)(2,1)S(1)}, f32[2,256]{1,0:T(2,128)S(1)}, f32[8,128]{1,0:T(8,128)S(1)}) custom-call(s32[5]{0:T(128)S(1)} %stack.23.refs_0_, bf16[2,256,256]{2,1,0:T(8,128)(2,1)S(1)} %get-tuple-element.140.refs_1_, bf16[2,256,256]{2,1,0:T(8,128)(2,1)S(1)} %collective-permute-done.refs_2_, ...), custom_call_target="tpu_custom_call" | custom-call | flops 66000003072 | bytes 1024 | tf_op jit(solution)/shard_map/pallas_call | solution.py:934
  12.9 0.5 collective-permute-start.3
  13.4 1.5 shard_map.352
  15.0 1.0 collective-permute-done.5.refs_6_
  16.0 6.9 %shard_map.353 = (f32[2,4,256,256]{3,2,1,0:T(8,128)S(1)}, bf16[2,4,256,256]{3,2,1,0:T(8,128)(2,1)S(1)}, f32[2,256]{1,0:T(2,128)S(1)}, f32[2,256]{1,0:T(2,128)S(1)}, f32[8,128]{1,0:T(8,128)S(1)}) custom-call(s32[5]{0:T(128)S(1)} %stack.23.refs_0_, bf16[2,4,256,256]{3,2,1,0:T(8,128)(2,1)S(1)} %get-tuple-element.150.refs_1_.refs_0_, ...), custom_call_target="tpu_custom_call" | custom-call | flops 1024 | bytes 1024 | tf_op jit(solution)/shard_map/pallas_call | solution.py:934
  23.8 1.8 %collective-permute-done.7.refs_8_.refs_4_ = f32[2,256]{1,0:T(2,128)S(1)} collective-permute-done((f32[2,256]{1,0:T(2,128)S(1)}, f32[2,256]{1,0:T(2,128)S(1)}, u32[]{:S(2)}, u32[]{:S(2)}) %collective-permute-start.7) | collective-permute-done | bytes 2080 | tf_op jit(solution)/shard_map/ppermute | solution.py:971
  25.7 6.5 %shard_map.355 = (bf16[9,128,256]{2,1,0:T(8,128)(2,1)S(1)}, f32[9,128,256]{2,1,0:T(8,128)S(1)}, bf16[9,128,256]{2,1,0:T(8,128)(2,1)S(1)}, f32[9,128,256]{2,1,0:T(8,128)S(1)}, f32[8,128]{1,0:T(8,128)S(1)}) custom-call(s32[5]{0:T(128)S(1)} %stack.23.refs_0_, bf16[2,4,256,256]{3,2,1,0:T(8,128)(2,1)S(1)} %get-tuple-element.150.refs_1_.refs_0_, ...), custom_call_target="tpu_custom_call" | custom-call | flops 1024 | bytes 1024 | tf_op jit(solution)/shard_map/pallas_call | solution.py:934
  32.2 2.7 %collective-permute-start.11 = (bf16[9,128,256]{2,1,0:T(8,128)(2,1)S(1)}, bf16[9,128,256]{2,1,0:T(8,128)(2,1)S(1)}, u32[]{:S(2)}, u32[]{:S(2)}) collective-permute-start(bf16[9,128,256]{2,1,0:T(8,128)(2,1)S(1)} %get-tuple-element.176), channel_id=1, source_target_pairs={{0,2},{2,0},{1,3},{3,1},{4,6},{6,4},{5,7},{7,5},{8,10},{10,8},{9,1... | collective-permute-start | bytes 1769480 | tf_op jit(solution)/shard_map/ppermute | solution.py:971
  34.9 1.5 collective-permute-start.12
  36.5 6.3 %shard_map.356 = (f32[2,4,256,256]{3,2,1,0:T(8,128)S(1)}, bf16[2,4,256,256]{3,2,1,0:T(8,128)(2,1)S(1)}, f32[2,256]{1,0:T(2,128)S(1)}, f32[8,128]{1,0:T(8,128)S(1)}) custom-call(s32[5]{0:T(128)S(1)} %stack.23.refs_0_, bf16[2,4,256,256]{3,2,1,0:T(8,128)(2,1)S(1)} %get-tuple-element.162.refs_3_.refs_1_, ...), custom_call_target="tpu_custom_call" | custom-call | flops 1024 | bytes 1024 | tf_op jit(solution)/shard_map/pallas_call | solution.py:934
  42.9 5.7 %shard_map.357 = (bf16[2,32,32,256]{3,2,1,0:T(8,128)(2,1)}, f32[2,4,8,256]{3,2,1,0:T(8,128)S(1)}, f32[16,256]{1,0:T(8,128)S(1)}, f32[2,8,256]{2,1,0:T(8,128)S(1)}, f32[8,128]{1,0:T(8,128)S(1)}) custom-call(f32[2,4,256,256]{3,2,1,0:T(8,128)S(1)} %get-tuple-element.160.refs_0_, f32[2,256]{1,0:T(2,128)S(1)} %get-tuple-element.161.refs_1_, ...), custom_call_target="tpu_custom_call" | custom-call | flops 1024 | bytes 1024 | tf_op jit(solution)/shard_map/pallas_call | solution.py:934
  48.7 1.5 collective-permute-done.12.refs_4_
  50.2 0.8 shard_map.358
  51.0 1.6 %collective-permute-start.13 = (bf16[9,64,256]{2,1,0:T(8,128)(2,1)S(1)}, bf16[9,64,256]{2,1,0:T(8,128)(2,1)S(1)}, u32[]{:S(2)}, u32[]{:S(2)}) collective-permute-start(bf16[9,64,256]{2,1,0:T(8,128)(2,1)S(1)} %get-tuple-element.185), channel_id=1, source_target_pairs={{0,4},{4,0},{1,5},{5,1},{2,6},{6,2},{3,7},{7,3},{8,12},{12,8},{9,1... | collective-permute-start | bytes 884744 | tf_op jit(solution)/shard_map/ppermute | solution.py:971
  52.6 0.5 collective-permute-start.14
  53.2 0.5 collective-permute-start.10
  53.7 0.8 collective-permute-done.10.refs_7_.refs_2_
  54.5 2.7 %shard_map.359 = (bf16[9,128,256]{2,1,0:T(8,128)(2,1)S(1)}, f32[9,128,256]{2,1,0:T(8,128)S(1)}, bf16[9,128,256]{2,1,0:T(8,128)(2,1)S(1)}, f32[9,128,256]{2,1,0:T(8,128)S(1)}, f32[8,128]{1,0:T(8,128)S(1)}) custom-call(s32[5]{0:T(128)S(1)} %stack.23.refs_0_, bf16[2,256,256]{2,1,0:T(8,128)(2,1)S(1)} %get-tuple-element.140.refs_1_, ...), custom_call_target="tpu_custom_call" | custom-call | flops 1024 | bytes 1024 | tf_op jit(solution)/shard_map/pallas_call | solution.py:934
  57.2 1.5 collective-permute-start.16
  58.8 0.5 collective-permute-start.17
  59.3 3.1 %shard_map.360 = (f32[2,3,32,32]{3,2,1,0:T(8,128)}, f32[2,3,16,16]{3,2,1,0:T(8,128)}, f32[8,128]{1,0:T(8,128)S(1)}, f32[8,128]{1,0:T(8,128)S(1)}) custom-call(f32[2,256]{1,0:T(2,128)S(1)} %broadcast_in_dim.2.refs_1_.refs_7_.refs_2_.refs_0_.refs_3_, f32[1,3]{1,0:T(1,128)} %bitcast.44, f32[2,4,8,256]{3,2,1,0:T(8,128)S(1)} %get-tuple-element.172.refs_2_, ...), custom_call_target="tpu_custom_call" | custom-call | flops 1024 | bytes 1024 | tf_op jit(solution)/shard_map/pallas_call | solution.py:934
  62.4 0.7 shard_map.361
  63.2 1.7 %collective-permute-start.18 = (bf16[2,9,32,256]{3,2,1,0:T(8,128)(2,1)S(1)}, bf16[2,9,32,256]{3,2,1,0:T(8,128)(2,1)S(1)}, u32[]{:S(2)}, u32[]{:S(2)}) collective-permute-start(bf16[2,9,32,256]{3,2,1,0:T(8,128)(2,1)S(1)} %get-tuple-element.208), channel_id=1, source_target_pairs={{0,8},{8,0},{1,9},{9,1},{2,10},{10,2},{3,11},{11,3},{4,12},{12,4},... | collective-permute-start | bytes 884744 | tf_op jit(solution)/shard_map/ppermute | solution.py:971
  64.8 2.3 %shard_map.362 = (f32[2,8,256]{2,1,0:T(8,128)S(1)}, f32[8,128]{1,0:T(8,128)S(1)}) custom-call(f32[2,4,256,256]{3,2,1,0:T(8,128)S(1)} %get-tuple-element.163.refs_4_.refs_0_, f32[2,4,256,256]{3,2,1,0:T(8,128)S(1)} %get-tuple-element.183.refs_1_, f32[2,256]{1,0:T(2,128)S(1)} %get-tuple-element.164.refs_5_.refs_2_, ...), custom_call_target="tpu_custom_call" | custom-call | flops 1024 | bytes 1024 | tf_op jit(solution)/shard_map/pallas_call | solution.py:934
  67.2 3.2 %shard_map.363 = (f32[2,256,256]{2,1,0:T(8,128)}, f32[2,256]{1,0:T(2,128)S(1)}, f32[8,128]{1,0:T(8,128)S(1)}) custom-call(s32[5]{0:T(128)S(1)} %stack.23.refs_0_, bf16[2,4,256,256]{3,2,1,0:T(8,128)(2,1)S(1)} %get-tuple-element.173.refs_2_.refs_1_, bf16[2,4,256,256]{3,2,1,0:T(8,128)(2,1)S(1)} %collective-permute-done.9.refs_3_.refs_2_, ...), custom_call_target="tpu_custom_call" | custom-call | flops 1024 | bytes 1024 | tf_op jit(solution)/shard_map/pallas_call | solution.py:934
  70.4 3.3 %shard_map.364 = (f32[6,256]{1,0:T(8,128)S(1)}, f32[8,256]{1,0:T(8,128)S(1)}, f32[8,128]{1,0:T(8,128)S(1)}) custom-call(s32[5]{0:T(128)S(1)} %stack.23.refs_0_, f32[2,256]{1,0:T(2,128)S(1)} %get-tuple-element.174.refs_6_.refs_1_, f32[2,256]{1,0:T(2,128)S(1)} %collective-permute-done.10.refs_7_.refs_2_, f32[2,256]{1,0:T(2,128)S(1)} %get-tuple-element.167.refs_7_.refs_3_, ...), custom_call_target="tpu_custom_call" | custom-call | flops 1024 | bytes 1024 | tf_op jit(solution)/shard_map/pallas_call | solution.py:934
  73.9 2.7 %collective-permute-start.19 = (bf16[2,9,32,256]{3,2,1,0:T(8,128)(2,1)S(1)}, bf16[2,9,32,256]{3,2,1,0:T(8,128)(2,1)S(1)}, u32[]{:S(2)}, u32[]{:S(2)}) collective-permute-start(bf16[2,9,32,256]{3,2,1,0:T(8,128)(2,1)S(1)} %get-tuple-element.213.refs_1_), channel_id=1, source_target_pairs={{0,16},{16,0},{1,17},{17,1},{2,18},{18,2},{3,19},{19,3},{4,20},{20... | collective-permute-start | bytes 884744 | tf_op jit(solution)/shard_map/ppermute | solution.py:971
  76.5 0.8 shard_map.366
  77.7 0.6 shard_map.367
  78.6 1.5 collective-permute-start.22
  80.1 0.6 collective-permute-start.23
  80.7 9.2 %collective-permute-done.19.refs_2_ = bf16[2,9,32,256]{3,2,1,0:T(8,128)(2,1)S(1)} collective-permute-done((bf16[2,9,32,256]{3,2,1,0:T(8,128)(2,1)S(1)}, bf16[2,9,32,256]{3,2,1,0:T(8,128)(2,1)S(1)}, u32[]{:S(2)}, u32[]{:S(2)}) %collective-permute-start.19) | collective-permute-done | bytes 294944 | tf_op jit(solution)/shard_map/ppermute | solution.py:971
  90.2 0.7 shard_map.368
  91.0 0.7 shard_map.369
  91.7 2.1 %collective-permute-start.26 = (bf16[2,9,32,256]{3,2,1,0:T(8,128)(2,1)S(1)}, bf16[2,9,32,256]{3,2,1,0:T(8,128)(2,1)S(1)}, u32[]{:S(2)}, u32[]{:S(2)}) collective-permute-start(bf16[2,9,32,256]{3,2,1,0:T(8,128)(2,1)S(1)} %get-tuple-element.226), channel_id=1, source_target_pairs={{0,8},{8,0},{1,9},{9,1},{2,10},{10,2},{3,11},{11,3},{4,12},{12,4},... | collective-permute-start | bytes 884744 | tf_op jit(solution)/shard_map/ppermute | solution.py:971
  93.8 7.7 %collective-permute-done.21.refs_2_ = bf16[2,10,32,256]{3,2,1,0:T(8,128)(2,1)S(1)} collective-permute-done((bf16[2,10,32,256]{3,2,1,0:T(8,128)(2,1)S(1)}, bf16[2,10,32,256]{3,2,1,0:T(8,128)(2,1)S(1)}, u32[]{:S(2)}, u32[]{:S(2)}) %collective-permute-start.21) | collective-permute-done | bytes 327712 | tf_op jit(solution)/shard_map/ppermute | solution.py:971
  101.5 0.7 shard_map.370
  102.2 1.6 %collective-permute-start.24 = (bf16[10,64,256]{2,1,0:T(8,128)(2,1)S(1)}, bf16[10,64,256]{2,1,0:T(8,128)(2,1)S(1)}, u32[]{:S(2)}, u32[]{:S(2)}) collective-permute-start(bf16[10,64,256]{2,1,0:T(8,128)(2,1)S(1)} %get-tuple-element.223.refs_1_), channel_id=1, source_target_pairs={{0,4},{4,0},{1,5},{5,1},{2,6},{6,2},{3,7},{7,3},{8,12},{12,8},{9,1... | collective-permute-start | bytes 983048 | tf_op jit(solution)/shard_map/ppermute | solution.py:971
  103.8 0.5 collective-permute-start.25
  104.3 2.5 %collective-permute-done.26.refs_1_ = bf16[2,9,32,256]{3,2,1,0:T(8,128)(2,1)S(1)} collective-permute-done((bf16[2,9,32,256]{3,2,1,0:T(8,128)(2,1)S(1)}, bf16[2,9,32,256]{3,2,1,0:T(8,128)(2,1)S(1)}, u32[]{:S(2)}, u32[]{:S(2)}) %collective-permute-start.26) | collective-permute-done | bytes 294944 | tf_op jit(solution)/shard_map/ppermute | solution.py:971
  107.4 2.7 %collective-permute-done.24.refs_2_ = bf16[10,64,256]{2,1,0:T(8,128)(2,1)S(1)} collective-permute-done((bf16[10,64,256]{2,1,0:T(8,128)(2,1)S(1)}, bf16[10,64,256]{2,1,0:T(8,128)(2,1)S(1)}, u32[]{:S(2)}, u32[]{:S(2)}) %collective-permute-start.24) | collective-permute-done | bytes 327712 | tf_op jit(solution)/shard_map/ppermute | solution.py:971
  110.1 1.3 collective-permute-done.25.refs_4_
  111.4 0.7 shard_map.372
  112.1 0.6 collective-permute-start.27
  113.2 9.2 %collective-permute-done.29.refs_2_ = bf16[2,9,32,256]{3,2,1,0:T(8,128)(2,1)S(1)} collective-permute-done((bf16[2,9,32,256]{3,2,1,0:T(8,128)(2,1)S(1)}, bf16[2,9,32,256]{3,2,1,0:T(8,128)(2,1)S(1)}, u32[]{:S(2)}, u32[]{:S(2)}) %collective-permute-start.29) | collective-permute-done | bytes 294944 | tf_op jit(solution)/shard_map/ppermute | solution.py:971
  122.4 0.7 shard_map.373
  123.2 2.1 %shard_map.374 = (f32[9,256,512]{2,1,0:T(8,128)}, f32[8,128]{1,0:T(8,128)S(1)}) custom-call(s32[5]{0:T(128)S(1)} %stack.23.refs_0_, bf16[10,128,256]{2,1,0:T(8,128)(2,1)S(1)} %get-tuple-element.229.refs_1_, bf16[10,128,256]{2,1,0:T(8,128)(2,1)S(1)} %get-tuple-element.230.refs_2_.refs_3_, f32[8,128]{1,0:T(8,128)S(1)} %get-tuple-element.234.refs_3_), custom_call_target="tpu_custom_call" | custom-call | flops 1024 | bytes 1024 | tf_op jit(solution)/shard_map/pallas_call | solution.py:934
  125.3 6.8 %collective-permute-done.30.refs_2_ = bf16[2,9,32,256]{3,2,1,0:T(8,128)(2,1)S(1)} collective-permute-done((bf16[2,9,32,256]{3,2,1,0:T(8,128)(2,1)S(1)}, bf16[2,9,32,256]{3,2,1,0:T(8,128)(2,1)S(1)}, u32[]{:S(2)}, u32[]{:S(2)}) %collective-permute-start.30) | collective-permute-done | bytes 294944 | tf_op jit(solution)/shard_map/ppermute | solution.py:971
  132.0 0.7 shard_map.375
  132.7 1.6 %collective-permute-start.31 = (bf16[9,64,256]{2,1,0:T(8,128)(2,1)S(1)}, bf16[9,64,256]{2,1,0:T(8,128)(2,1)S(1)}, u32[]{:S(2)}, u32[]{:S(2)}) collective-permute-start(bf16[9,64,256]{2,1,0:T(8,128)(2,1)S(1)} %get-tuple-element.236.refs_1_), channel_id=1, source_target_pairs={{0,4},{4,0},{1,5},{5,1},{2,6},{6,2},{3,7},{7,3},{8,12},{12,8},{9,1... | collective-permute-start | bytes 884744 | tf_op jit(solution)/shard_map/ppermute | solution.py:971
  134.3 0.5 collective-permute-start.32
  134.9 2.1 %shard_map.376 = (f32[9,256,512]{2,1,0:T(8,128)}, f32[8,128]{1,0:T(8,128)S(1)}) custom-call(s32[5]{0:T(128)S(1)} %stack.23.refs_0_, bf16[10,128,256]{2,1,0:T(8,128)(2,1)S(1)} %collective-permute-done.27.refs_1_.refs_2_, bf16[10,128,256]{2,1,0:T(8,128)(2,1)S(1)} %collective-permute-done.28.refs_2_.refs_4_, ...), custom_call_target="tpu_custom_call", output_to_operand_aliasing={{0}: (3, {})} | custom-call | flops 1024 | bytes 1024 | tf_op jit(solution)/shard_map/pallas_call | solution.py:934
  137.0 3.8 %collective-permute-done.31.refs_2_ = bf16[9,64,256]{2,1,0:T(8,128)(2,1)S(1)} collective-permute-done((bf16[9,64,256]{2,1,0:T(8,128)(2,1)S(1)}, bf16[9,64,256]{2,1,0:T(8,128)(2,1)S(1)}, u32[]{:S(2)}, u32[]{:S(2)}) %collective-permute-start.31) | collective-permute-done | bytes 294944 | tf_op jit(solution)/shard_map/ppermute | solution.py:971
  140.8 1.3 collective-permute-done.32.refs_4_
  142.1 0.7 shard_map.377
  142.8 0.6 collective-permute-start.33
  143.8 2.1 %shard_map.378 = (f32[9,256,512]{2,1,0:T(8,128)}, f32[8,128]{1,0:T(8,128)S(1)}) custom-call(s32[5]{0:T(128)S(1)} %stack.23.refs_0_, bf16[9,128,256]{2,1,0:T(8,128)(2,1)S(1)} %get-tuple-element.241.refs_1_, bf16[9,128,256]{2,1,0:T(8,128)(2,1)S(1)} %get-tuple-element.242.refs_2_, f32[8,128]{1,0:T(8,128)S(1)} %get-tuple-element.243.refs_3_), custom_call_target="tpu_custom_call" | custom-call | flops 1024 | bytes 1024 | tf_op jit(solution)/shard_map/pallas_call | solution.py:934
  145.9 3.2 %shard_map.379 = (f32[512,256]{1,0:T(8,128)}, f32[512,256]{1,0:T(8,128)}, f32[512,256]{1,0:T(8,128)}, f32[1,256]{1,0:T(1,128)}, f32[1,256]{1,0:T(1,128)}, /*inde...) custom-call(s32[5]{0:T(128)S(1)} %stack.23.refs_0_, ...), custom_call_target="tpu_custom_call" | custom-call | flops 1024 | bytes 1024 | tf_op jit(solution)/shard_map/pallas_call | solution.py:934
  149.1 6.9 %collective-permute-done.33.refs_1_ = bf16[9,128,256]{2,1,0:T(8,128)(2,1)S(1)} collective-permute-done((bf16[9,128,256]{2,1,0:T(8,128)(2,1)S(1)}, bf16[9,128,256]{2,1,0:T(8,128)(2,1)S(1)}, u32[]{:S(2)}, u32[]{:S(2)}) %collective-permute-start.33) | collective-permute-done | bytes 589856 | tf_op jit(solution)/shard_map/ppermute | solution.py:971
  156.2 2.1 %shard_map.380 = (f32[9,256,512]{2,1,0:T(8,128)}, f32[8,128]{1,0:T(8,128)}) custom-call(s32[5]{0:T(128)S(1)} %stack.23.refs_0_, bf16[9,128,256]{2,1,0:T(8,128)(2,1)S(1)} %collective-permute-done.33.refs_1_, bf16[9,128,256]{2,1,0:T(8,128)(2,1)S(1)} %collective-permute-done.34.refs_2_, ...), custom_call_target="tpu_custom_call", output_to_operand_aliasing={{0}: (3, {})} | custom-call | flops 1024 | bytes 1024 | tf_op jit(solution)/shard_map/pallas_call | solution.py:934
  (53 shorter events, 5.1 us)
Async XLA Ops:
  0.7 3.4 %copy-start.1 = (bf16[3,3,256,512]{3,2,1,0:T(8,128)(2,1)S(1)}, bf16[3,3,256,512]{3,2,1,0:T(8,128)(2,1)}, u32[]{:S(2)}) copy-start(bf16[3,3,256,512]{3,2,1,0:T(8,128)(2,1)} %param.31) | copy-start | bytes 7077892
  3.5 6.6 %collective-permute-start.1 = (bf16[9,256,256]{2,1,0:T(8,128)(2,1)S(1)}, bf16[9,256,256]{2,1,0:T(8,128)(2,1)S(1)}, u32[]{:S(2)}, u32[]{:S(2)}) collective-permute-start(bf16[9,256,256]{2,1,0:T(8,128)(2,1)S(1)} %get-tuple-element.141), channel_id=1, source_target_pairs={{0,1},{1,0},{2,3},{3,2},{4,5},{5,4},{6,7},{7,6},{8,9},{9,8},{10,11... | collective-permute-start | bytes 3538952 | tf_op jit(solution)/shard_map/ppermute | solution.py:971
  4.0 6.1 %collective-permute-start = (bf16[2,256,256]{2,1,0:T(8,128)(2,1)S(1)}, bf16[2,256,256]{2,1,0:T(8,128)(2,1)S(1)}, u32[]{:S(2)}, u32[]{:S(2)}) collective-permute-start(bf16[2,256,256]{2,1,0:T(8,128)(2,1)S(1)} %get-tuple-element.140.refs_1_), channel_id=1, source_target_pairs={{0,1},{1,0},{2,3},{3,2},{4,5},{5,4},{6,7},{7,6},{8,9},{9,8},{10,11... | collective-permute-start | bytes 786440 | tf_op jit(solution)/shard_map/ppermute | solution.py:971
  6.1 4.0 %collective-permute-start.2 = (f32[2,256]{1,0:T(2,128)S(1)}, f32[2,256]{1,0:T(2,128)S(1)}, u32[]{:S(2)}, u32[]{:S(2)}) collective-permute-start(f32[2,256]{1,0:T(2,128)S(1)} %get-tuple-element.145), channel_id=1, source_target_pairs={{0,1},{1,0},{2,3},{3,2},{4,5},{5,4},{6,7},{7,6},{8,9},{9,8},{10,11... | collective-permute-start | bytes 6152 | tf_op jit(solution)/shard_map/ppermute | solution.py:971
  9.9 5.1 %collective-permute-start.4 = (bf16[9,256,256]{2,1,0:T(8,128)(2,1)S(1)}, bf16[9,256,256]{2,1,0:T(8,128)(2,1)S(1)}, u32[]{:S(2)}, u32[]{:S(2)}) collective-permute-start(bf16[9,256,256]{2,1,0:T(8,128)(2,1)S(1)} %get-tuple-element.151), channel_id=1, source_target_pairs={{0,1},{1,0},{2,3},{3,2},{4,5},{5,4},{6,7},{7,6},{8,9},{9,8},{10,11... | collective-permute-start | bytes 3538952 | tf_op jit(solution)/shard_map/ppermute | solution.py:971
  10.1 3.3 %copy-start = (bf16[3,3,256,512]{3,2,1,0:T(8,128)(2,1)S(1)}, bf16[3,3,256,512]{3,2,1,0:T(8,128)(2,1)}, u32[]{:S(2)}) copy-start(bf16[3,3,256,512]{3,2,1,0:T(8,128)(2,1)} %param.33) | copy-start | bytes 7077892
  12.8 3.2 %copy-start.2 = (bf16[2,32,32,256]{3,2,1,0:T(8,128)(2,1)S(1)}, bf16[2,32,32,256]{3,2,1,0:T(8,128)(2,1)}, u32[]{:S(2)}) copy-start(bf16[2,32,32,256]{3,2,1,0:T(8,128)(2,1)} %refs_6_.3) | copy-start | bytes 3145732
  12.9 3.2 %collective-permute-start.3 = (bf16[2,4,256,256]{3,2,1,0:T(8,128)(2,1)S(1)}, bf16[2,4,256,256]{3,2,1,0:T(8,128)(2,1)S(1)}, u32[]{:S(2)}, u32[]{:S(2)}) collective-permute-start(bf16[2,4,256,256]{3,2,1,0:T(8,128)(2,1)S(1)} %get-tuple-element.150.refs_1_.refs_0_), channel_id=1, source_target_pairs={{0,1},{1,0},{2,3},{3,2},{4,5},{5,4},{6,7},{7,6},{8,9},{9,8},{10,11... | collective-permute-start | bytes 3145736 | tf_op jit(solution)/shard_map/ppermute | solution.py:971
  14.9 1.2 collective-permute-start.5
  22.9 2.7 %collective-permute-start.6 = (bf16[2,4,256,256]{3,2,1,0:T(8,128)(2,1)S(1)}, bf16[2,4,256,256]{3,2,1,0:T(8,128)(2,1)S(1)}, u32[]{:S(2)}, u32[]{:S(2)}) collective-permute-start(bf16[2,4,256,256]{3,2,1,0:T(8,128)(2,1)S(1)} %get-tuple-element.162.refs_3_.refs_1_), channel_id=1, source_target_pairs={{0,1},{1,0},{2,3},{3,2},{4,5},{5,4},{6,7},{7,6},{8,9},{9,8},{10,11... | collective-permute-start | bytes 3145736 | tf_op jit(solution)/shard_map/ppermute | solution.py:971
  23.2 2.5 %collective-permute-start.7 = (f32[2,256]{1,0:T(2,128)S(1)}, f32[2,256]{1,0:T(2,128)S(1)}, u32[]{:S(2)}, u32[]{:S(2)}) collective-permute-start(f32[2,256]{1,0:T(2,128)S(1)} %get-tuple-element.167.refs_7_.refs_3_), channel_id=1, source_target_pairs={{0,1},{1,0},{2,3},{3,2},{4,5},{5,4},{6,7},{7,6},{8,9},{9,8},{10,11... | collective-permute-start | bytes 6152 | tf_op jit(solution)/shard_map/ppermute | solution.py:971
  25.7 10.8 %copy-start.4 = (bf16[3,256]{1,0:T(4,128)(2,1)S(1)}, bf16[3,256]{1,0:T(4,128)(2,1)}, u32[]{:S(2)}) copy-start(bf16[3,256]{1,0:T(4,128)(2,1)} %refs_4_.7) | copy-start | bytes 4612
  32.2 16.5 %collective-permute-start.11 = (bf16[9,128,256]{2,1,0:T(8,128)(2,1)S(1)}, bf16[9,128,256]{2,1,0:T(8,128)(2,1)S(1)}, u32[]{:S(2)}, u32[]{:S(2)}) collective-permute-start(bf16[9,128,256]{2,1,0:T(8,128)(2,1)S(1)} %get-tuple-element.176), channel_id=1, source_target_pairs={{0,2},{2,0},{1,3},{3,1},{4,6},{6,4},{5,7},{7,5},{8,10},{10,8},{9,1... | collective-permute-start | bytes 1769480 | tf_op jit(solution)/shard_map/ppermute | solution.py:971
  34.9 15.2 %collective-permute-start.12 = (bf16[9,128,256]{2,1,0:T(8,128)(2,1)S(1)}, bf16[9,128,256]{2,1,0:T(8,128)(2,1)S(1)}, u32[]{:S(2)}, u32[]{:S(2)}) collective-permute-start(bf16[9,128,256]{2,1,0:T(8,128)(2,1)S(1)} %get-tuple-element.178), channel_id=1, source_target_pairs={{0,4},{4,0},{1,5},{5,1},{2,6},{6,2},{3,7},{7,3},{8,12},{12,8},{9,1... | collective-permute-start | bytes 1769480 | tf_op jit(solution)/shard_map/ppermute | solution.py:971
  42.8 11.7 %collective-permute-start.9 = (bf16[2,4,256,256]{3,2,1,0:T(8,128)(2,1)S(1)}, bf16[2,4,256,256]{3,2,1,0:T(8,128)(2,1)S(1)}, u32[]{:S(2)}, u32[]{:S(2)}) collective-permute-start(bf16[2,4,256,256]{3,2,1,0:T(8,128)(2,1)S(1)} %get-tuple-element.173.refs_2_.refs_1_), channel_id=1, source_target_pairs={{0,1},{1,0},{2,3},{3,2},{4,5},{5,4},{6,7},{7,6},{8,9},{9,8},{10,11... | collective-permute-start | bytes 3145736 | tf_op jit(solution)/shard_map/ppermute | solution.py:971
  51.0 11.4 %collective-permute-start.13 = (bf16[9,64,256]{2,1,0:T(8,128)(2,1)S(1)}, bf16[9,64,256]{2,1,0:T(8,128)(2,1)S(1)}, u32[]{:S(2)}, u32[]{:S(2)}) collective-permute-start(bf16[9,64,256]{2,1,0:T(8,128)(2,1)S(1)} %get-tuple-element.185), channel_id=1, source_target_pairs={{0,4},{4,0},{1,5},{5,1},{2,6},{6,2},{3,7},{7,3},{8,12},{12,8},{9,1... | collective-permute-start | bytes 884744 | tf_op jit(solution)/shard_map/ppermute | solution.py:971
  52.6 9.8 %collective-permute-start.14 = (bf16[9,64,256]{2,1,0:T(8,128)(2,1)S(1)}, bf16[9,64,256]{2,1,0:T(8,128)(2,1)S(1)}, u32[]{:S(2)}, u32[]{:S(2)}) collective-permute-start(bf16[9,64,256]{2,1,0:T(8,128)(2,1)S(1)} %get-tuple-element.187), channel_id=1, source_target_pairs={{0,2},{2,0},{1,3},{3,1},{4,6},{6,4},{5,7},{7,5},{8,10},{10,8},{9,1... | collective-permute-start | bytes 884744 | tf_op jit(solution)/shard_map/ppermute | solution.py:971
  53.2 6.1 %collective-permute-start.8 = (f32[2,4,8,256]{3,2,1,0:T(8,128)S(1)}, f32[2,4,8,256]{3,2,1,0:T(8,128)S(1)}, u32[]{:S(2)}, u32[]{:S(2)}) collective-permute-start(f32[2,4,8,256]{3,2,1,0:T(8,128)S(1)} %get-tuple-element.172.refs_2_), channel_id=1, source_target_pairs={{0,1},{1,0},{2,3},{3,2},{4,5},{5,4},{6,7},{7,6},{8,9},{9,8},{10,11... | collective-permute-start | bytes 196616 | tf_op jit(solution)/shard_map/ppermute | solution.py:971
  53.2 1.3 collective-permute-start.10
  57.2 19.3 %collective-permute-start.16 = (bf16[9,128,256]{2,1,0:T(8,128)(2,1)S(1)}, bf16[9,128,256]{2,1,0:T(8,128)(2,1)S(1)}, u32[]{:S(2)}, u32[]{:S(2)}) collective-permute-start(bf16[9,128,256]{2,1,0:T(8,128)(2,1)S(1)} %get-tuple-element.204), channel_id=1, source_target_pairs={{0,2},{2,0},{1,3},{3,1},{4,6},{6,4},{5,7},{7,5},{8,10},{10,8},{9,1... | collective-permute-start | bytes 1769480 | tf_op jit(solution)/shard_map/ppermute | solution.py:971
  58.8 17.8 %collective-permute-start.17 = (bf16[9,128,256]{2,1,0:T(8,128)(2,1)S(1)}, bf16[9,128,256]{2,1,0:T(8,128)(2,1)S(1)}, u32[]{:S(2)}, u32[]{:S(2)}) collective-permute-start(bf16[9,128,256]{2,1,0:T(8,128)(2,1)S(1)} %get-tuple-element.206), channel_id=1, source_target_pairs={{0,4},{4,0},{1,5},{5,1},{2,6},{6,2},{3,7},{7,3},{8,12},{12,8},{9,1... | collective-permute-start | bytes 1769480 | tf_op jit(solution)/shard_map/ppermute | solution.py:971
  63.2 10.5 %collective-permute-start.18 = (bf16[2,9,32,256]{3,2,1,0:T(8,128)(2,1)S(1)}, bf16[2,9,32,256]{3,2,1,0:T(8,128)(2,1)S(1)}, u32[]{:S(2)}, u32[]{:S(2)}) collective-permute-start(bf16[2,9,32,256]{3,2,1,0:T(8,128)(2,1)S(1)} %get-tuple-element.208), channel_id=1, source_target_pairs={{0,8},{8,0},{1,9},{9,1},{2,10},{10,2},{3,11},{11,3},{4,12},{12,4},... | collective-permute-start | bytes 884744 | tf_op jit(solution)/shard_map/ppermute | solution.py:971
  73.7 4.0 %copy-start.3 = (bf16[2,512]{1,0:T(2,128)(2,1)S(1)}, bf16[2,512]{1,0:T(2,128)(2,1)}, u32[]{:S(2)}) copy-start(bf16[2,512]{1,0:T(2,128)(2,1)} %refs_4_.9) | copy-start | bytes 6148
  73.9 16.0 %collective-permute-start.19 = (bf16[2,9,32,256]{3,2,1,0:T(8,128)(2,1)S(1)}, bf16[2,9,32,256]{3,2,1,0:T(8,128)(2,1)S(1)}, u32[]{:S(2)}, u32[]{:S(2)}) collective-permute-start(bf16[2,9,32,256]{3,2,1,0:T(8,128)(2,1)S(1)} %get-tuple-element.213.refs_1_), channel_id=1, source_target_pairs={{0,16},{16,0},{1,17},{17,1},{2,18},{18,2},{3,19},{19,3},{4,20},{20... | collective-permute-start | bytes 884744 | tf_op jit(solution)/shard_map/ppermute | solution.py:971
  76.5 1.2 collective-permute-start.15
  78.3 11.8 %collective-permute-start.20 = (f32[16,256]{1,0:T(8,128)S(1)}, f32[16,256]{1,0:T(8,128)S(1)}, u32[]{:S(2)}, u32[]{:S(2)}) collective-permute-start(f32[16,256]{1,0:T(8,128)S(1)} %get-tuple-element.214.refs_3_), channel_id=1, source_target_pairs={{0,16},{16,0},{1,17},{17,1},{2,18},{18,2},{3,19},{19,3},{4,20},{20... | collective-permute-start | bytes 49160 | tf_op jit(solution)/shard_map/ppermute | solution.py:971
  78.6 12.3 %collective-permute-start.22 = (bf16[9,64,256]{2,1,0:T(8,128)(2,1)S(1)}, bf16[9,64,256]{2,1,0:T(8,128)(2,1)S(1)}, u32[]{:S(2)}, u32[]{:S(2)}) collective-permute-start(bf16[9,64,256]{2,1,0:T(8,128)(2,1)S(1)} %get-tuple-element.218), channel_id=1, source_target_pairs={{0,4},{4,0},{1,5},{5,1},{2,6},{6,2},{3,7},{7,3},{8,12},{12,8},{9,1... | collective-permute-start | bytes 884744 | tf_op jit(solution)/shard_map/ppermute | solution.py:971
  80.1 10.8 %collective-permute-start.23 = (bf16[9,64,256]{2,1,0:T(8,128)(2,1)S(1)}, bf16[9,64,256]{2,1,0:T(8,128)(2,1)S(1)}, u32[]{:S(2)}, u32[]{:S(2)}) collective-permute-start(bf16[9,64,256]{2,1,0:T(8,128)(2,1)S(1)} %get-tuple-element.220), channel_id=1, source_target_pairs={{0,2},{2,0},{1,3},{3,1},{4,6},{6,4},{5,7},{7,5},{8,10},{10,8},{9,1... | collective-permute-start | bytes 884744 | tf_op jit(solution)/shard_map/ppermute | solution.py:971
  90.9 10.6 %collective-permute-start.21 = (bf16[2,10,32,256]{3,2,1,0:T(8,128)(2,1)S(1)}, bf16[2,10,32,256]{3,2,1,0:T(8,128)(2,1)S(1)}, u32[]{:S(2)}, u32[]{:S(2)}) collective-permute-start(bf16[2,10,32,256]{3,2,1,0:T(8,128)(2,1)S(1)} %get-tuple-element.216.refs_1_), channel_id=1, source_target_pairs={{0,8},{8,0},{1,9},{9,1},{2,10},{10,2},{3,11},{11,3},{4,12},{12,4},... | collective-permute-start | bytes 983048 | tf_op jit(solution)/shard_map/ppermute | solution.py:971
  91.7 15.2 %collective-permute-start.26 = (bf16[2,9,32,256]{3,2,1,0:T(8,128)(2,1)S(1)}, bf16[2,9,32,256]{3,2,1,0:T(8,128)(2,1)S(1)}, u32[]{:S(2)}, u32[]{:S(2)}) collective-permute-start(bf16[2,9,32,256]{3,2,1,0:T(8,128)(2,1)S(1)} %get-tuple-element.226), channel_id=1, source_target_pairs={{0,8},{8,0},{1,9},{9,1},{2,10},{10,2},{3,11},{11,3},{4,12},{12,4},... | collective-permute-start | bytes 884744 | tf_op jit(solution)/shard_map/ppermute | solution.py:971
  102.2 7.9 %collective-permute-start.24 = (bf16[10,64,256]{2,1,0:T(8,128)(2,1)S(1)}, bf16[10,64,256]{2,1,0:T(8,128)(2,1)S(1)}, u32[]{:S(2)}, u32[]{:S(2)}) collective-permute-start(bf16[10,64,256]{2,1,0:T(8,128)(2,1)S(1)} %get-tuple-element.223.refs_1_), channel_id=1, source_target_pairs={{0,4},{4,0},{1,5},{5,1},{2,6},{6,2},{3,7},{7,3},{8,12},{12,8},{9,1... | collective-permute-start | bytes 983048 | tf_op jit(solution)/shard_map/ppermute | solution.py:971
  103.8 7.6 %collective-permute-start.25 = (bf16[10,64,256]{2,1,0:T(8,128)(2,1)S(1)}, bf16[10,64,256]{2,1,0:T(8,128)(2,1)S(1)}, u32[]{:S(2)}, u32[]{:S(2)}) collective-permute-start(bf16[10,64,256]{2,1,0:T(8,128)(2,1)S(1)} %get-tuple-element.224.refs_3_), channel_id=1, source_target_pairs={{0,2},{2,0},{1,3},{3,1},{4,6},{6,4},{5,7},{7,5},{8,10},{10,8},{9,1... | collective-permute-start | bytes 983048 | tf_op jit(solution)/shard_map/ppermute | solution.py:971
  107.0 15.4 %collective-permute-start.29 = (bf16[2,9,32,256]{3,2,1,0:T(8,128)(2,1)S(1)}, bf16[2,9,32,256]{3,2,1,0:T(8,128)(2,1)S(1)}, u32[]{:S(2)}, u32[]{:S(2)}) collective-permute-start(bf16[2,9,32,256]{3,2,1,0:T(8,128)(2,1)S(1)} %get-tuple-element.231.refs_1_), channel_id=1, source_target_pairs={{0,16},{16,0},{1,17},{17,1},{2,18},{18,2},{3,19},{19,3},{4,20},{20... | collective-permute-start | bytes 884744 | tf_op jit(solution)/shard_map/ppermute | solution.py:971
  112.1 22.8 %collective-permute-start.27 = (bf16[10,128,256]{2,1,0:T(8,128)(2,1)S(1)}, bf16[10,128,256]{2,1,0:T(8,128)(2,1)S(1)}, u32[]{:S(2)}, u32[]{:S(2)}) collective-permute-start(bf16[10,128,256]{2,1,0:T(8,128)(2,1)S(1)} %get-tuple-element.229.refs_1_), channel_id=1, source_target_pairs={{0,2},{2,0},{1,3},{3,1},{4,6},{6,4},{5,7},{7,5},{8,10},{10,8},{9,1... | collective-permute-start | bytes 1966088 | tf_op jit(solution)/shard_map/ppermute | solution.py:971
  112.7 22.2 %collective-permute-start.28 = (bf16[10,128,256]{2,1,0:T(8,128)(2,1)S(1)}, bf16[10,128,256]{2,1,0:T(8,128)(2,1)S(1)}, u32[]{:S(2)}, u32[]{:S(2)}) collective-permute-start(bf16[10,128,256]{2,1,0:T(8,128)(2,1)S(1)} %get-tuple-element.230.refs_2_.refs_3_), channel_id=1, source_target_pairs={{0,4},{4,0},{1,5},{5,1},{2,6},{6,2},{3,7},{7,3},{8,12},{12,8},{9,1... | collective-permute-start | bytes 1966088 | tf_op jit(solution)/shard_map/ppermute | solution.py:971
  123.1 9.0 %collective-permute-start.30 = (bf16[2,9,32,256]{3,2,1,0:T(8,128)(2,1)S(1)}, bf16[2,9,32,256]{3,2,1,0:T(8,128)(2,1)S(1)}, u32[]{:S(2)}, u32[]{:S(2)}) collective-permute-start(bf16[2,9,32,256]{3,2,1,0:T(8,128)(2,1)S(1)} %get-tuple-element.233.refs_1_), channel_id=1, source_target_pairs={{0,8},{8,0},{1,9},{9,1},{2,10},{10,2},{3,11},{11,3},{4,12},{12,4},... | collective-permute-start | bytes 884744 | tf_op jit(solution)/shard_map/ppermute | solution.py:971
  132.7 8.1 %collective-permute-start.31 = (bf16[9,64,256]{2,1,0:T(8,128)(2,1)S(1)}, bf16[9,64,256]{2,1,0:T(8,128)(2,1)S(1)}, u32[]{:S(2)}, u32[]{:S(2)}) collective-permute-start(bf16[9,64,256]{2,1,0:T(8,128)(2,1)S(1)} %get-tuple-element.236.refs_1_), channel_id=1, source_target_pairs={{0,4},{4,0},{1,5},{5,1},{2,6},{6,2},{3,7},{7,3},{8,12},{12,8},{9,1... | collective-permute-start | bytes 884744 | tf_op jit(solution)/shard_map/ppermute | solution.py:971
  134.3 7.8 %collective-permute-start.32 = (bf16[9,64,256]{2,1,0:T(8,128)(2,1)S(1)}, bf16[9,64,256]{2,1,0:T(8,128)(2,1)S(1)}, u32[]{:S(2)}, u32[]{:S(2)}) collective-permute-start(bf16[9,64,256]{2,1,0:T(8,128)(2,1)S(1)} %get-tuple-element.237.refs_3_), channel_id=1, source_target_pairs={{0,2},{2,0},{1,3},{3,1},{4,6},{6,4},{5,7},{7,5},{8,10},{10,8},{9,1... | collective-permute-start | bytes 884744 | tf_op jit(solution)/shard_map/ppermute | solution.py:971
  142.8 13.2 %collective-permute-start.33 = (bf16[9,128,256]{2,1,0:T(8,128)(2,1)S(1)}, bf16[9,128,256]{2,1,0:T(8,128)(2,1)S(1)}, u32[]{:S(2)}, u32[]{:S(2)}) collective-permute-start(bf16[9,128,256]{2,1,0:T(8,128)(2,1)S(1)} %get-tuple-element.241.refs_1_), channel_id=1, source_target_pairs={{0,2},{2,0},{1,3},{3,1},{4,6},{6,4},{5,7},{7,5},{8,10},{10,8},{9,1... | collective-permute-start | bytes 1769480 | tf_op jit(solution)/shard_map/ppermute | solution.py:971
  143.4 12.9 %collective-permute-start.34 = (bf16[9,128,256]{2,1,0:T(8,128)(2,1)S(1)}, bf16[9,128,256]{2,1,0:T(8,128)(2,1)S(1)}, u32[]{:S(2)}, u32[]{:S(2)}) collective-permute-start(bf16[9,128,256]{2,1,0:T(8,128)(2,1)S(1)} %get-tuple-element.242.refs_2_), channel_id=1, source_target_pairs={{0,4},{4,0},{1,5},{5,1},{2,6},{6,2},{3,7},{7,3},{8,12},{12,8},{9,1... | collective-permute-start | bytes 1769480 | tf_op jit(solution)/shard_map/ppermute | solution.py:971
where the time goes:
time: 159 us
  Pallas kernels  71.8 us (45%)
  waiting for transfers between devices  57.5 us (36%)
  starting transfers between devices  27.2 us (17%)
  between operations  1.8 us (1%)
    pallas_call x33, Pallas kernels, run(): pl.pallas_call(inner, out_shape=tuple((member if index in hbm + scalars +...  71.8 us
    ppermute x35, waiting for transfers between devices, swap(): return lax.ppermute(values, axis_name, SWAP)  57.5 us
    ppermute x35, starting transfers between devices, swap(): return lax.ppermute(values, axis_name, SWAP)  27.2 us
  transfers between devices with their start and end apart: 35, of which 18 were waited for; matrix products, arithmetic and copies ran while one was open for 0% of the time, Pallas kernels for 33%

commit v1 on v0

--- a/solution.py
+++ b/solution.py
@@ -23,6 +23,11 @@
 UP_TAPS = (((0, 1),), ((0, 0), (1, 2)))
 
 
+GROUPS_TWO = ((3, ("x", "y", "near")), (3, ("y", "near", "x")), (3, ("near", "x", "y")))
+GROUPS_ONE = ((3, ("x", "y", "near")), (3, ("y", "near", "x")), (3, ("near", "x", "y")))
+AT = {"x": 0, "y": 1, "chan": 2, "near": 3, "far": 4}
+
+
 def dot(left, right, left_dim, right_dim):
     return lax.dot_general(
         left, right, (((left_dim,), (right_dim,)), ((), ())), preferred_element_type=F32
@@ -53,6 +58,17 @@
 
 def rows_at(index, count):
     return pl.ds(pl.multiple_of(index * count, count), count)
+
+
+def plane_at(image, plane):
+    return rows_at(4 * image + plane, PLANE)
+
+
+def squares_behind(ref, images):
+    parts = ref[ref.shape[0] - 16 :, :].astype(F32)
+    return jnp.concatenate(
+        [jnp.sum(parts[3 * b : 3 * b + 3], axis=0, keepdims=True) for b in range(images)], 0
+    )
 
 
 def rows_from(values, shift):
@@ -95,6 +111,14 @@
 def fetch(place, kernel, out, sem):
     share = out.shape[2]
     return pltpu.make_async_copy(kernel.at[:, :, rows_at(1 - place[2], share)], out, sem)
+
+
+def split_rows(values, count):
+    rows = []
+    for index in range(values.shape[0]):
+        rows += [part.astype(F32) for part in split_three(values[index : index + 1, :])]
+    blank = jnp.zeros((count - len(rows), values.shape[1]), F32)
+    return jnp.concatenate(rows + [blank], 0).astype(BF16)
 
 
 def style_kernel(
@@ -299,8 +323,8 @@
     conv,
     grad_conv,
     demod,
+    wide,
     square,
-    wide,
 ):
     share = own.shape[-1]
     columns = pl.ds(pl.multiple_of(place[2] * share, share), share)
@@ -332,31 +356,37 @@
                 grad = read_plane(wide, qy, qx) + dot(colours[image, plane], colour_weights[image], 0, 0)
                 row = row_of(demod, image) * row_of(valid, image)
                 grad = grad * leaky_slope(half_pre) * row
-                grad_conv[image, plane] = grad.astype(BF16)
+                grad_conv[plane_at(image, plane), :] = grad.astype(BF16)
                 product = column_sum(grad * rows)
                 products = product if products is None else products + product
         square[pl.ds(image, 1), :] = square_grad(products, row_of(demod, image))
 
     each(own.shape[0], one)
-
-
-def add_term(total, place, axis, kernel, tap, column, terms, outs):
-    at = tap
-    while at >= outs[0].shape[0]:
-        at, outs = at - outs[0].shape[0], outs[4:]
-    send, keep = outs[2 * axis : 2 * axis + 2]
-    half, share = send.shape[1], send.shape[2]
+    grad_conv[4 * PLANE * own.shape[0] :, :] = split_rows(square[...], 16)
+
+
+def group_of(groups, tap):
+    for index, (count, _) in enumerate(groups):
+        if tap < count:
+            return index, tap
+        tap -= count
+
+
+def first_taps(groups):
+    return [sum(count for count, _ in groups[:index]) for index in range(len(groups))]
+
+
+def add_term(groups, total, place, kernel, tap, column, lanes, terms, outs):
+    group, at = group_of(groups, tap)
+    axis = AT[groups[group][1][0]]
+    send, keep = outs[2 * group : 2 * group + 2]
+    half, share = send.shape[1], total.shape[1]
     columns = rows_at(column, share)
     for start, index, out in ((0, 1 - place[axis], send), (half, place[axis], keep)):
-        weight = kernel[tap, rows_at(index, half), columns].astype(F32)
-        value = total[start : start + half] + weight * terms[start : start + half]
-        out[at] = value.astype(out.dtype)
-
-
-def square_terms(place, axis, squared, grads):
-    half = squared.shape[1] // 2
-    rows = [squared[:, rows_at(1 - place[axis], half)], squared[:, rows_at(place[axis], half)]]
-    return 2.0 * exact(jnp.concatenate(rows, 1), grads[...], 0, 0)
+        rows = rows_at(index, half)
+        weight = kernel[tap, rows, columns].astype(F32)
+        value = total[start : start + half] + weight * terms[rows, :]
+        out[at, :, lanes] = value.astype(out.dtype)
 
 
 def shifted_kernel(scaled, moved):
@@ -368,82 +398,58 @@
     each(scaled.shape[0], one)
 
 
-def kernel_two_grad(
-    place,
-    scaled,
-    moved,
-    g_own,
-    g_other,
-    kernel,
-    styles,
-    q_own,
-    q_other,
-    *refs,
-):
-    outs, squared = refs[:-1], refs[-1]
+def kernel_two_grad(place, scaled, moved, g_own, g_other, kernel, styles, *refs):
+    outs, terms = refs[:-1], refs[-1]
     half = scaled.shape[3] // 2
-    squared[...] = styles[1] * styles[1]
-    for axis, column, grads, squares in (
-        (0, place[2], g_own, q_own),
-        (1, 1 - place[2], g_other, q_other),
-    ):
-        terms = square_terms(place, axis, squared, squares)
-        lanes = (rows_at(1 - place[axis], half), rows_at(place[axis], half))
-        for tap_y in range(3):
-            for tap_x in range(3):
-                left, right = [], []
-                for image in range(scaled.shape[0]):
-                    for qy in range(2):
-                        for qx in range(2):
-                            py, shift_y = source(qy, tap_y)
-                            px, shift_x = source(qx, tap_x)
-                            ref = scaled if shift_x == 0 else moved
-                            value = jnp.concatenate(
-                                [ref[image, 2 * py + px, :, at] for at in lanes], 1
-                            )
-                            left.append(rows_from(value, shift_y))
-                            right.append(grads[image, 2 * qy + qx])
-                total = dot(jnp.concatenate(left, 0), jnp.concatenate(right, 0), 0, 0)
-                tap = 3 * tap_y + tap_x
-                add_term(total, place, axis, kernel, tap, column, terms, outs)
-
-
-def kernel_one_grad(
-    place,
-    scaled,
-    g_own,
-    g_other,
-    kernel,
-    styles,
-    q_own,
-    q_other,
-    *refs,
-):
-    outs, (moved, squared) = refs[:-2], refs[-2:]
+    share = g_own.shape[1]
+    squared = styles[1] * styles[1]
+    for index, (column, grads) in enumerate(((place[2], g_own), (1 - place[2], g_other))):
+        terms[...] = 2.0 * exact(squared, squares_behind(grads, scaled.shape[0]), 0, 0)
+        for tap in range(9):
+            tap_y, tap_x = tap // 3, tap % 3
+            axis = AT[GROUPS_TWO[group_of(GROUPS_TWO, tap)[0]][1][0]]
+            lanes = (rows_at(1 - place[axis], half), rows_at(place[axis], half))
+            left, right = [], []
+            for image in range(scaled.shape[0]):
+                for qy in range(2):
+                    for qx in range(2):
+                        py, shift_y = source(qy, tap_y)
+                        px, shift_x = source(qx, tap_x)
+                        ref = scaled if shift_x == 0 else moved
+                        value = jnp.concatenate([ref[image, 2 * py + px, :, at] for at in lanes], 1)
+                        left.append(rows_from(value, shift_y))
+                        right.append(grads[plane_at(image, 2 * qy + qx), :])
+            total = dot(jnp.concatenate(left, 0), jnp.concatenate(right, 0), 0, 0)
+            columns = slice(index * share, (index + 1) * share)
+            add_term(GROUPS_TWO, total, place, kernel, tap, column, columns, terms, outs)
+
+
+def kernel_one_grad(place, scaled, g_own, g_other, kernel, styles, *refs):
+    outs, (moved, terms) = refs[:-2], refs[-2:]
     half = scaled.shape[2] // 2
-    images = scaled.shape[0]
+    images, share = scaled.shape[0], g_own.shape[1]
     for image in range(images):
         moved[image] = columns_from(scaled[image].astype(F32), 1).astype(BF16)
-    squared[...] = styles[0] * styles[0]
-    for axis, column, grads, squares in (
-        (0, place[2], g_own, q_own),
-        (1, 1 - place[2], g_other, q_other),
-    ):
-        terms = square_terms(place, axis, squared, squares)
-        lanes = (rows_at(1 - place[axis], half), rows_at(place[axis], half))
+    squared = styles[0] * styles[0]
+    for index, (column, grads) in enumerate(((place[2], g_own), (1 - place[2], g_other))):
+        terms[...] = 2.0 * exact(squared, squares_behind(grads, images), 0, 0)
         for qy in range(2):
             for qx in range(2):
-                right = jnp.concatenate([grads[b, 2 * qy + qx] for b in range(images)], 0)
+                planes = [grads[plane_at(b, 2 * qy + qx), :] for b in range(images)]
+                right = jnp.concatenate(planes, 0)
                 for shift_y, tap_y in UP_TAPS[qy]:
                     for shift_x, tap_x in UP_TAPS[qx]:
+                        tap = 3 * tap_y + tap_x
+                        axis = AT[GROUPS_ONE[group_of(GROUPS_ONE, tap)[0]][1][0]]
+                        lanes = (rows_at(1 - place[axis], half), rows_at(place[axis], half))
                         ref = moved if shift_x else scaled
                         left = [
                             rows_from(jnp.concatenate([ref[b, :, at] for at in lanes], 1), shift_y)
                             for b in range(images)
                         ]
                         total = dot(jnp.concatenate(left, 0), right, 0, 0)
-                        tap = 3 * tap_y + tap_x
-                        add_term(total, place, axis, kernel, tap, column, terms, outs)
+                        columns = slice(index * share, (index + 1) * share)
+                        add_term(GROUPS_ONE, total, place, kernel, tap, column, columns, terms, outs)
 
 
 def input_two_grad(
@@ -460,7 +466,8 @@
     grad_conv,
     square,
 ):
-    share = g_own.shape[3]
+    share = g_own.shape[1]
+    images = conv.shape[0]
     mine = pl.multiple_of(place[2] * share, share)
     theirs = pl.multiple_of((1 - place[2]) * share, share)
 
@@ -478,7 +485,7 @@
                         shift_y = source(qy, tap_y)[1]
                         tap = 3 * tap_y + tap_x
                         for grads, start in ((g_own, mine), (g_other, theirs)):
-                            left = rows_from(grads[image, 2 * qy + qx], -shift_y)
+                            left = rows_from(grads[plane_at(image, 2 * qy + qx), :], -shift_y)
                             right = kernel[tap, :, pl.ds(start, share)]
                             terms.setdefault(-shift_x, []).append((left, right, 1))
                 rows = gather_terms(terms)
@@ -494,21 +501,22 @@
                 )
                 row = row_of(demod, image) * row_of(styles.at[1], image)
                 grad = rows * leaky_slope(half_pre) * row
-                grad_conv[image, plane] = grad.astype(BF16)
+                grad_conv[plane_at(image, plane), :] = grad.astype(BF16)
                 product = column_sum(grad * values)
                 products = product if products is None else products + product
         square[pl.ds(image, 1), :] = square_grad(products, row_of(demod, image))
 
-    each(g_own.shape[0], one)
+    each(images, one)
+    grad_conv[4 * PLANE * images :, :] = split_rows(square[...], 16)
 
 
 def input_one_grad(
     place, g_own, g_other, kernel, features, styles, grad_features, sums
 ):
-    share = g_own.shape[3]
+    share = g_own.shape[1]
     mine = pl.multiple_of(place[2] * share, share)
     theirs = pl.multiple_of((1 - place[2]) * share, share)
-    images = g_own.shape[0]
+    images = features.shape[0]
     terms = {}
     for qy in range(2):
         for qx in range(2):
@@ -517,7 +525,10 @@
                     tap = 3 * tap_y + tap_x
                     for grads, start in ((g_own, mine), (g_other, theirs)):
                         left = jnp.concatenate(
-                            [rows_from(grads[b, 2 * qy + qx], -shift_y) for b in range(images)], 0
+                            [
+                                rows_from(grads[plane_at(b, 2 * qy + qx), :], -shift_y)
+                                for b in range(images)
+                            ], 0
                         )
                         right = kernel[tap, :, pl.ds(start, share)]
                         terms.setdefault(-shift_x, []).append((left, right, 1))
@@ -620,7 +631,9 @@
     return jnp.where(column == centre, 0.75, 0.0) + jnp.where(column == near, 0.25, 0.0)
 
 
-def rgb_kernel(valid, bias, own, other, rgb_in, grad_rgb, rgb_out, grad_in, sums, raster):
+def rgb_kernel(
+    valid, bias, own, other, rgb_in, grad_rgb, rgb_out, grad_in, grad_latent, pack, raster
+):
     images = rgb_in.shape[0]
     double = upsampling(RES, HALF)
     lane = lax.broadcasted_iota(jnp.int32, (HALF, PLANE), 1)
@@ -634,7 +647,8 @@
             plane = 2 * qy + qx
             rows = []
             for image in range(images):
-                both = own[image, plane] + other[image, plane]
+                rows_here = rows_at(1 + 4 * image + plane, 8)
+                both = own[rows_here, :] + other[rows_here, :]
                 rows += [mask * both[colour : colour + 1] for colour in range(3)]
             found = exact(jnp.concatenate(rows, 0), choose, 1, 0)
             for index in range(3 * images):
@@ -654,11 +668,18 @@
             grad = grad_rgb[image, colour].astype(F32) * keep
             grad_in[image, colour] = exact(exact(double, grad, 0, 0), double, 1, 0)
             biases[colour] = biases[colour] + jnp.sum(grad, keepdims=True)
-    sums[...] = jnp.concatenate(
-        [jnp.broadcast_to(member, (1, 128)) for member in [squares] + biases]
-        + [jnp.zeros((4, 128), F32)],
-        0,
-    )
+    total = own[:8, :] + other[:8, :]
+    for image in range(images):
+        grad_latent[image : image + 1, :] = jnp.concatenate(
+            [total[2 * image : 2 * image + 1], total[2 * image + 1 : 2 * image + 2]], 1
+        )
+    scalars = total[2 * images : 2 * images + 1]
+    lane = lax.broadcasted_iota(jnp.int32, scalars.shape, 1)
+    for index, value in enumerate([squares] + biases):
+        scalars = scalars + jnp.where(lane == 4 + index, value, 0.0)
+    for image in range(images):
+        scalars = scalars + jnp.where(lane == 8, valid[image : image + 1, :], 0.0)
+    pack[...] = jnp.concatenate([scalars, jnp.zeros((15, scalars.shape[1]), F32)], 0)
 
 
 def style_grads_kernel(
@@ -676,7 +697,10 @@
     a1,
     a2,
     a3,
-    grads,
+    latent,
+    rgb_grad,
+    planes,
+    pack,
     crossing,
 ):
     images, share = style_sums.shape
@@ -685,8 +709,8 @@
     for layer, (own, other, squares, sums) in enumerate(
         ((own_one, other_one, squares_one, style_sums), (own_two, other_two, squares_two, None))
     ):
-        back = exact(own[...], squares[:, mine], 1, 1) + exact(
-            other[...], squares[:, theirs], 1, 1
+        back = exact(squares_behind(own, images), squares[:, mine], 1, 1) + exact(
+            squares_behind(other, images), squares[:, theirs], 1, 1
         )
         if sums is None:
             direct = jnp.concatenate([sums_one[b, 2:3, :] for b in range(images)], 0)
@@ -694,11 +718,10 @@
             direct = sums[...]
         rows.append(direct + 2.0 * styles[layer] * back)
     rows.append(jnp.concatenate([sums_two[b, 2:3, :] for b in range(images)], 0))
-    grads[...] = jnp.concatenate(rows, 0)
-    latent = None
+    grad_latent = None
     for row, affine in zip(rows, (a1, a2, a3)):
         part = exact(row, affine[...].astype(F32), 1, 1)
-        latent = part if latent is None else latent + part
+        grad_latent = part if grad_latent is None else grad_latent + part
     lane = lax.broadcasted_iota(jnp.int32, (1, share), 1)
     scalars = jnp.zeros((1, share), F32)
     for index, (sums, row) in enumerate(
@@ -708,73 +731,50 @@
         for image in range(1, images):
             total = total + sums[image, row : row + 1, :]
         scalars = scalars + jnp.where(lane == index, jnp.sum(total, keepdims=True), 0.0)
-    pieces = [latent[b : b + 1, h * share : (h + 1) * share] for b in range(images) for h in (0, 1)]
-    blank = jnp.zeros((crossing.shape[0] - len(pieces) - 1, share), F32)
-    crossing[...] = jnp.concatenate(pieces + [scalars, blank], 0)
-
-
-def pack_kernel(
-    valid,
-    own,
-    other,
-    grads,
-    latent,
-    sums_one,
-    sums_two,
-    rgb_grad,
-    rgb_sums,
-    grad_latent,
-    pack,
-):
-    images, share = latent.shape[0], grads.shape[1]
-    total = own[...] + other[...]
-    count = 2 * images
+    pieces = [grad_latent[b : b + 1, h * share : (h + 1) * share] for b in range(images) for h in (0, 1)]
+    blank = jnp.zeros((8 - len(pieces) - 1, share), F32)
+    crossing[:8, :] = jnp.concatenate(pieces + [scalars, blank], 0)
     for image in range(images):
-        grad_latent[image : image + 1, :] = jnp.concatenate(
-            [total[2 * image : 2 * image + 1], total[2 * image + 1 : 2 * image + 2]], 1
-        )
+        for plane in range(4):
+            crossing[rows_at(1 + 4 * image + plane, 8), :] = planes[image, plane]
     values = latent[...].astype(F32)
-    rows = [values[:, :share], values[:, share:], grads[...]]
+    packed = [values[:, :share], values[:, share:]] + rows
     for sums in (sums_one, sums_two):
         bias = sums[0, 0:1, :]
         for image in range(1, images):
             bias = bias + sums[image, 0:1, :]
-        rows.append(bias)
-    rows.append(rgb_grad[:3, :])
-    lane = lax.broadcasted_iota(jnp.int32, (1, share), 1)
-    scalars = total[count : count + 1]
-    wide = jnp.concatenate([rgb_sums[...]] * (share // 128), 1)
-    for index in range(4):
-        scalars = scalars + jnp.where(lane == 4 + index, wide[index : index + 1], 0.0)
-    for image in range(images):
-        scalars = scalars + jnp.where(lane == 8, valid[image : image + 1, :], 0.0)
-    rows.append(scalars)
-    used = sum(member.shape[0] for member in rows)
-    if used < pack.shape[0]:
-        rows.append(jnp.zeros((pack.shape[0] - used, share), F32))
-    pack[...] = jnp.concatenate(rows, 0)
-
-
-def spread_kernel(place, *refs, images):
-    packs, outs, parts = refs[:-14], refs[-14:-1], refs[-1]
-    grads, biases, points = outs[0:3], outs[3:6], outs[6:8]
-    rgb_grad, gains, rms, rgb_bias, everything = outs[8:]
+        packed.append(bias)
+    packed += [rgb_grad[:3, :], jnp.zeros((1, share), F32)]
+    pack[...] = jnp.concatenate(packed, 0)
+
+
+def relay_kernel(source, out):
+    out[...] = source[...]
+
+
+def collect(place, packs, groups, everything):
     if len(packs) == 1:
         everything[...] = packs[0][...]
-    else:
-        own, got_own, other, got_other = packs
-        tap, rows = own.shape[0] - 1, everything.shape[1]
-        for index in range(8):
-            at = pl.ds(rows * index, rows)
-            near, far, second = (index >> 1) & 1, index & 1, index >> 2
-            line = 8 * far + 4 * near
-            for own_ref, other_ref, first_x, first_y in (
-                (own, other, place[0], place[1]),
-                (got_own, got_other, 1 - place[0], 1 - place[1]),
-            ):
-                parts[0, line + 2 * second + first_x] = own_ref[tap, at, :].astype(F32)
-                parts[1, line + 2 * first_y + second] = other_ref[tap, at, :].astype(F32)
-        everything[...] = parts[0] + parts[1]
+        return
+    taps, order = groups[0]
+    weight = {"far": 8, "near": 4, "y": 2, "x": 1}
+    rows, share = everything.shape[1:]
+    for index in range(8):
+        at = pl.ds(rows * index, rows)
+        device = (
+            weight["far"] * (index & 1)
+            + weight[order[2]] * ((index >> 1) & 1)
+            + weight[order[1]] * (index >> 2)
+        )
+        mine = place[AT[order[0]]]
+        for ref, first in zip(packs, (mine, 1 - mine)):
+            both = ref[taps, at, :].astype(F32)
+            everything[device + weight[order[0]] * first] = both[:, :share] + both[:, share:]
+
+
+def spread_kernel(place, *refs, images, groups):
+    packs, outs, everything = refs[:-10], refs[-10:-1], refs[-1]
+    collect(place, packs, groups, everything)
     count = everything.shape[0]
 
     def rows(start, size):
@@ -784,137 +784,154 @@
     at = 2 * images
     for layer in range(3):
         grad = rows(at, images)
-        grads[layer][...] = exact(latent, grad, 0, 0)
-        biases[layer][...] = jnp.sum(grad, axis=0, keepdims=True)
+        outs[layer][...] = exact(latent, grad, 0, 0)
+        outs[3 + layer][...] = jnp.sum(grad, axis=0, keepdims=True)
         at += images
     total = everything[0]
     for device in range(1, count):
         total = total + everything[device]
-    points[0][...] = total[at : at + 1]
-    points[1][...] = total[at + 1 : at + 2]
-    rgb_grad[...] = total[at + 2 : at + 5]
-    scalars = total[at + 5 : at + 6]
+    outs[6][...] = total[at : at + 1]
+    outs[7][...] = total[at + 1 : at + 2]
+    outs[8][...] = total[at + 2 : at + 5]
+
+
+def scalars_kernel(place, *refs, groups):
+    packs, (gains, rms, rgb_bias, everything) = refs[:-4], refs[-4:]
+    collect(place, packs, groups, everything)
+    scalars = everything[0, 0:1, :]
+    for device in range(1, everything.shape[0]):
+        scalars = scalars + everything[device, 0:1, :]
     lane = lax.broadcasted_iota(jnp.int32, scalars.shape, 1)
-
-    def scalar(index):
-        return jnp.sum(jnp.where(lane == index, scalars, 0.0))
-
     share = scalars.shape[1]
     real = jnp.sum(jnp.where(lane == 8, scalars, 0.0), keepdims=True)
     entries = jnp.where(lane == 4, 3.0 * RES * RES, 2.0 * share * RES * RES)
-    roots = jnp.sqrt(scalars / (real * entries))
-
-    def root(index):
-        return jnp.sum(jnp.where(lane == index, roots, 0.0))
-
-    for index, lane_at in enumerate((0, 1, 4)):
-        rms[index] = root(lane_at)
+    roots = jnp.sqrt(jnp.abs(scalars) / (real * entries))
+
+    def pick(values, index):
+        return jnp.sum(jnp.where(lane == index, values, 0.0))
+
+    for index, at in enumerate((0, 1, 4)):
+        rms[index] = pick(roots, at)
     for index in range(2):
-        gains[index] = scalar(2 + index)
+        gains[index] = pick(scalars, 2 + index)
     for index in range(3):
-        rgb_bias[index] = scalar(5 + index)
-
-
-def second_kernel(
-    place, keep_own, got_own, keep_other, got_other, s_own, k_own, s_other, k_other
-):
-    count = s_own.shape[1]
-    for axis, keep, got, send, kept in (
-        (1, keep_own, got_own, s_own, k_own),
-        (0, keep_other, got_other, s_other, k_other),
-    ):
-        away, here = rows_at(1 - place[axis], count), rows_at(place[axis], count)
-
-        def one(tap, keep=keep, got=got, send=send, kept=kept, away=away, here=here):
-            total = keep[tap, away, :] + got[tap, away, :].astype(F32)
+        rgb_bias[index] = pick(scalars, 5 + index)
+
+
+def fold_kernel(place, *refs, groups, stage):
+    count = len(groups)
+    sources, outs = refs[: 2 * count], refs[2 * count :]
+    for group, (taps, order) in enumerate(groups):
+        kept, got = sources[2 * group : 2 * group + 2]
+        send, keep = outs[2 * group : 2 * group + 2]
+        index = place[AT[order[stage]]]
+        away, here = rows_at(1 - index, send.shape[1]), rows_at(index, send.shape[1])
+
+        def one(tap, kept=kept, got=got, send=send, keep=keep, away=away, here=here):
+            total = kept[tap, away, :] + got[tap, away, :].astype(F32)
             send[tap] = total.astype(BF16)
-            kept[tap] = keep[tap, here, :] + got[tap, here, :].astype(F32)
-
-        each(keep.shape[0], one)
-
-
-def merge_kernel(place, keep_own, got_own, keep_other, got_other, send, keep):
-    count = send.shape[2]
-    away, here = rows_at(1 - place[3], count), rows_at(place[3], count)
-    for order, (kept, got) in enumerate(((keep_own, got_own), (keep_other, got_other))):
-
-        def one(tap, order=order, kept=kept, got=got):
-            total = kept[tap, away, :] + got[tap, away, :].astype(F32)
-            send[order, tap] = total.astype(BF16)
-            keep[order, tap] = kept[tap, here, :] + got[tap, here, :].astype(F32)
+            keep[tap] = kept[tap, here, :] + got[tap, here, :].astype(F32)
 
         each(kept.shape[0], one)
 
 
-def across_kernel(kept, got, out):
-    for order in range(kept.shape[0]):
-
-        def one(tap, order=order):
-            out[order, tap] = (kept[order, tap] + got[order, tap].astype(F32)).astype(BF16)
-
-        each(kept.shape[1], one)
-
-
-def total_kernel(place, mine, got, *refs):
-    packs, out = refs[:-1], refs[-1]
+def put_pack(out, tap, place_far, pack):
+    for order, part in enumerate(split_three(pack[...])[:2]):
+        columns = slice(order * pack.shape[1], (order + 1) * pack.shape[1])
+        out[tap, rows_at(place_far, pack.shape[0]), columns] = part
+
+
+def across_kernel(place, *refs, groups):
+    out = refs[-1]
+    for group, first in enumerate(first_taps(groups)):
+        kept, got = refs[2 * group : 2 * group + 2]
+
+        def one(tap, kept=kept, got=got, first=first):
+            out[first + tap] = (kept[tap] + got[tap].astype(F32)).astype(BF16)
+
+        each(kept.shape[0], one)
+    if len(refs) > 2 * len(groups) + 1:
+        out[9] = jnp.zeros(out.shape[1:], BF16)
+        put_pack(out, 9, place[4], refs[-2])
+
+
+def total_kernel(place, mine, got, *refs, groups):
+    packs, outs = refs[: -len(groups)], refs[-len(groups) :]
+    extra = groups[0][0]
     for index, pack in enumerate(packs):
-        rows = rows_at(place[4] if index == 0 else 1 - place[4], pack.shape[0])
-        for order, part in enumerate(split_three(pack[...])[:2]):
-            out[order, out.shape[1] - 1, rows, :] = part
-    for order in range(mine.shape[0]):
-
-        def one(tap, order=order):
-            total = mine[order, tap].astype(F32) + got[order, tap].astype(F32)
-            out[order, tap] = total.astype(BF16)
-
-        each(mine.shape[1], one)
-
-
-def join_near_kernel(place, own, got, *outs):
-    count = own.shape[2]
-    here, away = rows_at(place[3], count), rows_at(1 - place[3], count)
-    for order, out in enumerate(outs):
-
-        def one(tap, order=order, out=out):
-            out[tap, here, :] = own[order, tap]
-            out[tap, away, :] = got[order, tap]
-
-        each(own.shape[1], one)
-
-
-def join_pair_kernel(place, own, got_own, other, got_other, half_own, half_other):
-    count = own.shape[1]
-    for axis, mine, theirs, out in ((1, own, got_own, half_own), (0, other, got_other, half_other)):
-        here, away = rows_at(place[axis], count), rows_at(1 - place[axis], count)
-
-        def one(tap, mine=mine, theirs=theirs, out=out, here=here, away=away):
-            out[tap, here, :] = mine[tap]
-            out[tap, away, :] = theirs[tap]
+        put_pack(outs[0], extra, place[4] if index == 0 else 1 - place[4], pack)
+    if mine.shape[0] > 9:
+        outs[0][extra] = (mine[9].astype(F32) + got[9].astype(F32)).astype(BF16)
+    for out, first, (taps, _) in zip(outs, first_taps(groups), groups):
+
+        def one(tap, out=out, first=first):
+            total = mine[first + tap].astype(F32) + got[first + tap].astype(F32)
+            out[tap] = total.astype(BF16)
+
+        each(taps, one)
+
+
+def join_kernel(place, *refs, groups, stage):
+    count = len(groups)
+    sources, outs = refs[: 2 * count], refs[2 * count :]
+    for group, (taps, order) in enumerate(groups):
+        own, got = sources[2 * group : 2 * group + 2]
+        out = outs[group]
+        index = place[AT[order[stage]]]
+        here, away = rows_at(index, own.shape[1]), rows_at(1 - index, own.shape[1])
+
+        def one(tap, own=own, got=got, out=out, here=here, away=away):
+            out[tap, here, :] = own[tap]
+            out[tap, away, :] = got[tap]
 
         each(out.shape[0], one)
 
 
-def finish_kernel(place, own, other, *refs, away, first):
-    out, held, sems = refs[-3:]
-    _, taps, half, share = held.shape
-
-    def copy(tap, order):
-        column, index = (place[2], place[0]) if order == 0 else (1 - place[2], place[1])
+def finish_kernel(place, *refs, groups, away, between=None):
+    parts, (out, held, sems) = refs[: len(groups)], refs[-3:]
+    _, half, channels = held.shape
+    share = channels // 2
+    starts = first_taps(groups)
+    for part, first, (taps, order) in zip(parts, starts, groups):
+        index = place[AT[order[0]]]
         rows = rows_at(1 - index if away else index, half)
-        block = out.at[first + tap, rows, rows_at(column, share)]
-        return pltpu.make_async_copy(held.at[order, tap], block, sems.at[order, tap])
-
-    def one(tap):
-        for order, part in enumerate((own, other)):
-            held[order, tap] = part[tap].astype(F32)
-            copy(tap, order).start()
-
-    def last(tap):
-        for order in range(2):
-            copy(tap, order).wait()
-
-    each(taps, one)
-    each(taps, last)
+
+        def copy(tap, rows=rows):
+            return pltpu.make_async_copy(held.at[tap], out.at[tap, rows, :], sems.at[tap])
+
+        def one(tap, part=part, first=first, copy=copy):
+            for side, column in enumerate((place[2], 1 - place[2])):
+                value = part[tap, :, side * share : (side + 1) * share]
+                held[first + tap, :, rows_at(column, share)] = value.astype(F32)
+            copy(first + tap).start()
+
+        each(taps, one)
+    if between is not None:
+        between()
+    for first, (taps, order) in zip(starts, groups):
+        index = place[AT[order[0]]]
+        rows = rows_at(1 - index if away else index, half)
+
+        def last(tap, rows=rows, first=first):
+            pltpu.make_async_copy(
+                held.at[first + tap], out.at[first + tap, rows, :], sems.at[first + tap]
+            ).wait()
+
+        each(taps, last)
+
+
+def finish_scalars_kernel(place, *refs, groups):
+    count = len(groups)
+    parts, own, (out, gains, rms, rgb_bias, held, sems, everything) = (
+        refs[:count],
+        refs[count + 1],
+        refs[-7:],
+    )
+
+    def between():
+        scalars_kernel(place, own, parts[0], gains, rms, rgb_bias, everything, groups=groups)
+
+    finish_kernel(place, *parts, out, held, sems, groups=groups, away=True, between=between)
 
 
 def call(body, outs, scratch=(), smem=0, after=(), hbm=(), scalars=(), plain=(), loose=(), whole=(), micros=0, aliases=None):
@@ -948,6 +965,7 @@
             + (any_space,),
             scratch_shapes=scratch,
             input_output_aliases=aliases or {},
+            name=getattr(body, "func", body).__name__,
             compiler_params=pltpu.CompilerParams(vmem_limit_bytes=VMEM_BYTES),
             cost_estimate=pl.CostEstimate(
                 flops=2**10 + int(micros * 1.1e9), bytes_accessed=2**10, transcendentals=0
@@ -963,8 +981,11 @@
     return jax.ShapeDtypeStruct(dims, kind)
 
 
-def kernel_shapes(taps, rows, cols):
-    return (shape(taps, rows, cols, kind=BF16), shape(taps, rows, cols))
+def group_shapes(groups, rows, cols):
+    found = ()
+    for taps, _ in groups:
+        found += (shape(taps, rows, cols, kind=BF16), shape(taps, rows, cols))
+    return found
 
 
 def swap(values, axis_name):
@@ -984,91 +1005,113 @@
 
 
 class Reduction:
-    def __init__(self, place, parts, first=0):
-        self.place, self.first, self.taps = place, first, parts[0].shape[0]
-        self.sent_own, self.keep_own, self.sent_other, self.keep_other = parts
-        self.got = swap(self.sent_own, "x"), swap(self.sent_other, "y")
-
-    def second(self, token, micros=0):
-        taps, rows, cols = self.keep_own.shape
+    def __init__(self, place, groups, parts):
+        self.place, self.groups = place, groups
+        self.exchange(parts[0::2], 0)
+        self.keep = parts[1::2]
+
+    def exchange(self, parts, stage):
+        self.got = [swap(part, order[stage]) for part, (_, order) in zip(parts, self.groups)]
+
+    def pairs(self, own):
+        return [member for pair in zip(own, self.got) for member in pair]
+
+    def fold(self, token, stage, micros=STAGE):
+        _, rows, cols = self.keep[0].shape
         parts, token = call(
-            second_kernel,
-            kernel_shapes(taps, rows // 2, cols) * 2,
+            functools.partial(fold_kernel, groups=self.groups, stage=stage),
+            group_shapes(self.groups, rows // 2, cols),
             smem=1,
-            after=(token,),
+            after=token if isinstance(token, tuple) else (token,),
             micros=micros,
-        )(self.place, self.keep_own, self.got[0], self.keep_other, self.got[1])
-        sent_own, self.keep_own, sent_other, self.keep_other = parts
-        self.got = swap(sent_own, "y"), swap(sent_other, "x")
+        )(self.place, *self.pairs(self.keep))
+        self.exchange(parts[0::2], stage)
+        self.keep = parts[1::2]
         return token
 
-    def near(self, token, micros=0):
-        taps, rows, cols = self.keep_own.shape
-        piece = (2, taps, rows // 2, cols)
-        (send, self.keep), token = call(
-            merge_kernel, (shape(*piece, kind=BF16), shape(*piece)), smem=1, after=(token,), micros=micros
-        )(self.place, self.keep_own, self.got[0], self.keep_other, self.got[1])
-        self.got = swap(send, "near")
-        return token
-
-    def across(self, token, micros=0):
-        out = shape(*self.keep.shape, kind=BF16)
-        self.own, token = call(across_kernel, out, after=(token,), micros=micros)(
-            self.keep, self.got
-        )
+    def across(self, token, *packs, micros=STAGE):
+        _, rows, cols = self.keep[0].shape
+        self.own, token = call(
+            functools.partial(across_kernel, groups=self.groups),
+            shape(9 + len(packs), rows, cols, kind=BF16),
+            smem=1,
+            after=token if isinstance(token, tuple) else (token,),
+            micros=micros,
+        )(self.place, *self.pairs(self.keep), *packs)
         self.got = swap(self.own, "far")
         return token
 
-    def total(self, token, *packs, micros=0):
+    def total(self, token, *packs, micros=STAGE):
         if lax.axis_size("block") > 1:
             self.own = lax.psum(self.own.astype(F32) + self.got.astype(F32), "block").astype(BF16)
             self.got = jnp.zeros_like(self.own)
-        orders, taps, rows, cols = self.own.shape
-        out = shape(orders, taps + min(len(packs), 1), rows, cols, kind=BF16)
-        self.own, token = call(total_kernel, out, smem=1, after=(token,), micros=micros)(
-            self.place, self.own, self.got, *packs
+        taps, rows, cols = self.own.shape
+        outs = [shape(count, rows, cols, kind=BF16) for count, _ in self.groups]
+        if packs or taps > 9:
+            outs[0] = shape(self.groups[0][0] + 1, rows, cols, kind=BF16)
+        self.own, token = call(
+            functools.partial(total_kernel, groups=self.groups),
+            tuple(outs),
+            smem=1,
+            after=token if isinstance(token, tuple) else (token,),
+            micros=micros,
+        )(self.place, self.own, self.got, *packs)
+        self.exchange(self.own, 2)
+        return token
+
+    def join(self, token, stage, micros=STAGE):
+        outs = tuple(
+            shape(part.shape[0], 2 * part.shape[1], part.shape[2], kind=BF16) for part in self.own
         )
-        self.got = swap(self.own, "near")
+        self.own, token = call(
+            functools.partial(join_kernel, groups=self.groups, stage=stage),
+            outs,
+            smem=1,
+            after=token if isinstance(token, tuple) else (token,),
+            micros=micros,
+        )(self.place, *self.pairs(self.own))
+        self.exchange(self.own, stage - 1)
         return token
 
-    def join_near(self, token, micros=0):
-        _, taps, rows, cols = self.own.shape
-        quarter = shape(taps, 2 * rows, cols, kind=BF16)
-        self.own, token = call(
-            join_near_kernel, (quarter,) * 2, smem=1, after=(token,), micros=micros
-        )(self.place, self.own, self.got)
-        self.got = swap(self.own[0], "y"), swap(self.own[1], "x")
-        return token
-
-    def join_pair(self, token, micros=0):
-        taps, rows, cols = self.own[0].shape
-        half = shape(taps, 2 * rows, cols, kind=BF16)
-        self.own, token = call(
-            join_pair_kernel, (half,) * 2, smem=1, after=(token,), micros=micros
-        )(
-            self.place, self.own[0], self.got[0], self.own[1], self.got[1]
-        )
-        self.got = swap(self.own[0], "x"), swap(self.own[1], "y")
-        return token
-
     def finish_half(self, token, parts, out, away):
-        taps, (_, half, share) = self.taps, parts[0].shape
+        _, half, cols = parts[0].shape
+        last = 1 + len(parts)
         return call(
-            functools.partial(finish_kernel, away=away, first=self.first),
-            shape(9, 2 * half, 2 * share),
-            [pltpu.VMEM((2, taps, half, share), F32), pltpu.SemaphoreType.DMA((2, taps))],
+            functools.partial(finish_kernel, groups=self.groups, away=away),
+            shape(9, 2 * half, cols),
+            [pltpu.VMEM((9, half, cols), F32), pltpu.SemaphoreType.DMA((9,))],
+            smem=1,
+            after=token if isinstance(token, tuple) else (token,),
+            hbm=(0,),
+            loose=(last,) if out else (),
+            aliases={last: 0} if out else None,
+            micros=0,
+        )(self.place, *parts, *out)
+
+    def finish_own(self, token):
+        return self.finish_half(token, self.own, (), False)
+
+    def finish(self, token, out):
+        return self.finish_half(token, self.got, (out,), True)
+
+    def finish_scalars(self, token, out, devices):
+        _, half, cols = self.got[0].shape
+        last = 1 + len(self.got)
+        return call(
+            functools.partial(finish_scalars_kernel, groups=self.groups),
+            (shape(9, 2 * half, cols), shape(2), shape(3), shape(3)),
+            [
+                pltpu.VMEM((9, half, cols), F32),
+                pltpu.SemaphoreType.DMA((9,)),
+                pltpu.VMEM((devices, 16, cols // 2), F32),
+            ],
             smem=1,
             after=(token,),
             hbm=(0,),
-            loose=(3,) if out else (),
-            aliases={3: 0} if out else None,
-        )(self.place, *parts, *out)
-
-    def finish_own(self, token, out=()):
-        return self.finish_half(token, self.own, out, False)
-
-    def finish(self, token, out):
-        return self.finish_half(token, self.got, (out,), True)
+            scalars=(1, 2, 3),
+            loose=(last,),
+            aliases={last: 0},
+        )(self.place, *self.got, out, self.own[0])
 
 
 def gather_packs(pack):
@@ -1111,13 +1154,18 @@
     flat_one = kernel_one.reshape(9, share, channels)
     flat_two = kernel_two.reshape(9, share, channels)
     plane_shape = (images, 4, PLANE, share)
+    grad_kind = shape(images * 4 * PLANE + 16, share, kind=BF16)
     half = share // 2
     wide = pltpu.VMEM((share // 128, HALF, 2, RES, 128), F32)
 
     send_kind = shape(9, share, share, kind=BF16)
     (styles, scaled_one, send_one), token = call(
         style_kernel,
-        (shape(3, images, share), shape(images, PLANE, share, kind=BF16), send_kind),
+        (
+            shape(3, images, share),
+            shape(images, PLANE, share, kind=BF16),
+            send_kind,
+        ),
         [pltpu.SemaphoreType.DMA],
         smem=1,
         loose=tuple(range(2, 10)),
@@ -1191,15 +1239,10 @@
     squares_two, mine_two, theirs_two, add_two, colour_weights, token = layer_squares(
         1, flat_two, bias_two, token
     )
-    (conv_two, grad_conv_two, demod_two, square_two), token = call(
+    (conv_two, grad_conv_two, demod_two), token = call(
         conv_two_kernel,
-        (
-            shape(*plane_shape),
-            shape(*plane_shape, kind=BF16),
-            shape(images, share),
-            shape(images, share),
-        ),
-        [wide],
+        (shape(*plane_shape), grad_kind, shape(images, share)),
+        [wide, pltpu.VMEM((images, share), F32)],
         smem=1,
         after=(token,),
     )(
@@ -1218,14 +1261,15 @@
         grad_features,
     )
     grad_conv_two_other = swap(grad_conv_two, "chan")
-    square_two_other = swap(square_two, "chan")
     shifted_two, token = call(
         shifted_kernel, shape(*plane_shape, kind=BF16), after=(token,)
     )(scaled_two)
+    devices = lax.axis_size(DP)
+    alone = lax.axis_size("block") == 1
     parts_two, token = call(
         kernel_two_grad,
-        kernel_shapes(9, half, share) * 2,
-        [pltpu.VMEM((images, share), F32)],
+        group_shapes(GROUPS_TWO, half, channels),
+        [pltpu.VMEM((share, share), F32)],
         smem=1,
         after=(token,),
     )(
@@ -1236,13 +1280,12 @@
         grad_conv_two_other,
         flat_two,
         styles,
-        square_two,
-        square_two_other,
-    )
-    reduce_two = Reduction(place, parts_two)
-    (grad_scaled_two, grad_conv_one, square_one), token = call(
+    )
+    reduce_two = Reduction(place, GROUPS_TWO, parts_two)
+    (grad_scaled_two, grad_conv_one), token = call(
         input_two_grad,
-        (shape(*plane_shape), shape(*plane_shape, kind=BF16), shape(images, share)),
+        (shape(*plane_shape), grad_kind),
+        [pltpu.VMEM((images, share), F32)],
         smem=1,
         after=(token,),
     )(
@@ -1257,7 +1300,37 @@
         styles,
     )
     grad_conv_one_other = swap(grad_conv_one, "chan")
-    square_one_other = swap(square_one, "chan")
+    sums_one, token = call(
+        outputs_one_kernel, shape(images, 8, share), after=(token,)
+    )(
+        conv_one,
+        grad_scaled_two,
+        demod_one,
+        valid_rows,
+        noise_planes_one,
+        add_one,
+        styles,
+    )
+    token = reduce_two.fold(token, 1)
+    (grad_features_in, style_sums), token = call(
+        input_one_grad,
+        (shape(images, PLANE, share), shape(images, share)),
+        smem=1,
+        after=(token,),
+        plain=(0,),
+        loose=(4,),
+    )(place, grad_conv_one, grad_conv_one_other, flat_one, features, styles)
+    token = reduce_two.fold(token, 2)
+    parts_one, token = call(
+        kernel_one_grad,
+        group_shapes(GROUPS_ONE, half, channels),
+        [pltpu.VMEM((images, PLANE, share), BF16), pltpu.VMEM((share, share), F32)],
+        smem=1,
+        after=(token,),
+        micros=STAGE,
+    )(place, scaled_one, grad_conv_one, grad_conv_one_other, flat_one, styles)
+    reduce_one = Reduction(place, GROUPS_ONE, parts_one)
+    token = reduce_two.across(token)
     (features_out, rgb_planes, rgb_grad, sums_two), token = call(
         outputs_two_kernel,
         (
@@ -1281,65 +1354,18 @@
         styles,
         rgb_rows_in,
     )
-    rgb_planes_other = swap(rgb_planes, "chan")
-    token = reduce_two.second(token, STAGE)
-    parts_one, token = call(
-        kernel_one_grad,
-        kernel_shapes(9, half, share) * 2,
-        [pltpu.VMEM((images, PLANE, share), BF16), pltpu.VMEM((images, share), F32)],
-        smem=1,
-        after=(token,),
-    )(
-        place,
-        scaled_one,
-        grad_conv_one,
-        grad_conv_one_other,
-        flat_one,
-        styles,
-        square_one,
-        square_one_other,
-    )
-    reduce_one = Reduction(place, parts_one)
-    (rgb_out, grad_rgb_in, rgb_sums), token = call(
-        rgb_kernel,
-        (shape(*grad_rgb.shape), shape(*rgb_in.shape), shape(8, 128)),
-        [pltpu.VMEM((3 * images, RES, 128), F32)],
-        after=(token,),
-        plain=(0, 1),
-        loose=(1, 4, 5),
-    )(valid_rows, rgb_bias.reshape(1, -1), rgb_planes, rgb_planes_other, rgb_in, grad_rgb)
-    token = reduce_two.near(token, STAGE)
-    sums_one, token = call(
-        outputs_one_kernel, shape(images, 8, share), after=(token,)
-    )(
-        conv_one,
-        grad_scaled_two,
-        demod_one,
-        valid_rows,
-        noise_planes_one,
-        add_one,
-        styles,
-    )
-    (grad_features_in, style_sums), token = call(
-        input_one_grad,
-        (shape(images, PLANE, share), shape(images, share)),
-        smem=1,
-        after=(token,),
-        plain=(0,),
-        loose=(4,),
-    )(place, grad_conv_one, grad_conv_one_other, flat_one, features, styles)
-    (style_grads, crossing), token = call(
+    (pack, crossing), token = call(
         style_grads_kernel,
-        (shape(3 * images, share), shape(-(-(2 * images + 1) // 8) * 8, share)),
+        (shape(16, share), shape(8 + 32 * images, share)),
         smem=1,
         after=(token,),
         loose=(11, 12, 13),
     )(
         place,
-        square_one,
-        square_one_other,
-        square_two,
-        square_two_other,
+        grad_conv_one,
+        grad_conv_one_other,
+        grad_conv_two,
+        grad_conv_two_other,
         squares_one,
         squares_two,
         styles,
@@ -1349,58 +1375,67 @@
         affine_one,
         affine_two,
         affine_three,
-    )
-    crossing_other = swap(crossing, "chan")
-    token = reduce_two.across(token)
-    token = reduce_one.second(token)
-    (grad_latent, pack), token = call(
-        pack_kernel,
-        (shape(images, channels), shape(-(-(5 * images + 6) // 8) * 8, share)),
+        latent,
+        rgb_grad,
+        rgb_planes,
+    )
+    packs = [pack, swap(pack, "far")] if alone else []
+    token = reduce_one.fold(token, 1, micros=0)
+    token = reduce_two.total(token, *packs)
+    token = reduce_one.fold(token, 2)
+    token = reduce_two.join(token, 2)
+    token = reduce_one.across(token)
+    relayed, token = call(relay_kernel, shape(8 + 32 * images, share), after=(token,))(crossing)
+    crossing_other = swap(relayed, "chan")
+    token = reduce_two.join(token, 1)
+    (rgb_out, grad_rgb_in, grad_latent, scalars), token = call(
+        rgb_kernel,
+        (
+            shape(*grad_rgb.shape),
+            shape(*rgb_in.shape),
+            shape(images, channels),
+            shape(16, share),
+        ),
+        [pltpu.VMEM((3 * images, RES, 128), F32)],
         after=(token,),
-        plain=(0,),
-    )(
-        valid_rows,
-        crossing,
-        crossing_other,
-        style_grads,
-        latent,
-        sums_one,
-        sums_two,
-        rgb_grad,
-        rgb_sums,
-    )
-    devices = lax.axis_size(DP)
-    alone = lax.axis_size("block") == 1
-    packs = [pack, swap(pack, "far")] if alone else []
-    token = reduce_two.total(token, *packs, micros=STAGE)
-    token = reduce_one.near(token, STAGE)
-    token = reduce_two.join_near(token, STAGE)
-    token = reduce_one.across(token, STAGE)
-    token = reduce_two.join_pair(token, STAGE)
-    token = reduce_one.total(token, micros=STAGE)
+        plain=(0, 1, 2),
+        loose=(1, 4, 5),
+    )(valid_rows, rgb_bias.reshape(1, -1), crossing, crossing_other, rgb_in, grad_rgb)
+    rows = [scalars, swap(scalars, "far")] if alone else []
     sum_two, token = reduce_two.finish_own(token)
-    token = reduce_one.join_near(token)
+    token = reduce_one.total(token, *rows)
     sum_two, token = reduce_two.finish(token, sum_two)
+    token = reduce_one.join(token, 2)
     if alone:
-        packs = [reduce_two.own[0], reduce_two.got[0], reduce_two.own[1], reduce_two.got[1]]
+        packs = [reduce_two.own[0], reduce_two.got[0]]
     else:
         packs = [gather_packs(pack)]
-    token = reduce_one.join_pair(token, STAGE)
-    sum_one, token = reduce_one.finish_own(token)
     spread_out, token = call(
-        functools.partial(spread_kernel, images=images),
-        (shape(channels, share),) * 3
-        + (shape(1, share),) * 5
-        + (shape(3, share), shape(2), shape(3), shape(3)),
-        [pltpu.VMEM((devices,) + pack.shape, F32), pltpu.VMEM((2, devices) + pack.shape, F32)],
+        functools.partial(spread_kernel, images=images, groups=GROUPS_TWO),
+        (shape(channels, share),) * 3 + (shape(1, share),) * 5 + (shape(3, share),),
+        [pltpu.VMEM((devices, 16, share), F32)],
         smem=1,
         after=(token,),
-        scalars=(9, 10, 11),
         plain=tuple(range(9)),
     )(place, *packs)
+    token = reduce_one.join(token, 1)
+    sum_one, token = reduce_one.finish_own(token)
     affine_grads, affine_biases, points = spread_out[0:3], spread_out[3:6], spread_out[6:8]
-    rgb_total, gains, rms_values, rgb_bias_grad = spread_out[8:]
-    sum_one, token = reduce_one.finish(token, sum_one)
+    rgb_total = spread_out[8]
+    if alone:
+        found, token = reduce_one.finish_scalars(token, sum_one, devices)
+        sum_one, gains, rms_values, rgb_bias_grad = found
+    else:
+        rows = [gather_packs(scalars)]
+        (gains, rms_values, rgb_bias_grad), token = call(
+            functools.partial(scalars_kernel, groups=GROUPS_ONE),
+            (shape(2), shape(3), shape(3)),
+            [pltpu.VMEM((devices, 16, share), F32)],
+            smem=1,
+            after=(token,),
+            scalars=(0, 1, 2),
+        )(place, *rows)
+        sum_one, token = reduce_one.finish(token, sum_one)
     affine_outs = []
     for grad, bias in zip(affine_grads, affine_biases):
         affine_outs += [grad, bias.reshape(-1)]

time: 159 us -> 149 us (0.937)
  waiting for transfers between devices: 57.5 us -> 31 us
  starting transfers between devices: 27.2 us -> 42.6 us
    ppermute x35 -> x49, waiting for transfers between devices: 57.5 us -> 31 us  [swap(): return lax.ppermute(values, axis_name, SWAP)]
    ppermute x35 -> x49, starting transfers between devices: 27.2 us -> 42.6 us  [swap(): return lax.ppermute(values, axis_name, SWAP)]
  transfers between devices with their start and end apart: 35 -> 49, of which waited for: 18 -> 19; matrix products, arithmetic and copies ran while one was open for 0% -> 0% of each run, Pallas kernels for 33% -> 35%
where the time goes in v1:
time: 149 us; the launch traced here: 148 us
  Pallas kernels  72.4 us (49%)
  starting transfers between devices  42.6 us (29%)
  waiting for transfers between devices  31 us (21%)
  between operations  1.93 us (1%)
    pallas_call x33, Pallas kernels, run(): pl.pallas_call(inner, out_shape=tuple((member if index in hbm + scalars +...  72.4 us
    ppermute x49, starting transfers between devices, swap(): return lax.ppermute(values, axis_name, SWAP)  42.6 us
    ppermute x49, waiting for transfers between devices, swap(): return lax.ppermute(values, axis_name, SWAP)  31 us
  transfers between devices with their start and end apart: 49, of which 19 were waited for; matrix products, arithmetic and copies ran while one was open for 0% of the time, Pallas kernels for 35%

profile of v1, /device:TPU:0, one launch (start us, length us, event | category | flops | bytes accessed | tf_op | source)
XLA Modules:
  0.0 148.2 jit_solution(10893910815162445015)
XLA Ops:
  0.8 2.7 %style_kernel.1 = (f32[3,2,256]{2,1,0:T(2,128)S(1)}, bf16[2,256,256]{2,1,0:T(8,128)(2,1)S(1)}, bf16[9,256,256]{2,1,0:T(8,128)(2,1)S(1)}, f32[8,128]{1,0:T(8,128)S(1)}) custom-call(s32[5]{0:T(128)S(1)} %stack.23.refs_0_, bf16[9,256,512]{2,1,0:T(8,128)(2,1)} %bitcast.30, bf16[2,512]{1,0:T(2,128)(2,1)} %refs_14_.1, bf16[512,256]{1,0:T(8,128)(2,1)} %refs_11_.1, ...), custom_call_target="tpu_custom_call" | custom-call | flops 1024 | bytes 1024 | tf_op jit(solution)/shard_map/style_kernel/pallas_call | solution.py:951
  4.1 2.0 %squares_kernel.2 = (f32[256,512]{1,0:T(8,128)S(1)}, f32[2,256]{1,0:T(2,128)S(1)}, f32[2,256]{1,0:T(2,128)S(1)}, bf16[16,256]{1,0:T(8,128)(2,1)S(1)}, bf16[2,16,256]{2,1,0:T(8,128)(2,1)}, /*index=5*/f32[8,128]{1,0:T(8,128)S(1)}) custom-call(s32[5]{0:T(128)S(1)} %stack.23.refs_0_, ...), custom_call_target="tpu_custom_call" | custom-call | flops 1024 | bytes 1024 | tf_op jit(solution)/shard_map/squares_kernel/pallas_call | solution.py:951
  7.2 2.7 %planes_kernel.1 = (bf16[2,4,16,256]{3,2,1,0:T(8,128)(2,1)S(1)}, bf16[2,4,16,256]{3,2,1,0:T(8,128)(2,1)S(1)}, bf16[2,4,16,256]{3,2,1,0:T(8,128)(2,1)S(1)}, bf16[9,256,256]{2,1,0:T(8,128)(2,1)S(1)}, f32[8,128]{1,0:T(8,128)S(1)}) custom-call(s32[5]{0:T(128)S(1)} %stack.23.refs_0_, f32[2,256]{1,0:T(2,128)S(1)} %broadcast_in_dim.2.refs_1_.refs_7_.refs_3_.refs_2_.refs_0_, ...), custom_call_target="tpu_custom_call" | custom-call | flops 1024 | bytes 1024 | tf_op jit(solution)/shard_map/planes_kernel/pallas_call | solution.py:951
  10.1 2.7 %conv_one_kernel.1 = (f32[2,4,256,256]{3,2,1,0:T(8,128)S(1)}, bf16[2,4,256,256]{3,2,1,0:T(8,128)(2,1)S(1)}, f32[2,256]{1,0:T(2,128)S(1)}, f32[8,128]{1,0:T(8,128)S(1)}) custom-call(s32[5]{0:T(128)S(1)} %stack.23.refs_0_, bf16[2,256,256]{2,1,0:T(8,128)(2,1)S(1)} %get-tuple-element.162.refs_1_, bf16[2,256,256]{2,1,0:T(8,128)(2,1)S(1)} %collective-permute-done.refs_2_, ...), custom_call_target="tpu_custom_call" | custom-call | flops 66000003072 | bytes 1024 | tf_op jit(solution)/shard_map/conv_one_kernel/pallas_call | solution.py:951
  13.4 1.5 %squares_kernel.3 = (f32[256,512]{1,0:T(8,128)S(1)}, f32[2,256]{1,0:T(2,128)S(1)}, f32[2,256]{1,0:T(2,128)S(1)}, bf16[16,256]{1,0:T(8,128)(2,1)S(1)}, bf16[2,16,...) custom-call(s32[5]{0:T(128)S(1)} %stack.23.refs_0_, ...), custom_call_target="tpu_custom_call" | custom-call | flops 1024 | bytes 1024 | tf_op jit(solution)/shard_map/squares_kernel/pallas_call | solution.py:951
  15.1 1.0 collective-permute-done.5.refs_6_
  16.1 7.0 %conv_two_kernel.1 = (f32[2,4,256,256]{3,2,1,0:T(8,128)S(1)}, bf16[2064,256]{1,0:T(8,128)(2,1)S(1)}, f32[2,256]{1,0:T(2,128)S(1)}, f32[8,128]{1,0:T(8,128)S(1)}) custom-call(s32[5]{0:T(128)S(1)} %stack.23.refs_0_, bf16[2,4,256,256]{3,2,1,0:T(8,128)(2,1)S(1)} %get-tuple-element.172.refs_1_.refs_0_, ...), custom_call_target="tpu_custom_call" | custom-call | flops 1024 | bytes 1024 | tf_op jit(solution)/shard_map/conv_two_kernel/pallas_call | solution.py:951
  23.7 2.2 %collective-permute-done.6.refs_4_.refs_2_ = bf16[2064,256]{1,0:T(8,128)(2,1)S(1)} collective-permute-done((bf16[2064,256]{1,0:T(8,128)(2,1)S(1)}, bf16[2064,256]{1,0:T(8,128)(2,1)S(1)}, u32[]{:S(2)}, u32[]{:S(2)}) %collective-permute-start.6) | collective-permute-done | bytes 1056800 | tf_op jit(solution)/shard_map/ppermute | solution.py:992
  25.9 6.4 %kernel_two_grad.1 = (bf16[3,128,512]{2,1,0:T(8,128)(2,1)S(1)}, f32[3,128,512]{2,1,0:T(8,128)S(1)}, bf16[3,128,512]{2,1,0:T(8,128)(2,1)S(1)}, f32[3,128,512]{2,1...) custom-call(s32[5]{0:T(128)S(1)} %stack.23.refs_0_, ...), custom_call_target="tpu_custom_call" | custom-call | flops 1024 | bytes 1024 | tf_op jit(solution)/shard_map/kernel_two_grad/pallas_call | solution.py:951
  32.3 2.7 %collective-permute-start.7 = (bf16[3,128,512]{2,1,0:T(8,128)(2,1)S(1)}, bf16[3,128,512]{2,1,0:T(8,128)(2,1)S(1)}, u32[]{:S(2)}, u32[]{:S(2)}) collective-permute-start(bf16[3,128,512]{2,1,0:T(8,128)(2,1)S(1)} %get-tuple-element.189), channel_id=1, source_target_pairs={{0,2},{2,0},{1,3},{3,1},{4,6},{6,4},{5,7},{7,5},{8,10},{10,8},{9,1... | collective-permute-start | bytes 1179656 | tf_op jit(solution)/shard_map/ppermute | solution.py:992
  35.0 1.6 %collective-permute-start.8 = (bf16[3,128,512]{2,1,0:T(8,128)(2,1)S(1)}, bf16[3,128,512]{2,1,0:T(8,128)(2,1)S(1)}, u32[]{:S(2)}, u32[]{:S(2)}) collective-permute-start(bf16[3,128,512]{2,1,0:T(8,128)(2,1)S(1)} %get-tuple-element.191), channel_id=1, source_target_pairs={{0,4},{4,0},{1,5},{5,1},{2,6},{6,2},{3,7},{7,3},{8,12},{12,8},{9,1... | collective-permute-start | bytes 1179656 | tf_op jit(solution)/shard_map/ppermute | solution.py:992
  36.6 1.5 %collective-permute-start.9 = (bf16[3,128,512]{2,1,0:T(8,128)(2,1)S(1)}, bf16[3,128,512]{2,1,0:T(8,128)(2,1)S(1)}, u32[]{:S(2)}, u32[]{:S(2)}) collective-permute-start(bf16[3,128,512]{2,1,0:T(8,128)(2,1)S(1)} %get-tuple-element.193), channel_id=1, source_target_pairs={{0,8},{8,0},{1,9},{9,1},{2,10},{10,2},{3,11},{11,3},{4,12},{12,4},... | collective-permute-start | bytes 1179656 | tf_op jit(solution)/shard_map/ppermute | solution.py:992
  38.1 6.4 %input_two_grad.1 = (f32[2,4,256,256]{3,2,1,0:T(8,128)S(1)}, bf16[2064,256]{1,0:T(8,128)(2,1)S(1)}, f32[8,128]{1,0:T(8,128)S(1)}) custom-call(s32[5]{0:T(128)S(1)} %stack.23.refs_0_, bf16[2064,256]{1,0:T(8,128)(2,1)S(1)} %get-tuple-element.186.refs_3_.refs_1_, bf16[2064,256]{1,0:T(8,128)(2,1)S(1)} %collective-permute-done.6.refs_4_.refs_2_, ...), custom_call_target="tpu_custom_call" | custom-call | flops 1024 | bytes 1024 | tf_op jit(solution)/shard_map/input_two_grad/pallas_call | solution.py:951
  44.7 2.3 %outputs_one_kernel.1 = (f32[2,8,256]{2,1,0:T(8,128)S(1)}, f32[8,128]{1,0:T(8,128)S(1)}) custom-call(f32[2,4,256,256]{3,2,1,0:T(8,128)S(1)} %get-tuple-element.194.refs_4_.refs_0_, f32[2,4,256,256]{3,2,1,0:T(8,128)S(1)} %get-tuple-element.197.refs_1_, f32[2,256]{1,0:T(2,128)S(1)} %get-tuple-element.195.refs_5_.refs_2_, ...), custom_call_target="tpu_custom_call" | custom-call | flops 1024 | bytes 1024 | tf_op jit(solution)/shard_map/outputs_one_kernel/pallas_call | solution.py:951
  47.4 1.0 fold_kernel.4
  48.9 1.6 %collective-permute-start.11 = (bf16[3,64,512]{2,1,0:T(8,128)(2,1)S(1)}, bf16[3,64,512]{2,1,0:T(8,128)(2,1)S(1)}, u32[]{:S(2)}, u32[]{:S(2)}) collective-permute-start(bf16[3,64,512]{2,1,0:T(8,128)(2,1)S(1)} %get-tuple-element.203), channel_id=1, source_target_pairs={{0,8},{8,0},{1,9},{9,1},{2,10},{10,2},{3,11},{11,3},{4,12},{12,4},... | collective-permute-start | bytes 589832 | tf_op jit(solution)/shard_map/ppermute | solution.py:992
  51.0 3.2 %input_one_grad.1 = (f32[2,256,256]{2,1,0:T(8,128)}, f32[2,256]{1,0:T(2,128)S(1)}, f32[8,128]{1,0:T(8,128)S(1)}) custom-call(s32[5]{0:T(128)S(1)} %stack.23.refs_0_, bf16[2064,256]{1,0:T(8,128)(2,1)S(1)} %get-tuple-element.206.refs_1_.refs_2_, bf16[2064,256]{1,0:T(8,128)(2,1)S(1)} %collective-permute-done.13.refs_2_.refs_3_, ...), custom_call_target="tpu_custom_call" | custom-call | flops 1024 | bytes 1024 | tf_op jit(solution)/shard_map/input_one_grad/pallas_call | solution.py:951
  54.2 1.2 collective-permute-done.10.refs_2_
  56.2 0.7 fold_kernel.5
  56.9 1.3 collective-permute-start.14
  58.7 1.5 %collective-permute-start.16 = (bf16[3,32,512]{2,1,0:T(8,128)(2,1)S(1)}, bf16[3,32,512]{2,1,0:T(8,128)(2,1)S(1)}, u32[]{:S(2)}, u32[]{:S(2)}) collective-permute-start(bf16[3,32,512]{2,1,0:T(8,128)(2,1)S(1)} %get-tuple-element.214), channel_id=1, source_target_pairs={{0,4},{4,0},{1,5},{5,1},{2,6},{6,2},{3,7},{7,3},{8,12},{12,8},{9,1... | collective-permute-start | bytes 294920 | tf_op jit(solution)/shard_map/ppermute | solution.py:992
  60.2 2.8 %kernel_one_grad.1 = (bf16[3,128,512]{2,1,0:T(8,128)(2,1)S(1)}, f32[3,128,512]{2,1,0:T(8,128)S(1)}, bf16[3,128,512]{2,1,0:T(8,128)(2,1)S(1)}, f32[3,128,512]{2,1...) custom-call(s32[5]{0:T(128)S(1)} %stack.23.refs_0_, ...), custom_call_target="tpu_custom_call" | custom-call | flops 66000003072 | bytes 1024 | tf_op jit(solution)/shard_map/kernel_one_grad/pallas_call | solution.py:951
  63.1 1.5 %collective-permute-start.17 = (bf16[3,128,512]{2,1,0:T(8,128)(2,1)S(1)}, bf16[3,128,512]{2,1,0:T(8,128)(2,1)S(1)}, u32[]{:S(2)}, u32[]{:S(2)}) collective-permute-start(bf16[3,128,512]{2,1,0:T(8,128)(2,1)S(1)} %get-tuple-element.229), channel_id=1, source_target_pairs={{0,2},{2,0},{1,3},{3,1},{4,6},{6,4},{5,7},{7,5},{8,10},{10,8},{9,1... | collective-permute-start | bytes 1179656 | tf_op jit(solution)/shard_map/ppermute | solution.py:992
  65.1 0.8 collective-permute-start.19
  66.6 2.7 %collective-permute-start.23 = (bf16[9,32,512]{2,1,0:T(8,128)(2,1)S(1)}, bf16[9,32,512]{2,1,0:T(8,128)(2,1)S(1)}, u32[]{:S(2)}, u32[]{:S(2)}) collective-permute-start(bf16[9,32,512]{2,1,0:T(8,128)(2,1)S(1)} %get-tuple-element.241.refs_1_), channel_id=1, source_target_pairs={{0,16},{16,0},{1,17},{17,1},{2,18},{18,2},{3,19},{19,3},{4,20},{20... | collective-permute-start | bytes 884744 | tf_op jit(solution)/shard_map/ppermute | solution.py:992
  69.3 5.7 %outputs_two_kernel.1 = (bf16[2,32,32,256]{3,2,1,0:T(8,128)(2,1)}, f32[2,4,8,256]{3,2,1,0:T(8,128)S(1)}, f32[16,256]{1,0:T(8,128)S(1)}, f32[2,8,256]{2,1,0:T(8,128)S(1)}, f32[8,128]{1,0:T(8,128)S(1)}) custom-call(f32[2,4,256,256]{3,2,1,0:T(8,128)S(1)} %get-tuple-element.182.refs_0_, f32[2,256]{1,0:T(2,128)S(1)} %get-tuple-element.183.refs_1_, ...), custom_call_target="tpu_custom_call" | custom-call | flops 1024 | bytes 1024 | tf_op jit(solution)/shard_map/outputs_two_kernel/pallas_call | solution.py:951
  75.0 3.3 %style_grads_kernel.1 = (f32[16,256]{1,0:T(8,128)S(1)}, f32[72,256]{1,0:T(8,128)S(1)}, f32[8,128]{1,0:T(8,128)S(1)}) custom-call(s32[5]{0:T(128)S(1)} %stack.23.refs_0_, bf16[2064,256]{1,0:T(8,128)(2,1)S(1)} %get-tuple-element.206.refs_1_.refs_2_, bf16[2064,256]{1,0:T(8,128)(2,1)S(1)} %collective-permute-done.13.refs_2_.refs_3_, ...), custom_call_target="tpu_custom_call" | custom-call | flops 1024 | bytes 1024 | tf_op jit(solution)/shard_map/style_grads_kernel/pallas_call | solution.py:951
  78.6 1.3 collective-permute-done.19.refs_6_
  79.9 0.8 fold_kernel.6
  80.7 1.6 %collective-permute-start.20 = (bf16[3,64,512]{2,1,0:T(8,128)(2,1)S(1)}, bf16[3,64,512]{2,1,0:T(8,128)(2,1)S(1)}, u32[]{:S(2)}, u32[]{:S(2)}) collective-permute-start(bf16[3,64,512]{2,1,0:T(8,128)(2,1)S(1)} %get-tuple-element.236), channel_id=1, source_target_pairs={{0,4},{4,0},{1,5},{5,1},{2,6},{6,2},{3,7},{7,3},{8,12},{12,8},{9,1... | collective-permute-start | bytes 589832 | tf_op jit(solution)/shard_map/ppermute | solution.py:992
  83.1 0.7 total_kernel.2
  83.7 1.4 collective-permute-start.29
  85.1 0.8 collective-permute-start.30
  85.9 1.6 %collective-permute-done.20.refs_2_ = bf16[3,64,512]{2,1,0:T(8,128)(2,1)S(1)} collective-permute-done((bf16[3,64,512]{2,1,0:T(8,128)(2,1)S(1)}, bf16[3,64,512]{2,1,0:T(8,128)(2,1)S(1)}, u32[]{:S(2)}, u32[]{:S(2)}) %collective-permute-start.20) | collective-permute-done | bytes 196640 | tf_op jit(solution)/shard_map/ppermute | solution.py:992
  87.6 2.5 %collective-permute-done.21.refs_4_ = bf16[3,64,512]{2,1,0:T(8,128)(2,1)S(1)} collective-permute-done((bf16[3,64,512]{2,1,0:T(8,128)(2,1)S(1)}, bf16[3,64,512]{2,1,0:T(8,128)(2,1)S(1)}, u32[]{:S(2)}, u32[]{:S(2)}) %collective-permute-start.21) | collective-permute-done | bytes 196640 | tf_op jit(solution)/shard_map/ppermute | solution.py:992
  90.1 0.7 fold_kernel.7
  92.1 1.3 collective-permute-done.28.refs_2_
  94.2 1.5 collective-permute-start.34
  95.7 2.0 %collective-permute-start.32 = (bf16[4,64,512]{2,1,0:T(8,128)(2,1)S(1)}, bf16[4,64,512]{2,1,0:T(8,128)(2,1)S(1)}, u32[]{:S(2)}, u32[]{:S(2)}) collective-permute-start(bf16[4,64,512]{2,1,0:T(8,128)(2,1)S(1)} %get-tuple-element.258.refs_1_), channel_id=1, source_target_pairs={{0,4},{4,0},{1,5},{5,1},{2,6},{6,2},{3,7},{7,3},{8,12},{12,8},{9,1... | collective-permute-start | bytes 786440 | tf_op jit(solution)/shard_map/ppermute | solution.py:992
  98.4 1.6 %collective-permute-start.36 = (bf16[9,32,512]{2,1,0:T(8,128)(2,1)S(1)}, bf16[9,32,512]{2,1,0:T(8,128)(2,1)S(1)}, u32[]{:S(2)}, u32[]{:S(2)}) collective-permute-start(bf16[9,32,512]{2,1,0:T(8,128)(2,1)S(1)} %get-tuple-element.268.refs_1_), channel_id=1, source_target_pairs={{0,16},{16,0},{1,17},{17,1},{2,18},{18,2},{3,19},{19,3},{4,20},{20... | collective-permute-start | bytes 884744 | tf_op jit(solution)/shard_map/ppermute | solution.py:992
  100.0 2.1 %collective-permute-done.32.refs_2_ = bf16[4,64,512]{2,1,0:T(8,128)(2,1)S(1)} collective-permute-done((bf16[4,64,512]{2,1,0:T(8,128)(2,1)S(1)}, bf16[4,64,512]{2,1,0:T(8,128)(2,1)S(1)}, u32[]{:S(2)}, u32[]{:S(2)}) %collective-permute-start.32) | collective-permute-done | bytes 262176 | tf_op jit(solution)/shard_map/ppermute | solution.py:992
  102.0 0.7 join_kernel.5
  102.7 3.1 %rgb_kernel.1 = (f32[2,3,32,32]{3,2,1,0:T(8,128)}, f32[2,3,16,16]{3,2,1,0:T(8,128)}, f32[2,512]{1,0:T(2,128)}, f32[16,256]{1,0:T(8,128)S(1)}, f32[8,128]{1,0:T(8,128)S(1)}) custom-call(f32[2,256]{1,0:T(2,128)S(1)} %broadcast_in_dim.2.refs_1_.refs_7_.refs_3_.refs_2_.refs_0_, f32[1,3]{1,0:T(1,128)} %bitcast.44, ...), custom_call_target="tpu_custom_call" | custom-call | flops 1024 | bytes 1024 | tf_op jit(solution)/shard_map/rgb_kernel/pallas_call | solution.py:951
  105.9 1.7 %collective-permute-start.37 = (f32[16,256]{1,0:T(8,128)S(1)}, f32[16,256]{1,0:T(8,128)S(1)}, u32[]{:S(2)}, u32[]{:S(2)}) collective-permute-start(f32[16,256]{1,0:T(8,128)S(1)} %get-tuple-element.269.refs_3_), channel_id=1, source_target_pairs={{0,16},{16,0},{1,17},{17,1},{2,18},{18,2},{3,19},{19,3},{4,20},{20... | collective-permute-start | bytes 49160 | tf_op jit(solution)/shard_map/ppermute | solution.py:992
  107.6 1.8 %collective-permute-start.41 = (bf16[3,128,512]{2,1,0:T(8,128)(2,1)S(1)}, bf16[3,128,512]{2,1,0:T(8,128)(2,1)S(1)}, u32[]{:S(2)}, u32[]{:S(2)}) collective-permute-start(bf16[3,128,512]{2,1,0:T(8,128)(2,1)S(1)} %get-tuple-element.270.refs_2_), channel_id=1, source_target_pairs={{0,4},{4,0},{1,5},{5,1},{2,6},{6,2},{3,7},{7,3},{8,12},{12,8},{9,1... | collective-permute-start | bytes 1179656 | tf_op jit(solution)/shard_map/ppermute | solution.py:992
  109.4 1.1 collective-permute-start.42
  110.9 2.0 %finish_kernel.3 = (f32[9,256,512]{2,1,0:T(8,128)}, f32[8,128]{1,0:T(8,128)S(1)}) custom-call(s32[5]{0:T(128)S(1)} %stack.23.refs_0_, bf16[4,128,512]{2,1,0:T(8,128)(2,1)S(1)} %get-tuple-element.267.refs_1_, bf16[3,128,512]{2,1,0:T(8,128)(2,1)S(1)} %get-tuple-element.270.refs_2_, bf16[3,128,512]{2,1,0:T(8,128)(2,1)S(1)} %get-tuple-element.271.refs_3_, ...), custom_call_target="tpu_custom_call" | custom-call | flops 1024 | bytes 1024 | tf_op jit(solution)/shard_map/finish_kernel/pallas_call | solution.py:951
  113.0 2.7 %collective-permute-done.37.refs_4_ = f32[16,256]{1,0:T(8,128)S(1)} collective-permute-done((f32[16,256]{1,0:T(8,128)S(1)}, f32[16,256]{1,0:T(8,128)S(1)}, u32[]{:S(2)}, u32[]{:S(2)}) %collective-permute-start.37) | collective-permute-done | bytes 16416 | tf_op jit(solution)/shard_map/ppermute | solution.py:992
  115.7 0.7 total_kernel.3
  116.5 0.8 collective-permute-start.39
  117.2 0.7 collective-permute-start.40
  118.0 6.2 %collective-permute-done.42.refs_3_ = bf16[3,128,512]{2,1,0:T(8,128)(2,1)S(1)} collective-permute-done((bf16[3,128,512]{2,1,0:T(8,128)(2,1)S(1)}, bf16[3,128,512]{2,1,0:T(8,128)(2,1)S(1)}, u32[]{:S(2)}, u32[]{:S(2)}) %collective-permute-start.42) | collective-permute-done | bytes 393248 | tf_op jit(solution)/shard_map/ppermute | solution.py:992
  124.1 2.0 %finish_kernel.4 = (f32[9,256,512]{2,1,0:T(8,128)}, f32[8,128]{1,0:T(8,128)S(1)}) custom-call(s32[5]{0:T(128)S(1)} %stack.23.refs_0_, bf16[4,128,512]{2,1,0:T(8,128)(2,1)S(1)} %collective-permute-done.35.refs_1_.refs_2_, bf16[3,128,512]{2,1,0:T(8,128)(2,1)S(1)} %collective-permute-done.41.refs_2_, ...), custom_call_target="tpu_custom_call", output_to_operand_aliasing={{0}: (4, {})} | custom-call | flops 1024 | bytes 1024 | tf_op jit(solution)/shard_map/finish_kernel/pallas_call | solution.py:951
  127.1 1.0 collective-permute-start.45
  128.1 3.1 %spread_kernel.1 = (f32[512,256]{1,0:T(8,128)}, f32[512,256]{1,0:T(8,128)}, f32[512,256]{1,0:T(8,128)}, f32[1,256]{1,0:T(1,128)}, f32[1,256]{1,0:T(1,128)}, /*in...) custom-call(s32[5]{0:T(128)S(1)} %stack.23.refs_0_, ...), custom_call_target="tpu_custom_call" | custom-call | flops 1024 | bytes 1024 | tf_op jit(solution)/shard_map/spread_kernel/pallas_call | solution.py:951
  131.2 1.6 %collective-permute-done.44.refs_4_ = bf16[3,64,512]{2,1,0:T(8,128)(2,1)S(1)} collective-permute-done((bf16[3,64,512]{2,1,0:T(8,128)(2,1)S(1)}, bf16[3,64,512]{2,1,0:T(8,128)(2,1)S(1)}, u32[]{:S(2)}, u32[]{:S(2)}) %collective-permute-start.44) | collective-permute-done | bytes 196640 | tf_op jit(solution)/shard_map/ppermute | solution.py:992
  133.3 0.7 join_kernel.7
  134.5 1.1 collective-permute-start.47
  135.7 2.1 %collective-permute-start.48 = (bf16[3,128,512]{2,1,0:T(8,128)(2,1)S(1)}, bf16[3,128,512]{2,1,0:T(8,128)(2,1)S(1)}, u32[]{:S(2)}, u32[]{:S(2)}) collective-permute-start(bf16[3,128,512]{2,1,0:T(8,128)(2,1)S(1)} %get-tuple-element.293.refs_3_), channel_id=1, source_target_pairs={{0,8},{8,0},{1,9},{9,1},{2,10},{10,2},{3,11},{11,3},{4,12},{12,4},... | collective-permute-start | bytes 1179656 | tf_op jit(solution)/shard_map/ppermute | solution.py:992
  137.7 2.0 %finish_kernel.5 = (f32[9,256,512]{2,1,0:T(8,128)}, f32[8,128]{1,0:T(8,128)S(1)}) custom-call(s32[5]{0:T(128)S(1)} %stack.23.refs_0_, bf16[4,128,512]{2,1,0:T(8,128)(2,1)S(1)} %get-tuple-element.291.refs_1_.refs_5_, bf16[3,128,512]{2,1,0:T(8,128)(2,1)S(1)} %get-tuple-element.292.refs_2_, bf16[3,128,512]{2,1,0:T(8,128)(2,1)S(1)} %get-tuple-element.293.refs_3_, ...), custom_call_target="tpu_custom_call" | custom-call | flops 1024 | bytes 1024 | tf_op jit(solution)/shard_map/finish_kernel/pallas_call | solution.py:951
  139.8 3.1 %collective-permute-done.47.refs_2_ = bf16[3,128,512]{2,1,0:T(8,128)(2,1)S(1)} collective-permute-done((bf16[3,128,512]{2,1,0:T(8,128)(2,1)S(1)}, bf16[3,128,512]{2,1,0:T(8,128)(2,1)S(1)}, u32[]{:S(2)}, u32[]{:S(2)}) %collective-permute-start.47) | collective-permute-done | bytes 393248 | tf_op jit(solution)/shard_map/ppermute | solution.py:992
  142.8 1.5 collective-permute-done.48.refs_3_
  144.3 1.1 collective-permute-done.46.refs_1_
  145.4 2.6 %finish_scalars_kernel.1 = (f32[9,256,512]{2,1,0:T(8,128)}, f32[2]{0:T(128)}, f32[3]{0:T(128)}, f32[3]{0:T(128)}, f32[8,128]{1,0:T(8,128)}) custom-call(s32[5]{0:T(128)S(1)} %stack.23.refs_0_, bf16[4,128,512]{2,1,0:T(8,128)(2,1)S(1)} %collective-permute-done.46.refs_1_, ...), custom_call_target="tpu_custom_call", output_to_operand_aliasing={{0}: (4, {})} | custom-call | flops 1024 | bytes 1024 | tf_op jit(solution)/shard_map/finish_scalars_kernel/pallas_call | solution.py:951
  (93 shorter events, 13.1 us)
Async XLA Ops:
  0.7 3.4 %copy-start.1 = (bf16[3,3,256,512]{3,2,1,0:T(8,128)(2,1)S(1)}, bf16[3,3,256,512]{3,2,1,0:T(8,128)(2,1)}, u32[]{:S(2)}) copy-start(bf16[3,3,256,512]{3,2,1,0:T(8,128)(2,1)} %param.31) | copy-start | bytes 7077892
  3.5 6.6 %collective-permute-start.1 = (bf16[9,256,256]{2,1,0:T(8,128)(2,1)S(1)}, bf16[9,256,256]{2,1,0:T(8,128)(2,1)S(1)}, u32[]{:S(2)}, u32[]{:S(2)}) collective-permute-start(bf16[9,256,256]{2,1,0:T(8,128)(2,1)S(1)} %get-tuple-element.163), channel_id=1, source_target_pairs={{0,1},{1,0},{2,3},{3,2},{4,5},{5,4},{6,7},{7,6},{8,9},{9,8},{10,11... | collective-permute-start | bytes 3538952 | tf_op jit(solution)/shard_map/ppermute | solution.py:992
  4.0 6.1 %collective-permute-start = (bf16[2,256,256]{2,1,0:T(8,128)(2,1)S(1)}, bf16[2,256,256]{2,1,0:T(8,128)(2,1)S(1)}, u32[]{:S(2)}, u32[]{:S(2)}) collective-permute-start(bf16[2,256,256]{2,1,0:T(8,128)(2,1)S(1)} %get-tuple-element.162.refs_1_), channel_id=1, source_target_pairs={{0,1},{1,0},{2,3},{3,2},{4,5},{5,4},{6,7},{7,6},{8,9},{9,8},{10,11... | collective-permute-start | bytes 786440 | tf_op jit(solution)/shard_map/ppermute | solution.py:992
  6.1 4.0 %collective-permute-start.2 = (f32[2,256]{1,0:T(2,128)S(1)}, f32[2,256]{1,0:T(2,128)S(1)}, u32[]{:S(2)}, u32[]{:S(2)}) collective-permute-start(f32[2,256]{1,0:T(2,128)S(1)} %get-tuple-element.167), channel_id=1, source_target_pairs={{0,1},{1,0},{2,3},{3,2},{4,5},{5,4},{6,7},{7,6},{8,9},{9,8},{10,11... | collective-permute-start | bytes 6152 | tf_op jit(solution)/shard_map/ppermute | solution.py:992
  9.9 6.2 %copy-start.3 = (bf16[2,4,16,256]{3,2,1,0:T(8,128)(2,1)}, bf16[2,4,16,256]{3,2,1,0:T(8,128)(2,1)S(1)}, u32[]{:S(2)}) copy-start(bf16[2,4,16,256]{3,2,1,0:T(8,128)(2,1)S(1)} %get-tuple-element.177.refs_8_.refs_3_) | copy-start | bytes 196612
  9.9 6.2 %copy-start.5 = (bf16[2,4,16,256]{3,2,1,0:T(8,128)(2,1)}, bf16[2,4,16,256]{3,2,1,0:T(8,128)(2,1)S(1)}, u32[]{:S(2)}) copy-start(bf16[2,4,16,256]{3,2,1,0:T(8,128)(2,1)S(1)} %get-tuple-element.179.refs_10_.refs_5_) | copy-start | bytes 196612
  9.9 5.2 %collective-permute-start.4 = (bf16[9,256,256]{2,1,0:T(8,128)(2,1)S(1)}, bf16[9,256,256]{2,1,0:T(8,128)(2,1)S(1)}, u32[]{:S(2)}, u32[]{:S(2)}) collective-permute-start(bf16[9,256,256]{2,1,0:T(8,128)(2,1)S(1)} %get-tuple-element.173), channel_id=1, source_target_pairs={{0,1},{1,0},{2,3},{3,2},{4,5},{5,4},{6,7},{7,6},{8,9},{9,8},{10,11... | collective-permute-start | bytes 3538952 | tf_op jit(solution)/shard_map/ppermute | solution.py:992
  10.1 3.3 %copy-start = (bf16[3,3,256,512]{3,2,1,0:T(8,128)(2,1)S(1)}, bf16[3,3,256,512]{3,2,1,0:T(8,128)(2,1)}, u32[]{:S(2)}) copy-start(bf16[3,3,256,512]{3,2,1,0:T(8,128)(2,1)} %param.33) | copy-start | bytes 7077892
  12.9 3.3 %copy-start.2 = (bf16[2,32,32,256]{3,2,1,0:T(8,128)(2,1)S(1)}, bf16[2,32,32,256]{3,2,1,0:T(8,128)(2,1)}, u32[]{:S(2)}) copy-start(bf16[2,32,32,256]{3,2,1,0:T(8,128)(2,1)} %refs_6_.3) | copy-start | bytes 3145732
  12.9 3.2 %collective-permute-start.3 = (bf16[2,4,256,256]{3,2,1,0:T(8,128)(2,1)S(1)}, bf16[2,4,256,256]{3,2,1,0:T(8,128)(2,1)S(1)}, u32[]{:S(2)}, u32[]{:S(2)}) collective-permute-start(bf16[2,4,256,256]{3,2,1,0:T(8,128)(2,1)S(1)} %get-tuple-element.172.refs_1_.refs_0_), channel_id=1, source_target_pairs={{0,1},{1,0},{2,3},{3,2},{4,5},{5,4},{6,7},{7,6},{8,9},{9,8},{10,11... | collective-permute-start | bytes 3145736 | tf_op jit(solution)/shard_map/ppermute | solution.py:992
  14.9 8.3 %copy-start.7 = (bf16[16,256]{1,0:T(8,128)(2,1)}, bf16[16,256]{1,0:T(8,128)(2,1)S(1)}, u32[]{:S(2)}) copy-start(bf16[16,256]{1,0:T(8,128)(2,1)S(1)} %get-tuple-element.178.refs_9_.refs_4_) | copy-start | bytes 24580
  14.9 1.2 collective-permute-start.5
  23.2 2.7 %collective-permute-start.6 = (bf16[2064,256]{1,0:T(8,128)(2,1)S(1)}, bf16[2064,256]{1,0:T(8,128)(2,1)S(1)}, u32[]{:S(2)}, u32[]{:S(2)}) collective-permute-start(bf16[2064,256]{1,0:T(8,128)(2,1)S(1)} %get-tuple-element.186.refs_3_.refs_1_), channel_id=1, source_target_pairs={{0,1},{1,0},{2,3},{3,2},{4,5},{5,4},{6,7},{7,6},{8,9},{9,8},{10,11... | collective-permute-start | bytes 3170312 | tf_op jit(solution)/shard_map/ppermute | solution.py:992
  32.3 14.7 %collective-permute-start.7 = (bf16[3,128,512]{2,1,0:T(8,128)(2,1)S(1)}, bf16[3,128,512]{2,1,0:T(8,128)(2,1)S(1)}, u32[]{:S(2)}, u32[]{:S(2)}) collective-permute-start(bf16[3,128,512]{2,1,0:T(8,128)(2,1)S(1)} %get-tuple-element.189), channel_id=1, source_target_pairs={{0,2},{2,0},{1,3},{3,1},{4,6},{6,4},{5,7},{7,5},{8,10},{10,8},{9,1... | collective-permute-start | bytes 1179656 | tf_op jit(solution)/shard_map/ppermute | solution.py:992
  35.0 12.0 %collective-permute-start.8 = (bf16[3,128,512]{2,1,0:T(8,128)(2,1)S(1)}, bf16[3,128,512]{2,1,0:T(8,128)(2,1)S(1)}, u32[]{:S(2)}, u32[]{:S(2)}) collective-permute-start(bf16[3,128,512]{2,1,0:T(8,128)(2,1)S(1)} %get-tuple-element.191), channel_id=1, source_target_pairs={{0,4},{4,0},{1,5},{5,1},{2,6},{6,2},{3,7},{7,3},{8,12},{12,8},{9,1... | collective-permute-start | bytes 1179656 | tf_op jit(solution)/shard_map/ppermute | solution.py:992
  36.6 10.8 %collective-permute-start.9 = (bf16[3,128,512]{2,1,0:T(8,128)(2,1)S(1)}, bf16[3,128,512]{2,1,0:T(8,128)(2,1)S(1)}, u32[]{:S(2)}, u32[]{:S(2)}) collective-permute-start(bf16[3,128,512]{2,1,0:T(8,128)(2,1)S(1)} %get-tuple-element.193), channel_id=1, source_target_pairs={{0,8},{8,0},{1,9},{9,1},{2,10},{10,2},{3,11},{11,3},{4,12},{12,4},... | collective-permute-start | bytes 1179656 | tf_op jit(solution)/shard_map/ppermute | solution.py:992
  44.6 6.5 %collective-permute-start.13 = (bf16[2064,256]{1,0:T(8,128)(2,1)S(1)}, bf16[2064,256]{1,0:T(8,128)(2,1)S(1)}, u32[]{:S(2)}, u32[]{:S(2)}) collective-permute-start(bf16[2064,256]{1,0:T(8,128)(2,1)S(1)} %get-tuple-element.206.refs_1_.refs_2_), channel_id=1, source_target_pairs={{0,1},{1,0},{2,3},{3,2},{4,5},{5,4},{6,7},{7,6},{8,9},{9,8},{10,11... | collective-permute-start | bytes 3170312 | tf_op jit(solution)/shard_map/ppermute | solution.py:992
  48.4 7.0 %collective-permute-start.10 = (bf16[3,64,512]{2,1,0:T(8,128)(2,1)S(1)}, bf16[3,64,512]{2,1,0:T(8,128)(2,1)S(1)}, u32[]{:S(2)}, u32[]{:S(2)}) collective-permute-start(bf16[3,64,512]{2,1,0:T(8,128)(2,1)S(1)} %get-tuple-element.201), channel_id=1, source_target_pairs={{0,4},{4,0},{1,5},{5,1},{2,6},{6,2},{3,7},{7,3},{8,12},{12,8},{9,1... | collective-permute-start | bytes 589832 | tf_op jit(solution)/shard_map/ppermute | solution.py:992
  48.9 6.7 %collective-permute-start.11 = (bf16[3,64,512]{2,1,0:T(8,128)(2,1)S(1)}, bf16[3,64,512]{2,1,0:T(8,128)(2,1)S(1)}, u32[]{:S(2)}, u32[]{:S(2)}) collective-permute-start(bf16[3,64,512]{2,1,0:T(8,128)(2,1)S(1)} %get-tuple-element.203), channel_id=1, source_target_pairs={{0,8},{8,0},{1,9},{9,1},{2,10},{10,2},{3,11},{11,3},{4,12},{12,4},... | collective-permute-start | bytes 589832 | tf_op jit(solution)/shard_map/ppermute | solution.py:992
  50.5 5.7 %collective-permute-start.12 = (bf16[3,64,512]{2,1,0:T(8,128)(2,1)S(1)}, bf16[3,64,512]{2,1,0:T(8,128)(2,1)S(1)}, u32[]{:S(2)}, u32[]{:S(2)}) collective-permute-start(bf16[3,64,512]{2,1,0:T(8,128)(2,1)S(1)} %get-tuple-element.205), channel_id=1, source_target_pairs={{0,2},{2,0},{1,3},{3,1},{4,6},{6,4},{5,7},{7,5},{8,10},{10,8},{9,1... | collective-permute-start | bytes 589832 | tf_op jit(solution)/shard_map/ppermute | solution.py:992
  56.9 8.2 %collective-permute-start.14 = (bf16[3,32,512]{2,1,0:T(8,128)(2,1)S(1)}, bf16[3,32,512]{2,1,0:T(8,128)(2,1)S(1)}, u32[]{:S(2)}, u32[]{:S(2)}) collective-permute-start(bf16[3,32,512]{2,1,0:T(8,128)(2,1)S(1)} %get-tuple-element.210), channel_id=1, source_target_pairs={{0,8},{8,0},{1,9},{9,1},{2,10},{10,2},{3,11},{11,3},{4,12},{12,4},... | collective-permute-start | bytes 294920 | tf_op jit(solution)/shard_map/ppermute | solution.py:992
  58.1 7.8 %collective-permute-start.15 = (bf16[3,32,512]{2,1,0:T(8,128)(2,1)S(1)}, bf16[3,32,512]{2,1,0:T(8,128)(2,1)S(1)}, u32[]{:S(2)}, u32[]{:S(2)}) collective-permute-start(bf16[3,32,512]{2,1,0:T(8,128)(2,1)S(1)} %get-tuple-element.212), channel_id=1, source_target_pairs={{0,2},{2,0},{1,3},{3,1},{4,6},{6,4},{5,7},{7,5},{8,10},{10,8},{9,1... | collective-permute-start | bytes 294920 | tf_op jit(solution)/shard_map/ppermute | solution.py:992
  58.7 7.3 %collective-permute-start.16 = (bf16[3,32,512]{2,1,0:T(8,128)(2,1)S(1)}, bf16[3,32,512]{2,1,0:T(8,128)(2,1)S(1)}, u32[]{:S(2)}, u32[]{:S(2)}) collective-permute-start(bf16[3,32,512]{2,1,0:T(8,128)(2,1)S(1)} %get-tuple-element.214), channel_id=1, source_target_pairs={{0,4},{4,0},{1,5},{5,1},{2,6},{6,2},{3,7},{7,3},{8,12},{12,8},{9,1... | collective-permute-start | bytes 294920 | tf_op jit(solution)/shard_map/ppermute | solution.py:992
  63.1 15.6 %collective-permute-start.17 = (bf16[3,128,512]{2,1,0:T(8,128)(2,1)S(1)}, bf16[3,128,512]{2,1,0:T(8,128)(2,1)S(1)}, u32[]{:S(2)}, u32[]{:S(2)}) collective-permute-start(bf16[3,128,512]{2,1,0:T(8,128)(2,1)S(1)} %get-tuple-element.229), channel_id=1, source_target_pairs={{0,2},{2,0},{1,3},{3,1},{4,6},{6,4},{5,7},{7,5},{8,10},{10,8},{9,1... | collective-permute-start | bytes 1179656 | tf_op jit(solution)/shard_map/ppermute | solution.py:992
  64.6 14.0 %collective-permute-start.18 = (bf16[3,128,512]{2,1,0:T(8,128)(2,1)S(1)}, bf16[3,128,512]{2,1,0:T(8,128)(2,1)S(1)}, u32[]{:S(2)}, u32[]{:S(2)}) collective-permute-start(bf16[3,128,512]{2,1,0:T(8,128)(2,1)S(1)} %get-tuple-element.231), channel_id=1, source_target_pairs={{0,4},{4,0},{1,5},{5,1},{2,6},{6,2},{3,7},{7,3},{8,12},{12,8},{9,1... | collective-permute-start | bytes 1179656 | tf_op jit(solution)/shard_map/ppermute | solution.py:992
  65.1 14.8 %collective-permute-start.19 = (bf16[3,128,512]{2,1,0:T(8,128)(2,1)S(1)}, bf16[3,128,512]{2,1,0:T(8,128)(2,1)S(1)}, u32[]{:S(2)}, u32[]{:S(2)}) collective-permute-start(bf16[3,128,512]{2,1,0:T(8,128)(2,1)S(1)} %get-tuple-element.233), channel_id=1, source_target_pairs={{0,8},{8,0},{1,9},{9,1},{2,10},{10,2},{3,11},{11,3},{4,12},{12,4},... | collective-permute-start | bytes 1179656 | tf_op jit(solution)/shard_map/ppermute | solution.py:992
  65.9 3.4 %copy-start.10 = (bf16[3,256]{1,0:T(4,128)(2,1)S(1)}, bf16[3,256]{1,0:T(4,128)(2,1)}, u32[]{:S(2)}) copy-start(bf16[3,256]{1,0:T(4,128)(2,1)} %refs_4_.6) | copy-start | bytes 4612
  65.9 3.4 %copy-start.4 = (bf16[2,4,16,256]{3,2,1,0:T(8,128)(2,1)S(1)}, bf16[2,4,16,256]{3,2,1,0:T(8,128)(2,1)}, u32[]{:S(2)}) copy-start(bf16[2,4,16,256]{3,2,1,0:T(8,128)(2,1)} %copy-done.3) | copy-start | bytes 196612
  65.9 3.4 %copy-start.6 = (bf16[2,4,16,256]{3,2,1,0:T(8,128)(2,1)S(1)}, bf16[2,4,16,256]{3,2,1,0:T(8,128)(2,1)}, u32[]{:S(2)}) copy-start(bf16[2,4,16,256]{3,2,1,0:T(8,128)(2,1)} %copy-done.5) | copy-start | bytes 196612
  65.9 3.4 %copy-start.8 = (bf16[16,256]{1,0:T(8,128)(2,1)S(1)}, bf16[16,256]{1,0:T(8,128)(2,1)}, u32[]{:S(2)}) copy-start(bf16[16,256]{1,0:T(8,128)(2,1)} %copy-done.7) | copy-start | bytes 24580
  66.6 8.4 %copy-start.9 = (bf16[2,512]{1,0:T(2,128)(2,1)S(1)}, bf16[2,512]{1,0:T(2,128)(2,1)}, u32[]{:S(2)}) copy-start(bf16[2,512]{1,0:T(2,128)(2,1)} %refs_14_.1) | copy-start | bytes 6148
  66.6 16.4 %collective-permute-start.23 = (bf16[9,32,512]{2,1,0:T(8,128)(2,1)S(1)}, bf16[9,32,512]{2,1,0:T(8,128)(2,1)S(1)}, u32[]{:S(2)}, u32[]{:S(2)}) collective-permute-start(bf16[9,32,512]{2,1,0:T(8,128)(2,1)S(1)} %get-tuple-element.241.refs_1_), channel_id=1, source_target_pairs={{0,16},{16,0},{1,17},{17,1},{2,18},{18,2},{3,19},{19,3},{4,20},{20... | collective-permute-start | bytes 884744 | tf_op jit(solution)/shard_map/ppermute | solution.py:992
  78.3 4.7 %collective-permute-start.24 = (f32[16,256]{1,0:T(8,128)S(1)}, f32[16,256]{1,0:T(8,128)S(1)}, u32[]{:S(2)}, u32[]{:S(2)}) collective-permute-start(f32[16,256]{1,0:T(8,128)S(1)} %get-tuple-element.242.refs_3_), channel_id=1, source_target_pairs={{0,16},{16,0},{1,17},{17,1},{2,18},{18,2},{3,19},{19,3},{4,20},{20... | collective-permute-start | bytes 49160 | tf_op jit(solution)/shard_map/ppermute | solution.py:992
  80.7 6.8 %collective-permute-start.20 = (bf16[3,64,512]{2,1,0:T(8,128)(2,1)S(1)}, bf16[3,64,512]{2,1,0:T(8,128)(2,1)S(1)}, u32[]{:S(2)}, u32[]{:S(2)}) collective-permute-start(bf16[3,64,512]{2,1,0:T(8,128)(2,1)S(1)} %get-tuple-element.236), channel_id=1, source_target_pairs={{0,4},{4,0},{1,5},{5,1},{2,6},{6,2},{3,7},{7,3},{8,12},{12,8},{9,1... | collective-permute-start | bytes 589832 | tf_op jit(solution)/shard_map/ppermute | solution.py:992
  82.3 7.8 %collective-permute-start.21 = (bf16[3,64,512]{2,1,0:T(8,128)(2,1)S(1)}, bf16[3,64,512]{2,1,0:T(8,128)(2,1)S(1)}, u32[]{:S(2)}, u32[]{:S(2)}) collective-permute-start(bf16[3,64,512]{2,1,0:T(8,128)(2,1)S(1)} %get-tuple-element.238), channel_id=1, source_target_pairs={{0,8},{8,0},{1,9},{9,1},{2,10},{10,2},{3,11},{11,3},{4,12},{12,4},... | collective-permute-start | bytes 589832 | tf_op jit(solution)/shard_map/ppermute | solution.py:992
  82.3 7.8 %collective-permute-start.22 = (bf16[3,64,512]{2,1,0:T(8,128)(2,1)S(1)}, bf16[3,64,512]{2,1,0:T(8,128)(2,1)S(1)}, u32[]{:S(2)}, u32[]{:S(2)}) collective-permute-start(bf16[3,64,512]{2,1,0:T(8,128)(2,1)S(1)} %get-tuple-element.240), channel_id=1, source_target_pairs={{0,2},{2,0},{1,3},{3,1},{4,6},{6,4},{5,7},{7,5},{8,10},{10,8},{9,1... | collective-permute-start | bytes 589832 | tf_op jit(solution)/shard_map/ppermute | solution.py:992
  83.7 7.8 %collective-permute-start.29 = (bf16[3,32,512]{2,1,0:T(8,128)(2,1)S(1)}, bf16[3,32,512]{2,1,0:T(8,128)(2,1)S(1)}, u32[]{:S(2)}, u32[]{:S(2)}) collective-permute-start(bf16[3,32,512]{2,1,0:T(8,128)(2,1)S(1)} %get-tuple-element.252.refs_3_), channel_id=1, source_target_pairs={{0,2},{2,0},{1,3},{3,1},{4,6},{6,4},{5,7},{7,5},{8,10},{10,8},{9,1... | collective-permute-start | bytes 294920 | tf_op jit(solution)/shard_map/ppermute | solution.py:992
  85.1 7.0 %collective-permute-start.30 = (bf16[3,32,512]{2,1,0:T(8,128)(2,1)S(1)}, bf16[3,32,512]{2,1,0:T(8,128)(2,1)S(1)}, u32[]{:S(2)}, u32[]{:S(2)}) collective-permute-start(bf16[3,32,512]{2,1,0:T(8,128)(2,1)S(1)} %get-tuple-element.253.refs_5_), channel_id=1, source_target_pairs={{0,4},{4,0},{1,5},{5,1},{2,6},{6,2},{3,7},{7,3},{8,12},{12,8},{9,1... | collective-permute-start | bytes 294920 | tf_op jit(solution)/shard_map/ppermute | solution.py:992
  87.5 5.9 %collective-permute-start.28 = (bf16[4,32,512]{2,1,0:T(8,128)(2,1)S(1)}, bf16[4,32,512]{2,1,0:T(8,128)(2,1)S(1)}, u32[]{:S(2)}, u32[]{:S(2)}) collective-permute-start(bf16[4,32,512]{2,1,0:T(8,128)(2,1)S(1)} %get-tuple-element.251.refs_1_), channel_id=1, source_target_pairs={{0,8},{8,0},{1,9},{9,1},{2,10},{10,2},{3,11},{11,3},{4,12},{12,4},... | collective-permute-start | bytes 393224 | tf_op jit(solution)/shard_map/ppermute | solution.py:992
  90.8 4.8 %collective-permute-start.25 = (bf16[3,32,512]{2,1,0:T(8,128)(2,1)S(1)}, bf16[3,32,512]{2,1,0:T(8,128)(2,1)S(1)}, u32[]{:S(2)}, u32[]{:S(2)}) collective-permute-start(bf16[3,32,512]{2,1,0:T(8,128)(2,1)S(1)} %get-tuple-element.246), channel_id=1, source_target_pairs={{0,8},{8,0},{1,9},{9,1},{2,10},{10,2},{3,11},{11,3},{4,12},{12,4},... | collective-permute-start | bytes 294920 | tf_op jit(solution)/shard_map/ppermute | solution.py:992
  90.9 6.8 %collective-permute-start.26 = (bf16[3,32,512]{2,1,0:T(8,128)(2,1)S(1)}, bf16[3,32,512]{2,1,0:T(8,128)(2,1)S(1)}, u32[]{:S(2)}, u32[]{:S(2)}) collective-permute-start(bf16[3,32,512]{2,1,0:T(8,128)(2,1)S(1)} %get-tuple-element.248), channel_id=1, source_target_pairs={{0,2},{2,0},{1,3},{3,1},{4,6},{6,4},{5,7},{7,5},{8,10},{10,8},{9,1... | collective-permute-start | bytes 294920 | tf_op jit(solution)/shard_map/ppermute | solution.py:992
  91.5 6.2 %collective-permute-start.27 = (bf16[3,32,512]{2,1,0:T(8,128)(2,1)S(1)}, bf16[3,32,512]{2,1,0:T(8,128)(2,1)S(1)}, u32[]{:S(2)}, u32[]{:S(2)}) collective-permute-start(bf16[3,32,512]{2,1,0:T(8,128)(2,1)S(1)} %get-tuple-element.250), channel_id=1, source_target_pairs={{0,4},{4,0},{1,5},{5,1},{2,6},{6,2},{3,7},{7,3},{8,12},{12,8},{9,1... | collective-permute-start | bytes 294920 | tf_op jit(solution)/shard_map/ppermute | solution.py:992
  94.1 5.9 %collective-permute-start.33 = (bf16[3,64,512]{2,1,0:T(8,128)(2,1)S(1)}, bf16[3,64,512]{2,1,0:T(8,128)(2,1)S(1)}, u32[]{:S(2)}, u32[]{:S(2)}) collective-permute-start(bf16[3,64,512]{2,1,0:T(8,128)(2,1)S(1)} %get-tuple-element.259.refs_3_), channel_id=1, source_target_pairs={{0,8},{8,0},{1,9},{9,1},{2,10},{10,2},{3,11},{11,3},{4,12},{12,4},... | collective-permute-start | bytes 589832 | tf_op jit(solution)/shard_map/ppermute | solution.py:992
  94.2 5.8 %collective-permute-start.34 = (bf16[3,64,512]{2,1,0:T(8,128)(2,1)S(1)}, bf16[3,64,512]{2,1,0:T(8,128)(2,1)S(1)}, u32[]{:S(2)}, u32[]{:S(2)}) collective-permute-start(bf16[3,64,512]{2,1,0:T(8,128)(2,1)S(1)} %get-tuple-element.260.refs_5_), channel_id=1, source_target_pairs={{0,2},{2,0},{1,3},{3,1},{4,6},{6,4},{5,7},{7,5},{8,10},{10,8},{9,1... | collective-permute-start | bytes 589832 | tf_op jit(solution)/shard_map/ppermute | solution.py:992
  95.7 6.4 %collective-permute-start.32 = (bf16[4,64,512]{2,1,0:T(8,128)(2,1)S(1)}, bf16[4,64,512]{2,1,0:T(8,128)(2,1)S(1)}, u32[]{:S(2)}, u32[]{:S(2)}) collective-permute-start(bf16[4,64,512]{2,1,0:T(8,128)(2,1)S(1)} %get-tuple-element.258.refs_1_), channel_id=1, source_target_pairs={{0,4},{4,0},{1,5},{5,1},{2,6},{6,2},{3,7},{7,3},{8,12},{12,8},{9,1... | collective-permute-start | bytes 786440 | tf_op jit(solution)/shard_map/ppermute | solution.py:992
  98.3 4.4 %collective-permute-start.31 = (f32[72,256]{1,0:T(8,128)S(1)}, f32[72,256]{1,0:T(8,128)S(1)}, u32[]{:S(2)}, u32[]{:S(2)}) collective-permute-start(f32[72,256]{1,0:T(8,128)S(1)} %get-tuple-element.257), channel_id=1, source_target_pairs={{0,1},{1,0},{2,3},{3,2},{4,5},{5,4},{6,7},{7,6},{8,9},{9,8},{10,11... | collective-permute-start | bytes 221192 | tf_op jit(solution)/shard_map/ppermute | solution.py:992
  98.4 17.3 %collective-permute-start.36 = (bf16[9,32,512]{2,1,0:T(8,128)(2,1)S(1)}, bf16[9,32,512]{2,1,0:T(8,128)(2,1)S(1)}, u32[]{:S(2)}, u32[]{:S(2)}) collective-permute-start(bf16[9,32,512]{2,1,0:T(8,128)(2,1)S(1)} %get-tuple-element.268.refs_1_), channel_id=1, source_target_pairs={{0,16},{16,0},{1,17},{17,1},{2,18},{18,2},{3,19},{19,3},{4,20},{20... | collective-permute-start | bytes 884744 | tf_op jit(solution)/shard_map/ppermute | solution.py:992
  105.9 9.9 %collective-permute-start.37 = (f32[16,256]{1,0:T(8,128)S(1)}, f32[16,256]{1,0:T(8,128)S(1)}, u32[]{:S(2)}, u32[]{:S(2)}) collective-permute-start(f32[16,256]{1,0:T(8,128)S(1)} %get-tuple-element.269.refs_3_), channel_id=1, source_target_pairs={{0,16},{16,0},{1,17},{17,1},{2,18},{18,2},{3,19},{19,3},{4,20},{20... | collective-permute-start | bytes 49160 | tf_op jit(solution)/shard_map/ppermute | solution.py:992
  107.6 9.7 %collective-permute-start.41 = (bf16[3,128,512]{2,1,0:T(8,128)(2,1)S(1)}, bf16[3,128,512]{2,1,0:T(8,128)(2,1)S(1)}, u32[]{:S(2)}, u32[]{:S(2)}) collective-permute-start(bf16[3,128,512]{2,1,0:T(8,128)(2,1)S(1)} %get-tuple-element.270.refs_2_), channel_id=1, source_target_pairs={{0,4},{4,0},{1,5},{5,1},{2,6},{6,2},{3,7},{7,3},{8,12},{12,8},{9,1... | collective-permute-start | bytes 1179656 | tf_op jit(solution)/shard_map/ppermute | solution.py:992
  109.4 14.8 %collective-permute-start.42 = (bf16[3,128,512]{2,1,0:T(8,128)(2,1)S(1)}, bf16[3,128,512]{2,1,0:T(8,128)(2,1)S(1)}, u32[]{:S(2)}, u32[]{:S(2)}) collective-permute-start(bf16[3,128,512]{2,1,0:T(8,128)(2,1)S(1)} %get-tuple-element.271.refs_3_), channel_id=1, source_target_pairs={{0,8},{8,0},{1,9},{9,1},{2,10},{10,2},{3,11},{11,3},{4,12},{12,4},... | collective-permute-start | bytes 1179656 | tf_op jit(solution)/shard_map/ppermute | solution.py:992
  110.4 13.7 %collective-permute-start.35 = (bf16[4,128,512]{2,1,0:T(8,128)(2,1)S(1)}, bf16[4,128,512]{2,1,0:T(8,128)(2,1)S(1)}, u32[]{:S(2)}, u32[]{:S(2)}) collective-permute-start(bf16[4,128,512]{2,1,0:T(8,128)(2,1)S(1)} %get-tuple-element.267.refs_1_), channel_id=1, source_target_pairs={{0,2},{2,0},{1,3},{3,1},{4,6},{6,4},{5,7},{7,5},{8,10},{10,8},{9,1... | collective-permute-start | bytes 1572872 | tf_op jit(solution)/shard_map/ppermute | solution.py:992
  116.4 9.8 %collective-permute-start.38 = (bf16[4,32,512]{2,1,0:T(8,128)(2,1)S(1)}, bf16[4,32,512]{2,1,0:T(8,128)(2,1)S(1)}, u32[]{:S(2)}, u32[]{:S(2)}) collective-permute-start(bf16[4,32,512]{2,1,0:T(8,128)(2,1)S(1)} %get-tuple-element.274.refs_1_), channel_id=1, source_target_pairs={{0,8},{8,0},{1,9},{9,1},{2,10},{10,2},{3,11},{11,3},{4,12},{12,4},... | collective-permute-start | bytes 393224 | tf_op jit(solution)/shard_map/ppermute | solution.py:992
  116.5 9.7 %collective-permute-start.39 = (bf16[3,32,512]{2,1,0:T(8,128)(2,1)S(1)}, bf16[3,32,512]{2,1,0:T(8,128)(2,1)S(1)}, u32[]{:S(2)}, u32[]{:S(2)}) collective-permute-start(bf16[3,32,512]{2,1,0:T(8,128)(2,1)S(1)} %get-tuple-element.275.refs_3_), channel_id=1, source_target_pairs={{0,2},{2,0},{1,3},{3,1},{4,6},{6,4},{5,7},{7,5},{8,10},{10,8},{9,1... | collective-permute-start | bytes 294920 | tf_op jit(solution)/shard_map/ppermute | solution.py:992
  117.2 8.9 %collective-permute-start.40 = (bf16[3,32,512]{2,1,0:T(8,128)(2,1)S(1)}, bf16[3,32,512]{2,1,0:T(8,128)(2,1)S(1)}, u32[]{:S(2)}, u32[]{:S(2)}) collective-permute-start(bf16[3,32,512]{2,1,0:T(8,128)(2,1)S(1)} %get-tuple-element.276.refs_5_), channel_id=1, source_target_pairs={{0,4},{4,0},{1,5},{5,1},{2,6},{6,2},{3,7},{7,3},{8,12},{12,8},{9,1... | collective-permute-start | bytes 294920 | tf_op jit(solution)/shard_map/ppermute | solution.py:992
  126.8 6.4 %collective-permute-start.43 = (bf16[4,64,512]{2,1,0:T(8,128)(2,1)S(1)}, bf16[4,64,512]{2,1,0:T(8,128)(2,1)S(1)}, u32[]{:S(2)}, u32[]{:S(2)}) collective-permute-start(bf16[4,64,512]{2,1,0:T(8,128)(2,1)S(1)} %get-tuple-element.287.refs_1_), channel_id=1, source_target_pairs={{0,4},{4,0},{1,5},{5,1},{2,6},{6,2},{3,7},{7,3},{8,12},{12,8},{9,1... | collective-permute-start | bytes 786440 | tf_op jit(solution)/shard_map/ppermute | solution.py:992
  127.1 5.7 %collective-permute-start.44 = (bf16[3,64,512]{2,1,0:T(8,128)(2,1)S(1)}, bf16[3,64,512]{2,1,0:T(8,128)(2,1)S(1)}, u32[]{:S(2)}, u32[]{:S(2)}) collective-permute-start(bf16[3,64,512]{2,1,0:T(8,128)(2,1)S(1)} %get-tuple-element.288.refs_3_), channel_id=1, source_target_pairs={{0,8},{8,0},{1,9},{9,1},{2,10},{10,2},{3,11},{11,3},{4,12},{12,4},... | collective-permute-start | bytes 589832 | tf_op jit(solution)/shard_map/ppermute | solution.py:992
  127.1 5.7 %collective-permute-start.45 = (bf16[3,64,512]{2,1,0:T(8,128)(2,1)S(1)}, bf16[3,64,512]{2,1,0:T(8,128)(2,1)S(1)}, u32[]{:S(2)}, u32[]{:S(2)}) collective-permute-start(bf16[3,64,512]{2,1,0:T(8,128)(2,1)S(1)} %get-tuple-element.289.refs_5_), channel_id=1, source_target_pairs={{0,2},{2,0},{1,3},{3,1},{4,6},{6,4},{5,7},{7,5},{8,10},{10,8},{9,1... | collective-permute-start | bytes 589832 | tf_op jit(solution)/shard_map/ppermute | solution.py:992
  134.0 11.5 %collective-permute-start.46 = (bf16[4,128,512]{2,1,0:T(8,128)(2,1)S(1)}, bf16[4,128,512]{2,1,0:T(8,128)(2,1)S(1)}, u32[]{:S(2)}, u32[]{:S(2)}) collective-permute-start(bf16[4,128,512]{2,1,0:T(8,128)(2,1)S(1)} %get-tuple-element.291.refs_1_.refs_5_), channel_id=1, source_target_pairs={{0,2},{2,0},{1,3},{3,1},{4,6},{6,4},{5,7},{7,5},{8,10},{10,8},{9,1... | collective-permute-start | bytes 1572872 | tf_op jit(solution)/shard_map/ppermute | solution.py:992
  134.5 8.3 %collective-permute-start.47 = (bf16[3,128,512]{2,1,0:T(8,128)(2,1)S(1)}, bf16[3,128,512]{2,1,0:T(8,128)(2,1)S(1)}, u32[]{:S(2)}, u32[]{:S(2)}) collective-permute-start(bf16[3,128,512]{2,1,0:T(8,128)(2,1)S(1)} %get-tuple-element.292.refs_2_), channel_id=1, source_target_pairs={{0,4},{4,0},{1,5},{5,1},{2,6},{6,2},{3,7},{7,3},{8,12},{12,8},{9,1... | collective-permute-start | bytes 1179656 | tf_op jit(solution)/shard_map/ppermute | solution.py:992
  135.7 8.6 %collective-permute-start.48 = (bf16[3,128,512]{2,1,0:T(8,128)(2,1)S(1)}, bf16[3,128,512]{2,1,0:T(8,128)(2,1)S(1)}, u32[]{:S(2)}, u32[]{:S(2)}) collective-permute-start(bf16[3,128,512]{2,1,0:T(8,128)(2,1)S(1)} %get-tuple-element.293.refs_3_), channel_id=1, source_target_pairs={{0,8},{8,0},{1,9},{9,1},{2,10},{10,2},{3,11},{11,3},{4,12},{12,4},... | collective-permute-start | bytes 1179656 | tf_op jit(solution)/shard_map/ppermute | solution.py:992

commit v2 on v1

--- a/solution.py
+++ b/solution.py
@@ -631,9 +631,7 @@
     return jnp.where(column == centre, 0.75, 0.0) + jnp.where(column == near, 0.25, 0.0)
 
 
-def rgb_kernel(
-    valid, bias, own, other, rgb_in, grad_rgb, rgb_out, grad_in, grad_latent, pack, raster
-):
+def rgb_kernel(valid, bias, own, other, rgb_in, grad_rgb, rgb_out, grad_in, sums, raster):
     images = rgb_in.shape[0]
     double = upsampling(RES, HALF)
     lane = lax.broadcasted_iota(jnp.int32, (HALF, PLANE), 1)
@@ -647,8 +645,7 @@
             plane = 2 * qy + qx
             rows = []
             for image in range(images):
-                rows_here = rows_at(1 + 4 * image + plane, 8)
-                both = own[rows_here, :] + other[rows_here, :]
+                both = own[image, plane] + other[image, plane]
                 rows += [mask * both[colour : colour + 1] for colour in range(3)]
             found = exact(jnp.concatenate(rows, 0), choose, 1, 0)
             for index in range(3 * images):
@@ -668,18 +665,11 @@
             grad = grad_rgb[image, colour].astype(F32) * keep
             grad_in[image, colour] = exact(exact(double, grad, 0, 0), double, 1, 0)
             biases[colour] = biases[colour] + jnp.sum(grad, keepdims=True)
-    total = own[:8, :] + other[:8, :]
-    for image in range(images):
-        grad_latent[image : image + 1, :] = jnp.concatenate(
-            [total[2 * image : 2 * image + 1], total[2 * image + 1 : 2 * image + 2]], 1
-        )
-    scalars = total[2 * images : 2 * images + 1]
-    lane = lax.broadcasted_iota(jnp.int32, scalars.shape, 1)
-    for index, value in enumerate([squares] + biases):
-        scalars = scalars + jnp.where(lane == 4 + index, value, 0.0)
-    for image in range(images):
-        scalars = scalars + jnp.where(lane == 8, valid[image : image + 1, :], 0.0)
-    pack[...] = jnp.concatenate([scalars, jnp.zeros((15, scalars.shape[1]), F32)], 0)
+    sums[...] = jnp.concatenate(
+        [jnp.broadcast_to(member, (1, 128)) for member in [squares] + biases]
+        + [jnp.zeros((4, 128), F32)],
+        0,
+    )
 
 
 def style_grads_kernel(
@@ -699,7 +689,8 @@
     a3,
     latent,
     rgb_grad,
-    planes,
+    rgb_sums,
+    valid,
     pack,
     crossing,
 ):
@@ -731,12 +722,14 @@
         for image in range(1, images):
             total = total + sums[image, row : row + 1, :]
         scalars = scalars + jnp.where(lane == index, jnp.sum(total, keepdims=True), 0.0)
+    wide = jnp.concatenate([rgb_sums[...]] * (share // 128), 1)
+    for index in range(4):
+        scalars = scalars + jnp.where(lane == 4 + index, wide[index : index + 1], 0.0)
+    for image in range(images):
+        scalars = scalars + jnp.where(lane == 8, valid[image : image + 1, :], 0.0)
     pieces = [grad_latent[b : b + 1, h * share : (h + 1) * share] for b in range(images) for h in (0, 1)]
-    blank = jnp.zeros((8 - len(pieces) - 1, share), F32)
-    crossing[:8, :] = jnp.concatenate(pieces + [scalars, blank], 0)
-    for image in range(images):
-        for plane in range(4):
-            crossing[rows_at(1 + 4 * image + plane, 8), :] = planes[image, plane]
+    blank = jnp.zeros((crossing.shape[0] - len(pieces), share), F32)
+    crossing[...] = jnp.concatenate(pieces + [blank], 0)
     values = latent[...].astype(F32)
     packed = [values[:, :share], values[:, share:]] + rows
     for sums in (sums_one, sums_two):
@@ -744,8 +737,15 @@
         for image in range(1, images):
             bias = bias + sums[image, 0:1, :]
         packed.append(bias)
-    packed += [rgb_grad[:3, :], jnp.zeros((1, share), F32)]
+    packed += [rgb_grad[:3, :], scalars]
     pack[...] = jnp.concatenate(packed, 0)
+
+
+def latent_kernel(own, other, out):
+    total = own[...] + other[...]
+    for image in range(out.shape[0]):
+        halves = [total[2 * image + half : 2 * image + half + 1] for half in range(2)]
+        out[image : image + 1, :] = jnp.concatenate(halves, 1)
 
 
 def relay_kernel(source, out):
@@ -773,7 +773,7 @@
 
 
 def spread_kernel(place, *refs, images, groups):
-    packs, outs, everything = refs[:-10], refs[-10:-1], refs[-1]
+    packs, outs, everything = refs[:-11], refs[-11:-1], refs[-1]
     collect(place, packs, groups, everything)
     count = everything.shape[0]
 
@@ -793,15 +793,12 @@
     outs[6][...] = total[at : at + 1]
     outs[7][...] = total[at + 1 : at + 2]
     outs[8][...] = total[at + 2 : at + 5]
-
-
-def scalars_kernel(place, *refs, groups):
-    packs, (gains, rms, rgb_bias, everything) = refs[:-4], refs[-4:]
-    collect(place, packs, groups, everything)
-    scalars = everything[0, 0:1, :]
-    for device in range(1, everything.shape[0]):
-        scalars = scalars + everything[device, 0:1, :]
-    lane = lax.broadcasted_iota(jnp.int32, scalars.shape, 1)
+    outs[9][...] = total[total.shape[0] - 1 :]
+
+
+def scalars_kernel(own, other, gains, rms, rgb_bias):
+    lane = lax.broadcasted_iota(jnp.int32, own.shape, 1)
+    scalars = own[...] + jnp.where(lane < 4, other[...], 0.0)
     share = scalars.shape[1]
     real = jnp.sum(jnp.where(lane == 8, scalars, 0.0), keepdims=True)
     entries = jnp.where(lane == 4, 3.0 * RES * RES, 2.0 * share * RES * RES)
@@ -922,14 +919,10 @@
 
 def finish_scalars_kernel(place, *refs, groups):
     count = len(groups)
-    parts, own, (out, gains, rms, rgb_bias, held, sems, everything) = (
-        refs[:count],
-        refs[count + 1],
-        refs[-7:],
-    )
+    parts, (own, other, out, gains, rms, rgb_bias, held, sems) = refs[:count], refs[count + 1 :]
 
     def between():
-        scalars_kernel(place, own, parts[0], gains, rms, rgb_bias, everything, groups=groups)
+        scalars_kernel(own, other, gains, rms, rgb_bias)
 
     finish_kernel(place, *parts, out, held, sems, groups=groups, away=True, between=between)
 
@@ -1094,24 +1087,20 @@
     def finish(self, token, out):
         return self.finish_half(token, self.got, (out,), True)
 
-    def finish_scalars(self, token, out, devices):
+    def finish_scalars(self, token, out, own, other):
         _, half, cols = self.got[0].shape
         last = 1 + len(self.got)
         return call(
             functools.partial(finish_scalars_kernel, groups=self.groups),
             (shape(9, 2 * half, cols), shape(2), shape(3), shape(3)),
-            [
-                pltpu.VMEM((9, half, cols), F32),
-                pltpu.SemaphoreType.DMA((9,)),
-                pltpu.VMEM((devices, 16, cols // 2), F32),
-            ],
+            [pltpu.VMEM((9, half, cols), F32), pltpu.SemaphoreType.DMA((9,))],
             smem=1,
             after=(token,),
             hbm=(0,),
             scalars=(1, 2, 3),
             loose=(last,),
             aliases={last: 0},
-        )(self.place, *self.got, out, self.own[0])
+        )(self.place, *self.got, out, own, other)
 
 
 def gather_packs(pack):
@@ -1312,25 +1301,6 @@
         styles,
     )
     token = reduce_two.fold(token, 1)
-    (grad_features_in, style_sums), token = call(
-        input_one_grad,
-        (shape(images, PLANE, share), shape(images, share)),
-        smem=1,
-        after=(token,),
-        plain=(0,),
-        loose=(4,),
-    )(place, grad_conv_one, grad_conv_one_other, flat_one, features, styles)
-    token = reduce_two.fold(token, 2)
-    parts_one, token = call(
-        kernel_one_grad,
-        group_shapes(GROUPS_ONE, half, channels),
-        [pltpu.VMEM((images, PLANE, share), BF16), pltpu.VMEM((share, share), F32)],
-        smem=1,
-        after=(token,),
-        micros=STAGE,
-    )(place, scaled_one, grad_conv_one, grad_conv_one_other, flat_one, styles)
-    reduce_one = Reduction(place, GROUPS_ONE, parts_one)
-    token = reduce_two.across(token)
     (features_out, rgb_planes, rgb_grad, sums_two), token = call(
         outputs_two_kernel,
         (
@@ -1354,9 +1324,37 @@
         styles,
         rgb_rows_in,
     )
+    rgb_planes_other = swap(rgb_planes, "chan")
+    token = reduce_two.fold(token, 2)
+    parts_one, token = call(
+        kernel_one_grad,
+        group_shapes(GROUPS_ONE, half, channels),
+        [pltpu.VMEM((images, PLANE, share), BF16), pltpu.VMEM((share, share), F32)],
+        smem=1,
+        after=(token, rgb_planes_other),
+        micros=STAGE,
+    )(place, scaled_one, grad_conv_one, grad_conv_one_other, flat_one, styles)
+    reduce_one = Reduction(place, GROUPS_ONE, parts_one)
+    token = reduce_two.across(token)
+    (grad_features_in, style_sums), token = call(
+        input_one_grad,
+        (shape(images, PLANE, share), shape(images, share)),
+        smem=1,
+        after=(token,),
+        plain=(0,),
+        loose=(4,),
+    )(place, grad_conv_one, grad_conv_one_other, flat_one, features, styles)
+    (rgb_out, grad_rgb_in, rgb_sums), token = call(
+        rgb_kernel,
+        (shape(*grad_rgb.shape), shape(*rgb_in.shape), shape(8, 128)),
+        [pltpu.VMEM((3 * images, RES, 128), F32)],
+        after=(token,),
+        plain=(0, 1),
+        loose=(1, 4, 5),
+    )(valid_rows, rgb_bias.reshape(1, -1), rgb_planes, rgb_planes_other, rgb_in, grad_rgb)
     (pack, crossing), token = call(
         style_grads_kernel,
-        (shape(16, share), shape(8 + 32 * images, share)),
+        (shape(16, share), shape(8, share)),
         smem=1,
         after=(token,),
         loose=(11, 12, 13),
@@ -1377,7 +1375,8 @@
         affine_three,
         latent,
         rgb_grad,
-        rgb_planes,
+        rgb_sums,
+        valid_rows,
     )
     packs = [pack, swap(pack, "far")] if alone else []
     token = reduce_one.fold(token, 1, micros=0)
@@ -1385,25 +1384,14 @@
     token = reduce_one.fold(token, 2)
     token = reduce_two.join(token, 2)
     token = reduce_one.across(token)
-    relayed, token = call(relay_kernel, shape(8 + 32 * images, share), after=(token,))(crossing)
+    relayed, token = call(relay_kernel, shape(8, share), after=(token,))(crossing)
     crossing_other = swap(relayed, "chan")
     token = reduce_two.join(token, 1)
-    (rgb_out, grad_rgb_in, grad_latent, scalars), token = call(
-        rgb_kernel,
-        (
-            shape(*grad_rgb.shape),
-            shape(*rgb_in.shape),
-            shape(images, channels),
-            shape(16, share),
-        ),
-        [pltpu.VMEM((3 * images, RES, 128), F32)],
-        after=(token,),
-        plain=(0, 1, 2),
-        loose=(1, 4, 5),
-    )(valid_rows, rgb_bias.reshape(1, -1), crossing, crossing_other, rgb_in, grad_rgb)
-    rows = [scalars, swap(scalars, "far")] if alone else []
+    grad_latent, token = call(
+        latent_kernel, shape(images, channels), after=(token,), plain=(0,)
+    )(crossing, crossing_other)
     sum_two, token = reduce_two.finish_own(token)
-    token = reduce_one.total(token, *rows)
+    token = reduce_one.total(token)
     sum_two, token = reduce_two.finish(token, sum_two)
     token = reduce_one.join(token, 2)
     if alone:
@@ -1412,30 +1400,21 @@
         packs = [gather_packs(pack)]
     spread_out, token = call(
         functools.partial(spread_kernel, images=images, groups=GROUPS_TWO),
-        (shape(channels, share),) * 3 + (shape(1, share),) * 5 + (shape(3, share),),
+        (shape(channels, share),) * 3
+        + (shape(1, share),) * 5
+        + (shape(3, share), shape(1, share)),
         [pltpu.VMEM((devices, 16, share), F32)],
         smem=1,
         after=(token,),
         plain=tuple(range(9)),
     )(place, *packs)
+    row_other = swap(spread_out[9], "chan")
     token = reduce_one.join(token, 1)
     sum_one, token = reduce_one.finish_own(token)
     affine_grads, affine_biases, points = spread_out[0:3], spread_out[3:6], spread_out[6:8]
     rgb_total = spread_out[8]
-    if alone:
-        found, token = reduce_one.finish_scalars(token, sum_one, devices)
-        sum_one, gains, rms_values, rgb_bias_grad = found
-    else:
-        rows = [gather_packs(scalars)]
-        (gains, rms_values, rgb_bias_grad), token = call(
-            functools.partial(scalars_kernel, groups=GROUPS_ONE),
-            (shape(2), shape(3), shape(3)),
-            [pltpu.VMEM((devices, 16, share), F32)],
-            smem=1,
-            after=(token,),
-            scalars=(0, 1, 2),
-        )(place, *rows)
-        sum_one, token = reduce_one.finish(token, sum_one)
+    found, token = reduce_one.finish_scalars(token, sum_one, spread_out[9], row_other)
+    sum_one, gains, rms_values, rgb_bias_grad = found
     affine_outs = []
     for grad, bias in zip(affine_grads, affine_biases):
         affine_outs += [grad, bias.reshape(-1)]

time: 149 us -> 147 us (0.987)
  waiting for transfers between devices: 31 us -> 23.8 us
  starting transfers between devices: 42.6 us -> 47.7 us
    ppermute x49 -> x50, waiting for transfers between devices: 31 us -> 23.8 us  [swap(): return lax.ppermute(values, axis_name, SWAP)]
    ppermute x49 -> x50, starting transfers between devices: 42.6 us -> 47.7 us  [swap(): return lax.ppermute(values, axis_name, SWAP)]
    pallas_call x33 -> x34, Pallas kernels: 72.4 us -> 73.1 us  [run(): pl.pallas_call(inner, out_shape=tuple((member if index in hbm + scalars +...]
  transfers between devices with their start and end apart: 49 -> 50, of which waited for: 19 -> 15; matrix products, arithmetic and copies ran while one was open for 0% -> 0% of each run, Pallas kernels for 35% -> 35%
where the time goes in v2:
time: 147 us
  Pallas kernels  73.1 us (50%)
  starting transfers between devices  47.7 us (32%)
  waiting for transfers between devices  23.8 us (16%)
  between operations  1.84 us (1%)
    pallas_call x34, Pallas kernels, run(): pl.pallas_call(inner, out_shape=tuple((member if index in hbm + scalars +...  73.1 us
    ppermute x50, starting transfers between devices, swap(): return lax.ppermute(values, axis_name, SWAP)  47.7 us
    ppermute x50, waiting for transfers between devices, swap(): return lax.ppermute(values, axis_name, SWAP)  23.8 us
  transfers between devices with their start and end apart: 50, of which 15 were waited for; matrix products, arithmetic and copies ran while one was open for 0% of the time, Pallas kernels for 35%

profile of v2, /device:TPU:0, one launch (start us, length us, event | category | flops | bytes accessed | tf_op | source)
XLA Modules:
  0.0 146.6 jit_solution(4454158955587309302)
XLA Ops:
  0.8 2.7 %style_kernel.1 = (f32[3,2,256]{2,1,0:T(2,128)S(1)}, bf16[2,256,256]{2,1,0:T(8,128)(2,1)S(1)}, bf16[9,256,256]{2,1,0:T(8,128)(2,1)S(1)}, f32[8,128]{1,0:T(8,128)S(1)}) custom-call(s32[5]{0:T(128)S(1)} %stack.23.refs_0_, bf16[9,256,512]{2,1,0:T(8,128)(2,1)} %bitcast.30, bf16[2,512]{1,0:T(2,128)(2,1)} %refs_14_.1, bf16[512,256]{1,0:T(8,128)(2,1)} %refs_11_.1, ...), custom_call_target="tpu_custom_call" | custom-call | flops 1024 | bytes 1024 | tf_op jit(solution)/shard_map/style_kernel/pallas_call | solution.py:944
  4.1 2.0 %squares_kernel.2 = (f32[256,512]{1,0:T(8,128)S(1)}, f32[2,256]{1,0:T(2,128)S(1)}, f32[2,256]{1,0:T(2,128)S(1)}, bf16[16,256]{1,0:T(8,128)(2,1)S(1)}, bf16[2,16,256]{2,1,0:T(8,128)(2,1)}, /*index=5*/f32[8,128]{1,0:T(8,128)S(1)}) custom-call(s32[5]{0:T(128)S(1)} %stack.23.refs_0_, ...), custom_call_target="tpu_custom_call" | custom-call | flops 1024 | bytes 1024 | tf_op jit(solution)/shard_map/squares_kernel/pallas_call | solution.py:944
  7.2 2.7 %planes_kernel.1 = (bf16[2,4,16,256]{3,2,1,0:T(8,128)(2,1)S(1)}, bf16[2,4,16,256]{3,2,1,0:T(8,128)(2,1)S(1)}, bf16[2,4,16,256]{3,2,1,0:T(8,128)(2,1)S(1)}, bf16[9,256,256]{2,1,0:T(8,128)(2,1)S(1)}, f32[8,128]{1,0:T(8,128)S(1)}) custom-call(s32[5]{0:T(128)S(1)} %stack.23.refs_0_, ...), custom_call_target="tpu_custom_call" | custom-call | flops 1024 | bytes 1024 | tf_op jit(solution)/shard_map/planes_kernel/pallas_call | solution.py:944
  10.1 2.8 %conv_one_kernel.1 = (f32[2,4,256,256]{3,2,1,0:T(8,128)S(1)}, bf16[2,4,256,256]{3,2,1,0:T(8,128)(2,1)S(1)}, f32[2,256]{1,0:T(2,128)S(1)}, f32[8,128]{1,0:T(8,128)S(1)}) custom-call(s32[5]{0:T(128)S(1)} %stack.23.refs_0_, bf16[2,256,256]{2,1,0:T(8,128)(2,1)S(1)} %get-tuple-element.164.refs_1_, bf16[2,256,256]{2,1,0:T(8,128)(2,1)S(1)} %collective-permute-done.refs_2_, ...), custom_call_target="tpu_custom_call" | custom-call | flops 66000003072 | bytes 1024 | tf_op jit(solution)/shard_map/conv_one_kernel/pallas_call | solution.py:944
  13.4 1.5 %squares_kernel.3 = (f32[256,512]{1,0:T(8,128)S(1)}, f32[2,256]{1,0:T(2,128)S(1)}, f32[2,256]{1,0:T(2,128)S(1)}, bf16[16,256]{1,0:T(8,128)(2,1)S(1)}, bf16[2,16,...) custom-call(s32[5]{0:T(128)S(1)} %stack.23.refs_0_, ...), custom_call_target="tpu_custom_call" | custom-call | flops 1024 | bytes 1024 | tf_op jit(solution)/shard_map/squares_kernel/pallas_call | solution.py:944
  15.0 1.0 collective-permute-done.5.refs_6_
  16.0 7.1 %conv_two_kernel.1 = (f32[2,4,256,256]{3,2,1,0:T(8,128)S(1)}, bf16[2064,256]{1,0:T(8,128)(2,1)S(1)}, f32[2,256]{1,0:T(2,128)S(1)}, f32[8,128]{1,0:T(8,128)S(1)}) custom-call(s32[5]{0:T(128)S(1)} %stack.23.refs_0_, bf16[2,4,256,256]{3,2,1,0:T(8,128)(2,1)S(1)} %get-tuple-element.174.refs_1_.refs_0_, ...), custom_call_target="tpu_custom_call" | custom-call | flops 1024 | bytes 1024 | tf_op jit(solution)/shard_map/conv_two_kernel/pallas_call | solution.py:944
  23.6 2.2 %collective-permute-done.6.refs_4_.refs_2_ = bf16[2064,256]{1,0:T(8,128)(2,1)S(1)} collective-permute-done((bf16[2064,256]{1,0:T(8,128)(2,1)S(1)}, bf16[2064,256]{1,0:T(8,128)(2,1)S(1)}, u32[]{:S(2)}, u32[]{:S(2)}) %collective-permute-start.6) | collective-permute-done | bytes 1056800 | tf_op jit(solution)/shard_map/ppermute | solution.py:985
  25.8 6.4 %kernel_two_grad.1 = (bf16[3,128,512]{2,1,0:T(8,128)(2,1)S(1)}, f32[3,128,512]{2,1,0:T(8,128)S(1)}, bf16[3,128,512]{2,1,0:T(8,128)(2,1)S(1)}, f32[3,128,512]{2,1...) custom-call(s32[5]{0:T(128)S(1)} %stack.23.refs_0_, ...), custom_call_target="tpu_custom_call" | custom-call | flops 1024 | bytes 1024 | tf_op jit(solution)/shard_map/kernel_two_grad/pallas_call | solution.py:944
  32.3 2.7 %collective-permute-start.7 = (bf16[3,128,512]{2,1,0:T(8,128)(2,1)S(1)}, bf16[3,128,512]{2,1,0:T(8,128)(2,1)S(1)}, u32[]{:S(2)}, u32[]{:S(2)}) collective-permute-start(bf16[3,128,512]{2,1,0:T(8,128)(2,1)S(1)} %get-tuple-element.191), channel_id=1, source_target_pairs={{0,2},{2,0},{1,3},{3,1},{4,6},{6,4},{5,7},{7,5},{8,10},{10,8},{9,1... | collective-permute-start | bytes 1179656 | tf_op jit(solution)/shard_map/ppermute | solution.py:985
  35.0 1.6 %collective-permute-start.8 = (bf16[3,128,512]{2,1,0:T(8,128)(2,1)S(1)}, bf16[3,128,512]{2,1,0:T(8,128)(2,1)S(1)}, u32[]{:S(2)}, u32[]{:S(2)}) collective-permute-start(bf16[3,128,512]{2,1,0:T(8,128)(2,1)S(1)} %get-tuple-element.193), channel_id=1, source_target_pairs={{0,4},{4,0},{1,5},{5,1},{2,6},{6,2},{3,7},{7,3},{8,12},{12,8},{9,1... | collective-permute-start | bytes 1179656 | tf_op jit(solution)/shard_map/ppermute | solution.py:985
  36.5 1.5 %collective-permute-start.9 = (bf16[3,128,512]{2,1,0:T(8,128)(2,1)S(1)}, bf16[3,128,512]{2,1,0:T(8,128)(2,1)S(1)}, u32[]{:S(2)}, u32[]{:S(2)}) collective-permute-start(bf16[3,128,512]{2,1,0:T(8,128)(2,1)S(1)} %get-tuple-element.195), channel_id=1, source_target_pairs={{0,8},{8,0},{1,9},{9,1},{2,10},{10,2},{3,11},{11,3},{4,12},{12,4},... | collective-permute-start | bytes 1179656 | tf_op jit(solution)/shard_map/ppermute | solution.py:985
  38.1 6.4 %input_two_grad.1 = (f32[2,4,256,256]{3,2,1,0:T(8,128)S(1)}, bf16[2064,256]{1,0:T(8,128)(2,1)S(1)}, f32[8,128]{1,0:T(8,128)S(1)}) custom-call(s32[5]{0:T(128)S(1)} %stack.23.refs_0_, bf16[2064,256]{1,0:T(8,128)(2,1)S(1)} %get-tuple-element.188.refs_3_.refs_1_, bf16[2064,256]{1,0:T(8,128)(2,1)S(1)} %collective-permute-done.6.refs_4_.refs_2_, ...), custom_call_target="tpu_custom_call" | custom-call | flops 1024 | bytes 1024 | tf_op jit(solution)/shard_map/input_two_grad/pallas_call | solution.py:944
  44.5 2.3 %outputs_one_kernel.1 = (f32[2,8,256]{2,1,0:T(8,128)S(1)}, f32[8,128]{1,0:T(8,128)S(1)}) custom-call(f32[2,4,256,256]{3,2,1,0:T(8,128)S(1)} %get-tuple-element.196.refs_4_.refs_0_, f32[2,4,256,256]{3,2,1,0:T(8,128)S(1)} %get-tuple-element.199.refs_1_, f32[2,256]{1,0:T(2,128)S(1)} %get-tuple-element.197.refs_5_.refs_2_, ...), custom_call_target="tpu_custom_call" | custom-call | flops 1024 | bytes 1024 | tf_op jit(solution)/shard_map/outputs_one_kernel/pallas_call | solution.py:944
  47.3 1.0 fold_kernel.4
  48.9 1.6 %collective-permute-start.13 = (bf16[3,64,512]{2,1,0:T(8,128)(2,1)S(1)}, bf16[3,64,512]{2,1,0:T(8,128)(2,1)S(1)}, u32[]{:S(2)}, u32[]{:S(2)}) collective-permute-start(bf16[3,64,512]{2,1,0:T(8,128)(2,1)S(1)} %get-tuple-element.209), channel_id=1, source_target_pairs={{0,8},{8,0},{1,9},{9,1},{2,10},{10,2},{3,11},{11,3},{4,12},{12,4},... | collective-permute-start | bytes 589832 | tf_op jit(solution)/shard_map/ppermute | solution.py:985
  51.0 5.7 %outputs_two_kernel.1 = (bf16[2,32,32,256]{3,2,1,0:T(8,128)(2,1)}, f32[2,4,8,256]{3,2,1,0:T(8,128)S(1)}, f32[16,256]{1,0:T(8,128)S(1)}, f32[2,8,256]{2,1,0:T(8,128)S(1)}, f32[8,128]{1,0:T(8,128)S(1)}) custom-call(f32[2,4,256,256]{3,2,1,0:T(8,128)S(1)} %get-tuple-element.184.refs_0_, f32[2,256]{1,0:T(2,128)S(1)} %get-tuple-element.185.refs_1_, ...), custom_call_target="tpu_custom_call" | custom-call | flops 1024 | bytes 1024 | tf_op jit(solution)/shard_map/outputs_two_kernel/pallas_call | solution.py:944
  57.2 0.7 fold_kernel.5
  58.2 1.7 %collective-permute-start.16 = (bf16[3,32,512]{2,1,0:T(8,128)(2,1)S(1)}, bf16[3,32,512]{2,1,0:T(8,128)(2,1)S(1)}, u32[]{:S(2)}, u32[]{:S(2)}) collective-permute-start(bf16[3,32,512]{2,1,0:T(8,128)(2,1)S(1)} %get-tuple-element.216), channel_id=1, source_target_pairs={{0,2},{2,0},{1,3},{3,1},{4,6},{6,4},{5,7},{7,5},{8,10},{10,8},{9,1... | collective-permute-start | bytes 294920 | tf_op jit(solution)/shard_map/ppermute | solution.py:985
  59.9 1.5 %collective-permute-start.17 = (bf16[3,32,512]{2,1,0:T(8,128)(2,1)S(1)}, bf16[3,32,512]{2,1,0:T(8,128)(2,1)S(1)}, u32[]{:S(2)}, u32[]{:S(2)}) collective-permute-start(bf16[3,32,512]{2,1,0:T(8,128)(2,1)S(1)} %get-tuple-element.218), channel_id=1, source_target_pairs={{0,4},{4,0},{1,5},{5,1},{2,6},{6,2},{3,7},{7,3},{8,12},{12,8},{9,1... | collective-permute-start | bytes 294920 | tf_op jit(solution)/shard_map/ppermute | solution.py:985
  61.4 2.8 %kernel_one_grad.1 = (bf16[3,128,512]{2,1,0:T(8,128)(2,1)S(1)}, f32[3,128,512]{2,1,0:T(8,128)S(1)}, bf16[3,128,512]{2,1,0:T(8,128)(2,1)S(1)}, f32[3,128,512]{2,1...) custom-call(s32[5]{0:T(128)S(1)} %stack.23.refs_0_, ...), custom_call_target="tpu_custom_call" | custom-call | flops 66000003072 | bytes 1024 | tf_op jit(solution)/shard_map/kernel_one_grad/pallas_call | solution.py:944
  65.2 1.7 %collective-permute-start.20 = (bf16[3,128,512]{2,1,0:T(8,128)(2,1)S(1)}, bf16[3,128,512]{2,1,0:T(8,128)(2,1)S(1)}, u32[]{:S(2)}, u32[]{:S(2)}) collective-permute-start(bf16[3,128,512]{2,1,0:T(8,128)(2,1)S(1)} %get-tuple-element.240), channel_id=1, source_target_pairs={{0,8},{8,0},{1,9},{9,1},{2,10},{10,2},{3,11},{11,3},{4,12},{12,4},... | collective-permute-start | bytes 1179656 | tf_op jit(solution)/shard_map/ppermute | solution.py:985
  67.6 2.7 %collective-permute-start.24 = (bf16[9,32,512]{2,1,0:T(8,128)(2,1)S(1)}, bf16[9,32,512]{2,1,0:T(8,128)(2,1)S(1)}, u32[]{:S(2)}, u32[]{:S(2)}) collective-permute-start(bf16[9,32,512]{2,1,0:T(8,128)(2,1)S(1)} %get-tuple-element.248.refs_1_), channel_id=1, source_target_pairs={{0,16},{16,0},{1,17},{17,1},{2,18},{18,2},{3,19},{19,3},{4,20},{20... | collective-permute-start | bytes 884744 | tf_op jit(solution)/shard_map/ppermute | solution.py:985
  70.2 3.2 %input_one_grad.1 = (f32[2,256,256]{2,1,0:T(8,128)}, f32[2,256]{1,0:T(2,128)S(1)}, f32[8,128]{1,0:T(8,128)S(1)}) custom-call(s32[5]{0:T(128)S(1)} %stack.23.refs_0_, bf16[2064,256]{1,0:T(8,128)(2,1)S(1)} %get-tuple-element.205.refs_2_.refs_1_, bf16[2064,256]{1,0:T(8,128)(2,1)S(1)} %collective-permute-done.11.refs_3_.refs_2_, ...), custom_call_target="tpu_custom_call" | custom-call | flops 1024 | bytes 1024 | tf_op jit(solution)/shard_map/input_one_grad/pallas_call | solution.py:944
  73.4 3.1 %rgb_kernel.1 = (f32[2,3,32,32]{3,2,1,0:T(8,128)}, f32[2,3,16,16]{3,2,1,0:T(8,128)}, f32[8,128]{1,0:T(8,128)S(1)}, f32[8,128]{1,0:T(8,128)S(1)}) custom-call(f32[2,256]{1,0:T(2,128)S(1)} %broadcast_in_dim.2.refs_1_.refs_7_.refs_3_.refs_2_.refs_0_.refs_17_, f32[1,3]{1,0:T(1,128)} %bitcast.44, f32[2,4,8,256]{3,2,1,0:T(8,128)S(1)} %get-tuple-element.204.refs_2_, ...), custom_call_target="tpu_custom_call" | custom-call | flops 1024 | bytes 1024 | tf_op jit(solution)/shard_map/rgb_kernel/pallas_call | solution.py:944
  76.6 3.3 %style_grads_kernel.1 = (f32[16,256]{1,0:T(8,128)S(1)}, f32[8,256]{1,0:T(8,128)S(1)}, f32[8,128]{1,0:T(8,128)S(1)}) custom-call(s32[5]{0:T(128)S(1)} %stack.23.refs_0_, bf16[2064,256]{1,0:T(8,128)(2,1)S(1)} %get-tuple-element.205.refs_2_.refs_1_, bf16[2064,256]{1,0:T(8,128)(2,1)S(1)} %collective-permute-done.11.refs_3_.refs_2_, ...), custom_call_target="tpu_custom_call" | custom-call | flops 1024 | bytes 1024 | tf_op jit(solution)/shard_map/style_grads_kernel/pallas_call | solution.py:944
  80.3 1.0 collective-permute-done.20.refs_6_
  81.2 0.8 fold_kernel.6
  82.0 1.7 %collective-permute-start.21 = (bf16[3,64,512]{2,1,0:T(8,128)(2,1)S(1)}, bf16[3,64,512]{2,1,0:T(8,128)(2,1)S(1)}, u32[]{:S(2)}, u32[]{:S(2)}) collective-permute-start(bf16[3,64,512]{2,1,0:T(8,128)(2,1)S(1)} %get-tuple-element.243), channel_id=1, source_target_pairs={{0,4},{4,0},{1,5},{5,1},{2,6},{6,2},{3,7},{7,3},{8,12},{12,8},{9,1... | collective-permute-start | bytes 589832 | tf_op jit(solution)/shard_map/ppermute | solution.py:985
  83.7 1.5 %collective-permute-start.23 = (bf16[3,64,512]{2,1,0:T(8,128)(2,1)S(1)}, bf16[3,64,512]{2,1,0:T(8,128)(2,1)S(1)}, u32[]{:S(2)}, u32[]{:S(2)}) collective-permute-start(bf16[3,64,512]{2,1,0:T(8,128)(2,1)S(1)} %get-tuple-element.247), channel_id=1, source_target_pairs={{0,2},{2,0},{1,3},{3,1},{4,6},{6,4},{5,7},{7,5},{8,10},{10,8},{9,1... | collective-permute-start | bytes 589832 | tf_op jit(solution)/shard_map/ppermute | solution.py:985
  85.2 0.7 total_kernel.2
  85.9 1.1 collective-permute-start.30
  87.0 1.5 %collective-permute-start.31 = (bf16[3,32,512]{2,1,0:T(8,128)(2,1)S(1)}, bf16[3,32,512]{2,1,0:T(8,128)(2,1)S(1)}, u32[]{:S(2)}, u32[]{:S(2)}) collective-permute-start(bf16[3,32,512]{2,1,0:T(8,128)(2,1)S(1)} %get-tuple-element.260.refs_5_), channel_id=1, source_target_pairs={{0,4},{4,0},{1,5},{5,1},{2,6},{6,2},{3,7},{7,3},{8,12},{12,8},{9,1... | collective-permute-start | bytes 294920 | tf_op jit(solution)/shard_map/ppermute | solution.py:985
  89.4 0.6 collective-permute-done.23.refs_6_
  90.0 0.7 fold_kernel.7
  90.7 1.5 collective-permute-start.26
  92.2 1.6 %collective-permute-start.27 = (bf16[3,32,512]{2,1,0:T(8,128)(2,1)S(1)}, bf16[3,32,512]{2,1,0:T(8,128)(2,1)S(1)}, u32[]{:S(2)}, u32[]{:S(2)}) collective-permute-start(bf16[3,32,512]{2,1,0:T(8,128)(2,1)S(1)} %get-tuple-element.255), channel_id=1, source_target_pairs={{0,2},{2,0},{1,3},{3,1},{4,6},{6,4},{5,7},{7,5},{8,10},{10,8},{9,1... | collective-permute-start | bytes 294920 | tf_op jit(solution)/shard_map/ppermute | solution.py:985
  95.0 1.0 collective-permute-start.34
  96.5 1.8 %collective-permute-start.33 = (bf16[4,64,512]{2,1,0:T(8,128)(2,1)S(1)}, bf16[4,64,512]{2,1,0:T(8,128)(2,1)S(1)}, u32[]{:S(2)}, u32[]{:S(2)}) collective-permute-start(bf16[4,64,512]{2,1,0:T(8,128)(2,1)S(1)} %get-tuple-element.265.refs_1_), channel_id=1, source_target_pairs={{0,4},{4,0},{1,5},{5,1},{2,6},{6,2},{3,7},{7,3},{8,12},{12,8},{9,1... | collective-permute-start | bytes 786440 | tf_op jit(solution)/shard_map/ppermute | solution.py:985
  98.3 1.1 collective-permute-done.28.refs_6_
  100.1 3.4 %collective-permute-start.37 = (bf16[9,32,512]{2,1,0:T(8,128)(2,1)S(1)}, bf16[9,32,512]{2,1,0:T(8,128)(2,1)S(1)}, u32[]{:S(2)}, u32[]{:S(2)}) collective-permute-start(bf16[9,32,512]{2,1,0:T(8,128)(2,1)S(1)} %get-tuple-element.272.refs_1_), channel_id=1, source_target_pairs={{0,16},{16,0},{1,17},{17,1},{2,18},{18,2},{3,19},{19,3},{4,20},{20... | collective-permute-start | bytes 884744 | tf_op jit(solution)/shard_map/ppermute | solution.py:985
  103.5 0.7 join_kernel.5
  104.2 1.2 collective-permute-start.41
  105.4 1.1 collective-permute-start.42
  106.4 1.3 collective-permute-start.36
  108.3 2.0 %finish_kernel.3 = (f32[9,256,512]{2,1,0:T(8,128)}, f32[8,128]{1,0:T(8,128)S(1)}) custom-call(s32[5]{0:T(128)S(1)} %stack.23.refs_0_, bf16[4,128,512]{2,1,0:T(8,128)(2,1)S(1)} %get-tuple-element.271.refs_1_, bf16[3,128,512]{2,1,0:T(8,128)(2,1)S(1)} %get-tuple-element.273.refs_2_, bf16[3,128,512]{2,1,0:T(8,128)(2,1)S(1)} %get-tuple-element.274.refs_3_, ...), custom_call_target="tpu_custom_call" | custom-call | flops 1024 | bytes 1024 | tf_op jit(solution)/shard_map/finish_kernel/pallas_call | solution.py:944
  110.3 7.2 %collective-permute-done.37.refs_2_ = bf16[9,32,512]{2,1,0:T(8,128)(2,1)S(1)} collective-permute-done((bf16[9,32,512]{2,1,0:T(8,128)(2,1)S(1)}, bf16[9,32,512]{2,1,0:T(8,128)(2,1)S(1)}, u32[]{:S(2)}, u32[]{:S(2)}) %collective-permute-start.37) | collective-permute-done | bytes 294944 | tf_op jit(solution)/shard_map/ppermute | solution.py:985
  117.6 0.6 total_kernel.3
  118.3 1.1 collective-permute-start.39
  119.9 3.5 %collective-permute-done.42.refs_3_ = bf16[3,128,512]{2,1,0:T(8,128)(2,1)S(1)} collective-permute-done((bf16[3,128,512]{2,1,0:T(8,128)(2,1)S(1)}, bf16[3,128,512]{2,1,0:T(8,128)(2,1)S(1)}, u32[]{:S(2)}, u32[]{:S(2)}) %collective-permute-start.42) | collective-permute-done | bytes 393248 | tf_op jit(solution)/shard_map/ppermute | solution.py:985
  123.3 2.0 %finish_kernel.4 = (f32[9,256,512]{2,1,0:T(8,128)}, f32[8,128]{1,0:T(8,128)S(1)}) custom-call(s32[5]{0:T(128)S(1)} %stack.23.refs_0_, bf16[4,128,512]{2,1,0:T(8,128)(2,1)S(1)} %collective-permute-done.36.refs_1_.refs_2_, bf16[3,128,512]{2,1,0:T(8,128)(2,1)S(1)} %collective-permute-done.41.refs_2_, ...), custom_call_target="tpu_custom_call", output_to_operand_aliasing={{0}: (4, {})} | custom-call | flops 1024 | bytes 1024 | tf_op jit(solution)/shard_map/finish_kernel/pallas_call | solution.py:944
  126.0 1.2 collective-permute-start.43
  127.2 1.3 collective-permute-start.45
  128.5 3.1 %spread_kernel.1 = (f32[512,256]{1,0:T(8,128)}, f32[512,256]{1,0:T(8,128)}, f32[512,256]{1,0:T(8,128)}, f32[1,256]{1,0:T(1,128)}, f32[1,256]{1,0:T(1,128)}, /*in...) custom-call(s32[5]{0:T(128)S(1)} %stack.23.refs_0_, ...), custom_call_target="tpu_custom_call" | custom-call | flops 1024 | bytes 1024 | tf_op jit(solution)/shard_map/spread_kernel/pallas_call | solution.py:944
  131.8 1.1 collective-permute-done.44.refs_4_
  132.9 0.6 join_kernel.7
  133.6 1.4 collective-permute-start.46
  134.9 1.1 collective-permute-start.47
  136.1 0.8 collective-permute-start.48
  136.9 2.0 %finish_kernel.5 = (f32[9,256,512]{2,1,0:T(8,128)}, f32[8,128]{1,0:T(8,128)S(1)}) custom-call(s32[5]{0:T(128)S(1)} %stack.23.refs_0_, bf16[3,128,512]{2,1,0:T(8,128)(2,1)S(1)} %get-tuple-element.294.refs_1_, bf16[3,128,512]{2,1,0:T(8,128)(2,1)S(1)} %get-tuple-element.295.refs_2_, bf16[3,128,512]{2,1,0:T(8,128)(2,1)S(1)} %get-tuple-element.296.refs_3_, ...), custom_call_target="tpu_custom_call" | custom-call | flops 1024 | bytes 1024 | tf_op jit(solution)/shard_map/finish_kernel/pallas_call | solution.py:944
  139.0 2.7 %collective-permute-done.46.refs_1_ = bf16[3,128,512]{2,1,0:T(8,128)(2,1)S(1)} collective-permute-done((bf16[3,128,512]{2,1,0:T(8,128)(2,1)S(1)}, bf16[3,128,512]{2,1,0:T(8,128)(2,1)S(1)}, u32[]{:S(2)}, u32[]{:S(2)}) %collective-permute-start.46) | collective-permute-done | bytes 393248 | tf_op jit(solution)/shard_map/ppermute | solution.py:985
  141.7 1.1 collective-permute-done.47.refs_2_
  142.8 1.1 collective-permute-done.48.refs_3_
  143.8 2.6 %finish_scalars_kernel.1 = (f32[9,256,512]{2,1,0:T(8,128)}, f32[2]{0:T(128)}, f32[3]{0:T(128)}, f32[3]{0:T(128)}, f32[8,128]{1,0:T(8,128)}) custom-call(s32[5]{0:T(128)S(1)} %stack.23.refs_0_, bf16[3,128,512]{2,1,0:T(8,128)(2,1)S(1)} %collective-permute-done.46.refs_1_, ...), custom_call_target="tpu_custom_call", output_to_operand_aliasing={{0}: (4, {})} | custom-call | flops 1024 | bytes 1024 | tf_op jit(solution)/shard_map/finish_scalars_kernel/pallas_call | solution.py:944
  (84 shorter events, 12.1 us)
Async XLA Ops:
  0.7 3.4 %copy-start.1 = (bf16[3,3,256,512]{3,2,1,0:T(8,128)(2,1)S(1)}, bf16[3,3,256,512]{3,2,1,0:T(8,128)(2,1)}, u32[]{:S(2)}) copy-start(bf16[3,3,256,512]{3,2,1,0:T(8,128)(2,1)} %param.31) | copy-start | bytes 7077892
  3.5 6.6 %collective-permute-start.1 = (bf16[9,256,256]{2,1,0:T(8,128)(2,1)S(1)}, bf16[9,256,256]{2,1,0:T(8,128)(2,1)S(1)}, u32[]{:S(2)}, u32[]{:S(2)}) collective-permute-start(bf16[9,256,256]{2,1,0:T(8,128)(2,1)S(1)} %get-tuple-element.165), channel_id=1, source_target_pairs={{0,1},{1,0},{2,3},{3,2},{4,5},{5,4},{6,7},{7,6},{8,9},{9,8},{10,11... | collective-permute-start | bytes 3538952 | tf_op jit(solution)/shard_map/ppermute | solution.py:985
  4.0 6.1 %collective-permute-start = (bf16[2,256,256]{2,1,0:T(8,128)(2,1)S(1)}, bf16[2,256,256]{2,1,0:T(8,128)(2,1)S(1)}, u32[]{:S(2)}, u32[]{:S(2)}) collective-permute-start(bf16[2,256,256]{2,1,0:T(8,128)(2,1)S(1)} %get-tuple-element.164.refs_1_), channel_id=1, source_target_pairs={{0,1},{1,0},{2,3},{3,2},{4,5},{5,4},{6,7},{7,6},{8,9},{9,8},{10,11... | collective-permute-start | bytes 786440 | tf_op jit(solution)/shard_map/ppermute | solution.py:985
  6.1 4.0 %collective-permute-start.2 = (f32[2,256]{1,0:T(2,128)S(1)}, f32[2,256]{1,0:T(2,128)S(1)}, u32[]{:S(2)}, u32[]{:S(2)}) collective-permute-start(f32[2,256]{1,0:T(2,128)S(1)} %get-tuple-element.169), channel_id=1, source_target_pairs={{0,1},{1,0},{2,3},{3,2},{4,5},{5,4},{6,7},{7,6},{8,9},{9,8},{10,11... | collective-permute-start | bytes 6152 | tf_op jit(solution)/shard_map/ppermute | solution.py:985
  9.9 5.1 %collective-permute-start.4 = (bf16[9,256,256]{2,1,0:T(8,128)(2,1)S(1)}, bf16[9,256,256]{2,1,0:T(8,128)(2,1)S(1)}, u32[]{:S(2)}, u32[]{:S(2)}) collective-permute-start(bf16[9,256,256]{2,1,0:T(8,128)(2,1)S(1)} %get-tuple-element.175), channel_id=1, source_target_pairs={{0,1},{1,0},{2,3},{3,2},{4,5},{5,4},{6,7},{7,6},{8,9},{9,8},{10,11... | collective-permute-start | bytes 3538952 | tf_op jit(solution)/shard_map/ppermute | solution.py:985
  10.1 3.3 %copy-start = (bf16[3,3,256,512]{3,2,1,0:T(8,128)(2,1)S(1)}, bf16[3,3,256,512]{3,2,1,0:T(8,128)(2,1)}, u32[]{:S(2)}) copy-start(bf16[3,3,256,512]{3,2,1,0:T(8,128)(2,1)} %param.33) | copy-start | bytes 7077892
  12.9 3.2 %copy-start.2 = (bf16[2,32,32,256]{3,2,1,0:T(8,128)(2,1)S(1)}, bf16[2,32,32,256]{3,2,1,0:T(8,128)(2,1)}, u32[]{:S(2)}) copy-start(bf16[2,32,32,256]{3,2,1,0:T(8,128)(2,1)} %refs_6_.3) | copy-start | bytes 3145732
  12.9 3.2 %collective-permute-start.3 = (bf16[2,4,256,256]{3,2,1,0:T(8,128)(2,1)S(1)}, bf16[2,4,256,256]{3,2,1,0:T(8,128)(2,1)S(1)}, u32[]{:S(2)}, u32[]{:S(2)}) collective-permute-start(bf16[2,4,256,256]{3,2,1,0:T(8,128)(2,1)S(1)} %get-tuple-element.174.refs_1_.refs_0_), channel_id=1, source_target_pairs={{0,1},{1,0},{2,3},{3,2},{4,5},{5,4},{6,7},{7,6},{8,9},{9,8},{10,11... | collective-permute-start | bytes 3145736 | tf_op jit(solution)/shard_map/ppermute | solution.py:985
  14.9 1.2 collective-permute-start.5
  23.1 2.7 %collective-permute-start.6 = (bf16[2064,256]{1,0:T(8,128)(2,1)S(1)}, bf16[2064,256]{1,0:T(8,128)(2,1)S(1)}, u32[]{:S(2)}, u32[]{:S(2)}) collective-permute-start(bf16[2064,256]{1,0:T(8,128)(2,1)S(1)} %get-tuple-element.188.refs_3_.refs_1_), channel_id=1, source_target_pairs={{0,1},{1,0},{2,3},{3,2},{4,5},{5,4},{6,7},{7,6},{8,9},{9,8},{10,11... | collective-permute-start | bytes 3170312 | tf_op jit(solution)/shard_map/ppermute | solution.py:985
  32.3 14.6 %collective-permute-start.7 = (bf16[3,128,512]{2,1,0:T(8,128)(2,1)S(1)}, bf16[3,128,512]{2,1,0:T(8,128)(2,1)S(1)}, u32[]{:S(2)}, u32[]{:S(2)}) collective-permute-start(bf16[3,128,512]{2,1,0:T(8,128)(2,1)S(1)} %get-tuple-element.191), channel_id=1, source_target_pairs={{0,2},{2,0},{1,3},{3,1},{4,6},{6,4},{5,7},{7,5},{8,10},{10,8},{9,1... | collective-permute-start | bytes 1179656 | tf_op jit(solution)/shard_map/ppermute | solution.py:985
  35.0 11.9 %collective-permute-start.8 = (bf16[3,128,512]{2,1,0:T(8,128)(2,1)S(1)}, bf16[3,128,512]{2,1,0:T(8,128)(2,1)S(1)}, u32[]{:S(2)}, u32[]{:S(2)}) collective-permute-start(bf16[3,128,512]{2,1,0:T(8,128)(2,1)S(1)} %get-tuple-element.193), channel_id=1, source_target_pairs={{0,4},{4,0},{1,5},{5,1},{2,6},{6,2},{3,7},{7,3},{8,12},{12,8},{9,1... | collective-permute-start | bytes 1179656 | tf_op jit(solution)/shard_map/ppermute | solution.py:985
  36.5 10.8 %collective-permute-start.9 = (bf16[3,128,512]{2,1,0:T(8,128)(2,1)S(1)}, bf16[3,128,512]{2,1,0:T(8,128)(2,1)S(1)}, u32[]{:S(2)}, u32[]{:S(2)}) collective-permute-start(bf16[3,128,512]{2,1,0:T(8,128)(2,1)S(1)} %get-tuple-element.195), channel_id=1, source_target_pairs={{0,8},{8,0},{1,9},{9,1},{2,10},{10,2},{3,11},{11,3},{4,12},{12,4},... | collective-permute-start | bytes 1179656 | tf_op jit(solution)/shard_map/ppermute | solution.py:985
  47.3 3.7 %copy-start.4 = (bf16[3,256]{1,0:T(4,128)(2,1)S(1)}, bf16[3,256]{1,0:T(4,128)(2,1)}, u32[]{:S(2)}) copy-start(bf16[3,256]{1,0:T(4,128)(2,1)} %refs_4_.6) | copy-start | bytes 4612
  48.3 8.8 %collective-permute-start.12 = (bf16[3,64,512]{2,1,0:T(8,128)(2,1)S(1)}, bf16[3,64,512]{2,1,0:T(8,128)(2,1)S(1)}, u32[]{:S(2)}, u32[]{:S(2)}) collective-permute-start(bf16[3,64,512]{2,1,0:T(8,128)(2,1)S(1)} %get-tuple-element.207), channel_id=1, source_target_pairs={{0,4},{4,0},{1,5},{5,1},{2,6},{6,2},{3,7},{7,3},{8,12},{12,8},{9,1... | collective-permute-start | bytes 589832 | tf_op jit(solution)/shard_map/ppermute | solution.py:985
  48.9 8.3 %collective-permute-start.13 = (bf16[3,64,512]{2,1,0:T(8,128)(2,1)S(1)}, bf16[3,64,512]{2,1,0:T(8,128)(2,1)S(1)}, u32[]{:S(2)}, u32[]{:S(2)}) collective-permute-start(bf16[3,64,512]{2,1,0:T(8,128)(2,1)S(1)} %get-tuple-element.209), channel_id=1, source_target_pairs={{0,8},{8,0},{1,9},{9,1},{2,10},{10,2},{3,11},{11,3},{4,12},{12,4},... | collective-permute-start | bytes 589832 | tf_op jit(solution)/shard_map/ppermute | solution.py:985
  50.4 6.7 %collective-permute-start.14 = (bf16[3,64,512]{2,1,0:T(8,128)(2,1)S(1)}, bf16[3,64,512]{2,1,0:T(8,128)(2,1)S(1)}, u32[]{:S(2)}, u32[]{:S(2)}) collective-permute-start(bf16[3,64,512]{2,1,0:T(8,128)(2,1)S(1)} %get-tuple-element.211), channel_id=1, source_target_pairs={{0,2},{2,0},{1,3},{3,1},{4,6},{6,4},{5,7},{7,5},{8,10},{10,8},{9,1... | collective-permute-start | bytes 589832 | tf_op jit(solution)/shard_map/ppermute | solution.py:985
  51.0 10.4 %collective-permute-start.11 = (bf16[2064,256]{1,0:T(8,128)(2,1)S(1)}, bf16[2064,256]{1,0:T(8,128)(2,1)S(1)}, u32[]{:S(2)}, u32[]{:S(2)}) collective-permute-start(bf16[2064,256]{1,0:T(8,128)(2,1)S(1)} %get-tuple-element.205.refs_2_.refs_1_), channel_id=1, source_target_pairs={{0,1},{1,0},{2,3},{3,2},{4,5},{5,4},{6,7},{7,6},{8,9},{9,8},{10,11... | collective-permute-start | bytes 3170312 | tf_op jit(solution)/shard_map/ppermute | solution.py:985
  56.7 4.8 %collective-permute-start.10 = (f32[2,4,8,256]{3,2,1,0:T(8,128)S(1)}, f32[2,4,8,256]{3,2,1,0:T(8,128)S(1)}, u32[]{:S(2)}, u32[]{:S(2)}) collective-permute-start(f32[2,4,8,256]{3,2,1,0:T(8,128)S(1)} %get-tuple-element.204.refs_2_), channel_id=1, source_target_pairs={{0,1},{1,0},{2,3},{3,2},{4,5},{5,4},{6,7},{7,6},{8,9},{9,8},{10,11... | collective-permute-start | bytes 196616 | tf_op jit(solution)/shard_map/ppermute | solution.py:985
  57.9 7.3 %collective-permute-start.15 = (bf16[3,32,512]{2,1,0:T(8,128)(2,1)S(1)}, bf16[3,32,512]{2,1,0:T(8,128)(2,1)S(1)}, u32[]{:S(2)}, u32[]{:S(2)}) collective-permute-start(bf16[3,32,512]{2,1,0:T(8,128)(2,1)S(1)} %get-tuple-element.214), channel_id=1, source_target_pairs={{0,8},{8,0},{1,9},{9,1},{2,10},{10,2},{3,11},{11,3},{4,12},{12,4},... | collective-permute-start | bytes 294920 | tf_op jit(solution)/shard_map/ppermute | solution.py:985
  58.2 8.7 %collective-permute-start.16 = (bf16[3,32,512]{2,1,0:T(8,128)(2,1)S(1)}, bf16[3,32,512]{2,1,0:T(8,128)(2,1)S(1)}, u32[]{:S(2)}, u32[]{:S(2)}) collective-permute-start(bf16[3,32,512]{2,1,0:T(8,128)(2,1)S(1)} %get-tuple-element.216), channel_id=1, source_target_pairs={{0,2},{2,0},{1,3},{3,1},{4,6},{6,4},{5,7},{7,5},{8,10},{10,8},{9,1... | collective-permute-start | bytes 294920 | tf_op jit(solution)/shard_map/ppermute | solution.py:985
  59.9 7.1 %collective-permute-start.17 = (bf16[3,32,512]{2,1,0:T(8,128)(2,1)S(1)}, bf16[3,32,512]{2,1,0:T(8,128)(2,1)S(1)}, u32[]{:S(2)}, u32[]{:S(2)}) collective-permute-start(bf16[3,32,512]{2,1,0:T(8,128)(2,1)S(1)} %get-tuple-element.218), channel_id=1, source_target_pairs={{0,4},{4,0},{1,5},{5,1},{2,6},{6,2},{3,7},{7,3},{8,12},{12,8},{9,1... | collective-permute-start | bytes 294920 | tf_op jit(solution)/shard_map/ppermute | solution.py:985
  64.3 16.0 %collective-permute-start.18 = (bf16[3,128,512]{2,1,0:T(8,128)(2,1)S(1)}, bf16[3,128,512]{2,1,0:T(8,128)(2,1)S(1)}, u32[]{:S(2)}, u32[]{:S(2)}) collective-permute-start(bf16[3,128,512]{2,1,0:T(8,128)(2,1)S(1)} %get-tuple-element.236), channel_id=1, source_target_pairs={{0,2},{2,0},{1,3},{3,1},{4,6},{6,4},{5,7},{7,5},{8,10},{10,8},{9,1... | collective-permute-start | bytes 1179656 | tf_op jit(solution)/shard_map/ppermute | solution.py:985
  64.9 15.4 %collective-permute-start.19 = (bf16[3,128,512]{2,1,0:T(8,128)(2,1)S(1)}, bf16[3,128,512]{2,1,0:T(8,128)(2,1)S(1)}, u32[]{:S(2)}, u32[]{:S(2)}) collective-permute-start(bf16[3,128,512]{2,1,0:T(8,128)(2,1)S(1)} %get-tuple-element.238), channel_id=1, source_target_pairs={{0,4},{4,0},{1,5},{5,1},{2,6},{6,2},{3,7},{7,3},{8,12},{12,8},{9,1... | collective-permute-start | bytes 1179656 | tf_op jit(solution)/shard_map/ppermute | solution.py:985
  65.2 16.0 %collective-permute-start.20 = (bf16[3,128,512]{2,1,0:T(8,128)(2,1)S(1)}, bf16[3,128,512]{2,1,0:T(8,128)(2,1)S(1)}, u32[]{:S(2)}, u32[]{:S(2)}) collective-permute-start(bf16[3,128,512]{2,1,0:T(8,128)(2,1)S(1)} %get-tuple-element.240), channel_id=1, source_target_pairs={{0,8},{8,0},{1,9},{9,1},{2,10},{10,2},{3,11},{11,3},{4,12},{12,4},... | collective-permute-start | bytes 1179656 | tf_op jit(solution)/shard_map/ppermute | solution.py:985
  67.6 17.6 %collective-permute-start.24 = (bf16[9,32,512]{2,1,0:T(8,128)(2,1)S(1)}, bf16[9,32,512]{2,1,0:T(8,128)(2,1)S(1)}, u32[]{:S(2)}, u32[]{:S(2)}) collective-permute-start(bf16[9,32,512]{2,1,0:T(8,128)(2,1)S(1)} %get-tuple-element.248.refs_1_), channel_id=1, source_target_pairs={{0,16},{16,0},{1,17},{17,1},{2,18},{18,2},{3,19},{19,3},{4,20},{20... | collective-permute-start | bytes 884744 | tf_op jit(solution)/shard_map/ppermute | solution.py:985
  70.2 6.3 %copy-start.3 = (bf16[2,512]{1,0:T(2,128)(2,1)S(1)}, bf16[2,512]{1,0:T(2,128)(2,1)}, u32[]{:S(2)}) copy-start(bf16[2,512]{1,0:T(2,128)(2,1)} %refs_14_.1) | copy-start | bytes 6148
  79.9 5.3 %collective-permute-start.25 = (f32[16,256]{1,0:T(8,128)S(1)}, f32[16,256]{1,0:T(8,128)S(1)}, u32[]{:S(2)}, u32[]{:S(2)}) collective-permute-start(f32[16,256]{1,0:T(8,128)S(1)} %get-tuple-element.249.refs_3_), channel_id=1, source_target_pairs={{0,16},{16,0},{1,17},{17,1},{2,18},{18,2},{3,19},{19,3},{4,20},{20... | collective-permute-start | bytes 49160 | tf_op jit(solution)/shard_map/ppermute | solution.py:985
  82.0 6.5 %collective-permute-start.21 = (bf16[3,64,512]{2,1,0:T(8,128)(2,1)S(1)}, bf16[3,64,512]{2,1,0:T(8,128)(2,1)S(1)}, u32[]{:S(2)}, u32[]{:S(2)}) collective-permute-start(bf16[3,64,512]{2,1,0:T(8,128)(2,1)S(1)} %get-tuple-element.243), channel_id=1, source_target_pairs={{0,4},{4,0},{1,5},{5,1},{2,6},{6,2},{3,7},{7,3},{8,12},{12,8},{9,1... | collective-permute-start | bytes 589832 | tf_op jit(solution)/shard_map/ppermute | solution.py:985
  83.7 5.7 %collective-permute-start.22 = (bf16[3,64,512]{2,1,0:T(8,128)(2,1)S(1)}, bf16[3,64,512]{2,1,0:T(8,128)(2,1)S(1)}, u32[]{:S(2)}, u32[]{:S(2)}) collective-permute-start(bf16[3,64,512]{2,1,0:T(8,128)(2,1)S(1)} %get-tuple-element.245), channel_id=1, source_target_pairs={{0,8},{8,0},{1,9},{9,1},{2,10},{10,2},{3,11},{11,3},{4,12},{12,4},... | collective-permute-start | bytes 589832 | tf_op jit(solution)/shard_map/ppermute | solution.py:985
  83.7 6.3 %collective-permute-start.23 = (bf16[3,64,512]{2,1,0:T(8,128)(2,1)S(1)}, bf16[3,64,512]{2,1,0:T(8,128)(2,1)S(1)}, u32[]{:S(2)}, u32[]{:S(2)}) collective-permute-start(bf16[3,64,512]{2,1,0:T(8,128)(2,1)S(1)} %get-tuple-element.247), channel_id=1, source_target_pairs={{0,2},{2,0},{1,3},{3,1},{4,6},{6,4},{5,7},{7,5},{8,10},{10,8},{9,1... | collective-permute-start | bytes 589832 | tf_op jit(solution)/shard_map/ppermute | solution.py:985
  85.9 7.9 %collective-permute-start.30 = (bf16[3,32,512]{2,1,0:T(8,128)(2,1)S(1)}, bf16[3,32,512]{2,1,0:T(8,128)(2,1)S(1)}, u32[]{:S(2)}, u32[]{:S(2)}) collective-permute-start(bf16[3,32,512]{2,1,0:T(8,128)(2,1)S(1)} %get-tuple-element.259.refs_3_), channel_id=1, source_target_pairs={{0,2},{2,0},{1,3},{3,1},{4,6},{6,4},{5,7},{7,5},{8,10},{10,8},{9,1... | collective-permute-start | bytes 294920 | tf_op jit(solution)/shard_map/ppermute | solution.py:985
  87.0 7.4 %collective-permute-start.31 = (bf16[3,32,512]{2,1,0:T(8,128)(2,1)S(1)}, bf16[3,32,512]{2,1,0:T(8,128)(2,1)S(1)}, u32[]{:S(2)}, u32[]{:S(2)}) collective-permute-start(bf16[3,32,512]{2,1,0:T(8,128)(2,1)S(1)} %get-tuple-element.260.refs_5_), channel_id=1, source_target_pairs={{0,4},{4,0},{1,5},{5,1},{2,6},{6,2},{3,7},{7,3},{8,12},{12,8},{9,1... | collective-permute-start | bytes 294920 | tf_op jit(solution)/shard_map/ppermute | solution.py:985
  88.5 5.8 %collective-permute-start.29 = (bf16[4,32,512]{2,1,0:T(8,128)(2,1)S(1)}, bf16[4,32,512]{2,1,0:T(8,128)(2,1)S(1)}, u32[]{:S(2)}, u32[]{:S(2)}) collective-permute-start(bf16[4,32,512]{2,1,0:T(8,128)(2,1)S(1)} %get-tuple-element.258.refs_1_), channel_id=1, source_target_pairs={{0,8},{8,0},{1,9},{9,1},{2,10},{10,2},{3,11},{11,3},{4,12},{12,4},... | collective-permute-start | bytes 393224 | tf_op jit(solution)/shard_map/ppermute | solution.py:985
  90.7 5.7 %collective-permute-start.26 = (bf16[3,32,512]{2,1,0:T(8,128)(2,1)S(1)}, bf16[3,32,512]{2,1,0:T(8,128)(2,1)S(1)}, u32[]{:S(2)}, u32[]{:S(2)}) collective-permute-start(bf16[3,32,512]{2,1,0:T(8,128)(2,1)S(1)} %get-tuple-element.253), channel_id=1, source_target_pairs={{0,8},{8,0},{1,9},{9,1},{2,10},{10,2},{3,11},{11,3},{4,12},{12,4},... | collective-permute-start | bytes 294920 | tf_op jit(solution)/shard_map/ppermute | solution.py:985
  92.2 6.1 %collective-permute-start.27 = (bf16[3,32,512]{2,1,0:T(8,128)(2,1)S(1)}, bf16[3,32,512]{2,1,0:T(8,128)(2,1)S(1)}, u32[]{:S(2)}, u32[]{:S(2)}) collective-permute-start(bf16[3,32,512]{2,1,0:T(8,128)(2,1)S(1)} %get-tuple-element.255), channel_id=1, source_target_pairs={{0,2},{2,0},{1,3},{3,1},{4,6},{6,4},{5,7},{7,5},{8,10},{10,8},{9,1... | collective-permute-start | bytes 294920 | tf_op jit(solution)/shard_map/ppermute | solution.py:985
  93.8 5.6 %collective-permute-start.28 = (bf16[3,32,512]{2,1,0:T(8,128)(2,1)S(1)}, bf16[3,32,512]{2,1,0:T(8,128)(2,1)S(1)}, u32[]{:S(2)}, u32[]{:S(2)}) collective-permute-start(bf16[3,32,512]{2,1,0:T(8,128)(2,1)S(1)} %get-tuple-element.257), channel_id=1, source_target_pairs={{0,4},{4,0},{1,5},{5,1},{2,6},{6,2},{3,7},{7,3},{8,12},{12,8},{9,1... | collective-permute-start | bytes 294920 | tf_op jit(solution)/shard_map/ppermute | solution.py:985
  95.0 8.6 %collective-permute-start.34 = (bf16[3,64,512]{2,1,0:T(8,128)(2,1)S(1)}, bf16[3,64,512]{2,1,0:T(8,128)(2,1)S(1)}, u32[]{:S(2)}, u32[]{:S(2)}) collective-permute-start(bf16[3,64,512]{2,1,0:T(8,128)(2,1)S(1)} %get-tuple-element.266.refs_3_), channel_id=1, source_target_pairs={{0,8},{8,0},{1,9},{9,1},{2,10},{10,2},{3,11},{11,3},{4,12},{12,4},... | collective-permute-start | bytes 589832 | tf_op jit(solution)/shard_map/ppermute | solution.py:985
  95.9 7.6 %collective-permute-start.35 = (bf16[3,64,512]{2,1,0:T(8,128)(2,1)S(1)}, bf16[3,64,512]{2,1,0:T(8,128)(2,1)S(1)}, u32[]{:S(2)}, u32[]{:S(2)}) collective-permute-start(bf16[3,64,512]{2,1,0:T(8,128)(2,1)S(1)} %get-tuple-element.267.refs_5_), channel_id=1, source_target_pairs={{0,2},{2,0},{1,3},{3,1},{4,6},{6,4},{5,7},{7,5},{8,10},{10,8},{9,1... | collective-permute-start | bytes 589832 | tf_op jit(solution)/shard_map/ppermute | solution.py:985
  96.5 7.1 %collective-permute-start.33 = (bf16[4,64,512]{2,1,0:T(8,128)(2,1)S(1)}, bf16[4,64,512]{2,1,0:T(8,128)(2,1)S(1)}, u32[]{:S(2)}, u32[]{:S(2)}) collective-permute-start(bf16[4,64,512]{2,1,0:T(8,128)(2,1)S(1)} %get-tuple-element.265.refs_1_), channel_id=1, source_target_pairs={{0,4},{4,0},{1,5},{5,1},{2,6},{6,2},{3,7},{7,3},{8,12},{12,8},{9,1... | collective-permute-start | bytes 786440 | tf_op jit(solution)/shard_map/ppermute | solution.py:985
  100.0 7.7 %collective-permute-start.32 = (f32[8,256]{1,0:T(8,128)S(1)}, f32[8,256]{1,0:T(8,128)S(1)}, u32[]{:S(2)}, u32[]{:S(2)}) collective-permute-start(f32[8,256]{1,0:T(8,128)S(1)} %get-tuple-element.264), channel_id=1, source_target_pairs={{0,1},{1,0},{2,3},{3,2},{4,5},{5,4},{6,7},{7,6},{8,9},{9,8},{10,11... | collective-permute-start | bytes 24584 | tf_op jit(solution)/shard_map/ppermute | solution.py:985
  100.1 17.5 %collective-permute-start.37 = (bf16[9,32,512]{2,1,0:T(8,128)(2,1)S(1)}, bf16[9,32,512]{2,1,0:T(8,128)(2,1)S(1)}, u32[]{:S(2)}, u32[]{:S(2)}) collective-permute-start(bf16[9,32,512]{2,1,0:T(8,128)(2,1)S(1)} %get-tuple-element.272.refs_1_), channel_id=1, source_target_pairs={{0,16},{16,0},{1,17},{17,1},{2,18},{18,2},{3,19},{19,3},{4,20},{20... | collective-permute-start | bytes 884744 | tf_op jit(solution)/shard_map/ppermute | solution.py:985
  104.2 15.2 %collective-permute-start.41 = (bf16[3,128,512]{2,1,0:T(8,128)(2,1)S(1)}, bf16[3,128,512]{2,1,0:T(8,128)(2,1)S(1)}, u32[]{:S(2)}, u32[]{:S(2)}) collective-permute-start(bf16[3,128,512]{2,1,0:T(8,128)(2,1)S(1)} %get-tuple-element.273.refs_2_), channel_id=1, source_target_pairs={{0,4},{4,0},{1,5},{5,1},{2,6},{6,2},{3,7},{7,3},{8,12},{12,8},{9,1... | collective-permute-start | bytes 1179656 | tf_op jit(solution)/shard_map/ppermute | solution.py:985
  105.4 18.0 %collective-permute-start.42 = (bf16[3,128,512]{2,1,0:T(8,128)(2,1)S(1)}, bf16[3,128,512]{2,1,0:T(8,128)(2,1)S(1)}, u32[]{:S(2)}, u32[]{:S(2)}) collective-permute-start(bf16[3,128,512]{2,1,0:T(8,128)(2,1)S(1)} %get-tuple-element.274.refs_3_), channel_id=1, source_target_pairs={{0,8},{8,0},{1,9},{9,1},{2,10},{10,2},{3,11},{11,3},{4,12},{12,4},... | collective-permute-start | bytes 1179656 | tf_op jit(solution)/shard_map/ppermute | solution.py:985
  106.4 16.9 %collective-permute-start.36 = (bf16[4,128,512]{2,1,0:T(8,128)(2,1)S(1)}, bf16[4,128,512]{2,1,0:T(8,128)(2,1)S(1)}, u32[]{:S(2)}, u32[]{:S(2)}) collective-permute-start(bf16[4,128,512]{2,1,0:T(8,128)(2,1)S(1)} %get-tuple-element.271.refs_1_), channel_id=1, source_target_pairs={{0,2},{2,0},{1,3},{3,1},{4,6},{6,4},{5,7},{7,5},{8,10},{10,8},{9,1... | collective-permute-start | bytes 1572872 | tf_op jit(solution)/shard_map/ppermute | solution.py:985
  118.2 7.2 %collective-permute-start.38 = (bf16[3,32,512]{2,1,0:T(8,128)(2,1)S(1)}, bf16[3,32,512]{2,1,0:T(8,128)(2,1)S(1)}, u32[]{:S(2)}, u32[]{:S(2)}) collective-permute-start(bf16[3,32,512]{2,1,0:T(8,128)(2,1)S(1)} %get-tuple-element.277.refs_1_), channel_id=1, source_target_pairs={{0,8},{8,0},{1,9},{9,1},{2,10},{10,2},{3,11},{11,3},{4,12},{12,4},... | collective-permute-start | bytes 294920 | tf_op jit(solution)/shard_map/ppermute | solution.py:985
  118.3 7.1 %collective-permute-start.39 = (bf16[3,32,512]{2,1,0:T(8,128)(2,1)S(1)}, bf16[3,32,512]{2,1,0:T(8,128)(2,1)S(1)}, u32[]{:S(2)}, u32[]{:S(2)}) collective-permute-start(bf16[3,32,512]{2,1,0:T(8,128)(2,1)S(1)} %get-tuple-element.278.refs_3_), channel_id=1, source_target_pairs={{0,2},{2,0},{1,3},{3,1},{4,6},{6,4},{5,7},{7,5},{8,10},{10,8},{9,1... | collective-permute-start | bytes 294920 | tf_op jit(solution)/shard_map/ppermute | solution.py:985
  119.4 6.0 %collective-permute-start.40 = (bf16[3,32,512]{2,1,0:T(8,128)(2,1)S(1)}, bf16[3,32,512]{2,1,0:T(8,128)(2,1)S(1)}, u32[]{:S(2)}, u32[]{:S(2)}) collective-permute-start(bf16[3,32,512]{2,1,0:T(8,128)(2,1)S(1)} %get-tuple-element.279.refs_5_), channel_id=1, source_target_pairs={{0,4},{4,0},{1,5},{5,1},{2,6},{6,2},{3,7},{7,3},{8,12},{12,8},{9,1... | collective-permute-start | bytes 294920 | tf_op jit(solution)/shard_map/ppermute | solution.py:985
  126.0 5.7 %collective-permute-start.43 = (bf16[3,64,512]{2,1,0:T(8,128)(2,1)S(1)}, bf16[3,64,512]{2,1,0:T(8,128)(2,1)S(1)}, u32[]{:S(2)}, u32[]{:S(2)}) collective-permute-start(bf16[3,64,512]{2,1,0:T(8,128)(2,1)S(1)} %get-tuple-element.290.refs_1_), channel_id=1, source_target_pairs={{0,4},{4,0},{1,5},{5,1},{2,6},{6,2},{3,7},{7,3},{8,12},{12,8},{9,1... | collective-permute-start | bytes 589832 | tf_op jit(solution)/shard_map/ppermute | solution.py:985
  127.2 5.7 %collective-permute-start.44 = (bf16[3,64,512]{2,1,0:T(8,128)(2,1)S(1)}, bf16[3,64,512]{2,1,0:T(8,128)(2,1)S(1)}, u32[]{:S(2)}, u32[]{:S(2)}) collective-permute-start(bf16[3,64,512]{2,1,0:T(8,128)(2,1)S(1)} %get-tuple-element.291.refs_3_), channel_id=1, source_target_pairs={{0,8},{8,0},{1,9},{9,1},{2,10},{10,2},{3,11},{11,3},{4,12},{12,4},... | collective-permute-start | bytes 589832 | tf_op jit(solution)/shard_map/ppermute | solution.py:985
  127.2 5.7 %collective-permute-start.45 = (bf16[3,64,512]{2,1,0:T(8,128)(2,1)S(1)}, bf16[3,64,512]{2,1,0:T(8,128)(2,1)S(1)}, u32[]{:S(2)}, u32[]{:S(2)}) collective-permute-start(bf16[3,64,512]{2,1,0:T(8,128)(2,1)S(1)} %get-tuple-element.292.refs_5_), channel_id=1, source_target_pairs={{0,2},{2,0},{1,3},{3,1},{4,6},{6,4},{5,7},{7,5},{8,10},{10,8},{9,1... | collective-permute-start | bytes 589832 | tf_op jit(solution)/shard_map/ppermute | solution.py:985
  133.6 8.1 %collective-permute-start.46 = (bf16[3,128,512]{2,1,0:T(8,128)(2,1)S(1)}, bf16[3,128,512]{2,1,0:T(8,128)(2,1)S(1)}, u32[]{:S(2)}, u32[]{:S(2)}) collective-permute-start(bf16[3,128,512]{2,1,0:T(8,128)(2,1)S(1)} %get-tuple-element.294.refs_1_), channel_id=1, source_target_pairs={{0,2},{2,0},{1,3},{3,1},{4,6},{6,4},{5,7},{7,5},{8,10},{10,8},{9,1... | collective-permute-start | bytes 1179656 | tf_op jit(solution)/shard_map/ppermute | solution.py:985
  134.9 7.8 %collective-permute-start.47 = (bf16[3,128,512]{2,1,0:T(8,128)(2,1)S(1)}, bf16[3,128,512]{2,1,0:T(8,128)(2,1)S(1)}, u32[]{:S(2)}, u32[]{:S(2)}) collective-permute-start(bf16[3,128,512]{2,1,0:T(8,128)(2,1)S(1)} %get-tuple-element.295.refs_2_), channel_id=1, source_target_pairs={{0,4},{4,0},{1,5},{5,1},{2,6},{6,2},{3,7},{7,3},{8,12},{12,8},{9,1... | collective-permute-start | bytes 1179656 | tf_op jit(solution)/shard_map/ppermute | solution.py:985
  136.1 7.8 %collective-permute-start.48 = (bf16[3,128,512]{2,1,0:T(8,128)(2,1)S(1)}, bf16[3,128,512]{2,1,0:T(8,128)(2,1)S(1)}, u32[]{:S(2)}, u32[]{:S(2)}) collective-permute-start(bf16[3,128,512]{2,1,0:T(8,128)(2,1)S(1)} %get-tuple-element.296.refs_3_), channel_id=1, source_target_pairs={{0,8},{8,0},{1,9},{9,1},{2,10},{10,2},{3,11},{11,3},{4,12},{12,4},... | collective-permute-start | bytes 1179656 | tf_op jit(solution)/shard_map/ppermute | solution.py:985
  136.9 2.0 %collective-permute-start.49 = (f32[1,256]{1,0:T(1,128)S(1)}, f32[1,256]{1,0:T(1,128)S(1)}, u32[]{:S(2)}, u32[]{:S(2)}) collective-permute-start(f32[1,256]{1,0:T(1,128)S(1)} %get-tuple-element.299.refs_5_), channel_id=1, source_target_pairs={{0,1},{1,0},{2,3},{3,2},{4,5},{5,4},{6,7},{7,6},{8,9},{9,8},{10,11... | collective-permute-start | bytes 3080 | tf_op jit(solution)/shard_map/ppermute | solution.py:985

commit v3 on v2

--- a/solution.py
+++ b/solution.py
@@ -1392,8 +1392,9 @@
     )(crossing, crossing_other)
     sum_two, token = reduce_two.finish_own(token)
     token = reduce_one.total(token)
+    _, token = call(relay_kernel, shape(8, share), after=(token, *reduce_two.got))(crossing)
+    token = reduce_one.join(token, 2)
     sum_two, token = reduce_two.finish(token, sum_two)
-    token = reduce_one.join(token, 2)
     if alone:
         packs = [reduce_two.own[0], reduce_two.got[0]]
     else:

time: 147 us -> 147 us (level)
    pallas_call x34 -> x35, Pallas kernels: 73.1 us -> 73.7 us  [run(): pl.pallas_call(inner, out_shape=tuple((member if index in hbm + scalars +...]
  transfers between devices with their start and end apart: 50 -> 50, of which waited for: 15 -> 14; matrix products, arithmetic and copies ran while one was open for 0% -> 0% of each run, Pallas kernels for 35% -> 36%
where the time goes in v3:
time: 147 us
  Pallas kernels  73.7 us (50%)
  starting transfers between devices  48.1 us (33%)
  waiting for transfers between devices  23.2 us (16%)
  between operations  1.83 us (1%)
    pallas_call x35, Pallas kernels, run(): pl.pallas_call(inner, out_shape=tuple((member if index in hbm + scalars +...  73.7 us
    ppermute x50, starting transfers between devices, swap(): return lax.ppermute(values, axis_name, SWAP)  48.1 us
    ppermute x50, waiting for transfers between devices, swap(): return lax.ppermute(values, axis_name, SWAP)  23.2 us
  transfers between devices with their start and end apart: 50, of which 14 were waited for; matrix products, arithmetic and copies ran while one was open for 0% of the time, Pallas kernels for 36%

profile of v3, /device:TPU:0, one launch (start us, length us, event | category | flops | bytes accessed | tf_op | source)
XLA Modules:
  0.0 146.9 jit_solution(18018810918722655106)
XLA Ops:
  0.8 2.7 %style_kernel.1 = (f32[3,2,256]{2,1,0:T(2,128)S(1)}, bf16[2,256,256]{2,1,0:T(8,128)(2,1)S(1)}, bf16[9,256,256]{2,1,0:T(8,128)(2,1)S(1)}, f32[8,128]{1,0:T(8,128)S(1)}) custom-call(s32[5]{0:T(128)S(1)} %stack.23.refs_0_, bf16[9,256,512]{2,1,0:T(8,128)(2,1)} %bitcast.30, bf16[2,512]{1,0:T(2,128)(2,1)} %refs_14_.1, bf16[512,256]{1,0:T(8,128)(2,1)} %refs_11_.1, ...), custom_call_target="tpu_custom_call" | custom-call | flops 1024 | bytes 1024 | tf_op jit(solution)/shard_map/style_kernel/pallas_call | solution.py:944
  4.1 2.0 %squares_kernel.2 = (f32[256,512]{1,0:T(8,128)S(1)}, f32[2,256]{1,0:T(2,128)S(1)}, f32[2,256]{1,0:T(2,128)S(1)}, bf16[16,256]{1,0:T(8,128)(2,1)S(1)}, bf16[2,16,256]{2,1,0:T(8,128)(2,1)}, /*index=5*/f32[8,128]{1,0:T(8,128)S(1)}) custom-call(s32[5]{0:T(128)S(1)} %stack.23.refs_0_, ...), custom_call_target="tpu_custom_call" | custom-call | flops 1024 | bytes 1024 | tf_op jit(solution)/shard_map/squares_kernel/pallas_call | solution.py:944
  7.2 2.7 %planes_kernel.1 = (bf16[2,4,16,256]{3,2,1,0:T(8,128)(2,1)S(1)}, bf16[2,4,16,256]{3,2,1,0:T(8,128)(2,1)S(1)}, bf16[2,4,16,256]{3,2,1,0:T(8,128)(2,1)S(1)}, bf16[9,256,256]{2,1,0:T(8,128)(2,1)S(1)}, f32[8,128]{1,0:T(8,128)S(1)}) custom-call(s32[5]{0:T(128)S(1)} %stack.23.refs_0_, ...), custom_call_target="tpu_custom_call" | custom-call | flops 1024 | bytes 1024 | tf_op jit(solution)/shard_map/planes_kernel/pallas_call | solution.py:944
  10.1 2.8 %conv_one_kernel.1 = (f32[2,4,256,256]{3,2,1,0:T(8,128)S(1)}, bf16[2,4,256,256]{3,2,1,0:T(8,128)(2,1)S(1)}, f32[2,256]{1,0:T(2,128)S(1)}, f32[8,128]{1,0:T(8,128)S(1)}) custom-call(s32[5]{0:T(128)S(1)} %stack.23.refs_0_, bf16[2,256,256]{2,1,0:T(8,128)(2,1)S(1)} %get-tuple-element.165.refs_1_, bf16[2,256,256]{2,1,0:T(8,128)(2,1)S(1)} %collective-permute-done.refs_2_, ...), custom_call_target="tpu_custom_call" | custom-call | flops 66000003072 | bytes 1024 | tf_op jit(solution)/shard_map/conv_one_kernel/pallas_call | solution.py:944
  13.4 1.5 %squares_kernel.3 = (f32[256,512]{1,0:T(8,128)S(1)}, f32[2,256]{1,0:T(2,128)S(1)}, f32[2,256]{1,0:T(2,128)S(1)}, bf16[16,256]{1,0:T(8,128)(2,1)S(1)}, bf16[2,16,...) custom-call(s32[5]{0:T(128)S(1)} %stack.23.refs_0_, ...), custom_call_target="tpu_custom_call" | custom-call | flops 1024 | bytes 1024 | tf_op jit(solution)/shard_map/squares_kernel/pallas_call | solution.py:944
  15.0 1.0 collective-permute-done.5.refs_6_
  16.0 7.1 %conv_two_kernel.1 = (f32[2,4,256,256]{3,2,1,0:T(8,128)S(1)}, bf16[2064,256]{1,0:T(8,128)(2,1)S(1)}, f32[2,256]{1,0:T(2,128)S(1)}, f32[8,128]{1,0:T(8,128)S(1)}) custom-call(s32[5]{0:T(128)S(1)} %stack.23.refs_0_, bf16[2,4,256,256]{3,2,1,0:T(8,128)(2,1)S(1)} %get-tuple-element.175.refs_1_.refs_0_, ...), custom_call_target="tpu_custom_call" | custom-call | flops 1024 | bytes 1024 | tf_op jit(solution)/shard_map/conv_two_kernel/pallas_call | solution.py:944
  23.6 2.2 %collective-permute-done.6.refs_4_.refs_2_ = bf16[2064,256]{1,0:T(8,128)(2,1)S(1)} collective-permute-done((bf16[2064,256]{1,0:T(8,128)(2,1)S(1)}, bf16[2064,256]{1,0:T(8,128)(2,1)S(1)}, u32[]{:S(2)}, u32[]{:S(2)}) %collective-permute-start.6) | collective-permute-done | bytes 1056800 | tf_op jit(solution)/shard_map/ppermute | solution.py:985
  25.8 6.4 %kernel_two_grad.1 = (bf16[3,128,512]{2,1,0:T(8,128)(2,1)S(1)}, f32[3,128,512]{2,1,0:T(8,128)S(1)}, bf16[3,128,512]{2,1,0:T(8,128)(2,1)S(1)}, f32[3,128,512]{2,1...) custom-call(s32[5]{0:T(128)S(1)} %stack.23.refs_0_, ...), custom_call_target="tpu_custom_call" | custom-call | flops 1024 | bytes 1024 | tf_op jit(solution)/shard_map/kernel_two_grad/pallas_call | solution.py:944
  32.3 2.7 %collective-permute-start.7 = (bf16[3,128,512]{2,1,0:T(8,128)(2,1)S(1)}, bf16[3,128,512]{2,1,0:T(8,128)(2,1)S(1)}, u32[]{:S(2)}, u32[]{:S(2)}) collective-permute-start(bf16[3,128,512]{2,1,0:T(8,128)(2,1)S(1)} %get-tuple-element.192), channel_id=1, source_target_pairs={{0,2},{2,0},{1,3},{3,1},{4,6},{6,4},{5,7},{7,5},{8,10},{10,8},{9,1... | collective-permute-start | bytes 1179656 | tf_op jit(solution)/shard_map/ppermute | solution.py:985
  35.0 1.6 %collective-permute-start.8 = (bf16[3,128,512]{2,1,0:T(8,128)(2,1)S(1)}, bf16[3,128,512]{2,1,0:T(8,128)(2,1)S(1)}, u32[]{:S(2)}, u32[]{:S(2)}) collective-permute-start(bf16[3,128,512]{2,1,0:T(8,128)(2,1)S(1)} %get-tuple-element.194), channel_id=1, source_target_pairs={{0,4},{4,0},{1,5},{5,1},{2,6},{6,2},{3,7},{7,3},{8,12},{12,8},{9,1... | collective-permute-start | bytes 1179656 | tf_op jit(solution)/shard_map/ppermute | solution.py:985
  36.5 1.5 %collective-permute-start.9 = (bf16[3,128,512]{2,1,0:T(8,128)(2,1)S(1)}, bf16[3,128,512]{2,1,0:T(8,128)(2,1)S(1)}, u32[]{:S(2)}, u32[]{:S(2)}) collective-permute-start(bf16[3,128,512]{2,1,0:T(8,128)(2,1)S(1)} %get-tuple-element.196), channel_id=1, source_target_pairs={{0,8},{8,0},{1,9},{9,1},{2,10},{10,2},{3,11},{11,3},{4,12},{12,4},... | collective-permute-start | bytes 1179656 | tf_op jit(solution)/shard_map/ppermute | solution.py:985
  38.1 6.4 %input_two_grad.1 = (f32[2,4,256,256]{3,2,1,0:T(8,128)S(1)}, bf16[2064,256]{1,0:T(8,128)(2,1)S(1)}, f32[8,128]{1,0:T(8,128)S(1)}) custom-call(s32[5]{0:T(128)S(1)} %stack.23.refs_0_, bf16[2064,256]{1,0:T(8,128)(2,1)S(1)} %get-tuple-element.189.refs_3_.refs_1_, bf16[2064,256]{1,0:T(8,128)(2,1)S(1)} %collective-permute-done.6.refs_4_.refs_2_, ...), custom_call_target="tpu_custom_call" | custom-call | flops 1024 | bytes 1024 | tf_op jit(solution)/shard_map/input_two_grad/pallas_call | solution.py:944
  44.5 2.3 %outputs_one_kernel.1 = (f32[2,8,256]{2,1,0:T(8,128)S(1)}, f32[8,128]{1,0:T(8,128)S(1)}) custom-call(f32[2,4,256,256]{3,2,1,0:T(8,128)S(1)} %get-tuple-element.197.refs_4_.refs_0_, f32[2,4,256,256]{3,2,1,0:T(8,128)S(1)} %get-tuple-element.200.refs_1_, f32[2,256]{1,0:T(2,128)S(1)} %get-tuple-element.198.refs_5_.refs_2_, ...), custom_call_target="tpu_custom_call" | custom-call | flops 1024 | bytes 1024 | tf_op jit(solution)/shard_map/outputs_one_kernel/pallas_call | solution.py:944
  47.3 1.0 fold_kernel.4
  48.9 1.6 %collective-permute-start.13 = (bf16[3,64,512]{2,1,0:T(8,128)(2,1)S(1)}, bf16[3,64,512]{2,1,0:T(8,128)(2,1)S(1)}, u32[]{:S(2)}, u32[]{:S(2)}) collective-permute-start(bf16[3,64,512]{2,1,0:T(8,128)(2,1)S(1)} %get-tuple-element.210), channel_id=1, source_target_pairs={{0,8},{8,0},{1,9},{9,1},{2,10},{10,2},{3,11},{11,3},{4,12},{12,4},... | collective-permute-start | bytes 589832 | tf_op jit(solution)/shard_map/ppermute | solution.py:985
  51.0 5.7 %outputs_two_kernel.1 = (bf16[2,32,32,256]{3,2,1,0:T(8,128)(2,1)}, f32[2,4,8,256]{3,2,1,0:T(8,128)S(1)}, f32[16,256]{1,0:T(8,128)S(1)}, f32[2,8,256]{2,1,0:T(8,128)S(1)}, f32[8,128]{1,0:T(8,128)S(1)}) custom-call(f32[2,4,256,256]{3,2,1,0:T(8,128)S(1)} %get-tuple-element.185.refs_0_, f32[2,256]{1,0:T(2,128)S(1)} %get-tuple-element.186.refs_1_, ...), custom_call_target="tpu_custom_call" | custom-call | flops 1024 | bytes 1024 | tf_op jit(solution)/shard_map/outputs_two_kernel/pallas_call | solution.py:944
  57.2 0.7 fold_kernel.5
  58.2 1.7 %collective-permute-start.16 = (bf16[3,32,512]{2,1,0:T(8,128)(2,1)S(1)}, bf16[3,32,512]{2,1,0:T(8,128)(2,1)S(1)}, u32[]{:S(2)}, u32[]{:S(2)}) collective-permute-start(bf16[3,32,512]{2,1,0:T(8,128)(2,1)S(1)} %get-tuple-element.217), channel_id=1, source_target_pairs={{0,2},{2,0},{1,3},{3,1},{4,6},{6,4},{5,7},{7,5},{8,10},{10,8},{9,1... | collective-permute-start | bytes 294920 | tf_op jit(solution)/shard_map/ppermute | solution.py:985
  59.9 1.5 %collective-permute-start.17 = (bf16[3,32,512]{2,1,0:T(8,128)(2,1)S(1)}, bf16[3,32,512]{2,1,0:T(8,128)(2,1)S(1)}, u32[]{:S(2)}, u32[]{:S(2)}) collective-permute-start(bf16[3,32,512]{2,1,0:T(8,128)(2,1)S(1)} %get-tuple-element.219), channel_id=1, source_target_pairs={{0,4},{4,0},{1,5},{5,1},{2,6},{6,2},{3,7},{7,3},{8,12},{12,8},{9,1... | collective-permute-start | bytes 294920 | tf_op jit(solution)/shard_map/ppermute | solution.py:985
  61.4 2.8 %kernel_one_grad.1 = (bf16[3,128,512]{2,1,0:T(8,128)(2,1)S(1)}, f32[3,128,512]{2,1,0:T(8,128)S(1)}, bf16[3,128,512]{2,1,0:T(8,128)(2,1)S(1)}, f32[3,128,512]{2,1...) custom-call(s32[5]{0:T(128)S(1)} %stack.23.refs_0_, ...), custom_call_target="tpu_custom_call" | custom-call | flops 66000003072 | bytes 1024 | tf_op jit(solution)/shard_map/kernel_one_grad/pallas_call | solution.py:944
  65.2 1.7 %collective-permute-start.20 = (bf16[3,128,512]{2,1,0:T(8,128)(2,1)S(1)}, bf16[3,128,512]{2,1,0:T(8,128)(2,1)S(1)}, u32[]{:S(2)}, u32[]{:S(2)}) collective-permute-start(bf16[3,128,512]{2,1,0:T(8,128)(2,1)S(1)} %get-tuple-element.241), channel_id=1, source_target_pairs={{0,8},{8,0},{1,9},{9,1},{2,10},{10,2},{3,11},{11,3},{4,12},{12,4},... | collective-permute-start | bytes 1179656 | tf_op jit(solution)/shard_map/ppermute | solution.py:985
  66.9 0.6 across_kernel.2
  67.6 2.7 %collective-permute-start.24 = (bf16[9,32,512]{2,1,0:T(8,128)(2,1)S(1)}, bf16[9,32,512]{2,1,0:T(8,128)(2,1)S(1)}, u32[]{:S(2)}, u32[]{:S(2)}) collective-permute-start(bf16[9,32,512]{2,1,0:T(8,128)(2,1)S(1)} %get-tuple-element.249.refs_1_), channel_id=1, source_target_pairs={{0,16},{16,0},{1,17},{17,1},{2,18},{18,2},{3,19},{19,3},{4,20},{20... | collective-permute-start | bytes 884744 | tf_op jit(solution)/shard_map/ppermute | solution.py:985
  70.2 3.2 %input_one_grad.1 = (f32[2,256,256]{2,1,0:T(8,128)}, f32[2,256]{1,0:T(2,128)S(1)}, f32[8,128]{1,0:T(8,128)S(1)}) custom-call(s32[5]{0:T(128)S(1)} %stack.23.refs_0_, bf16[2064,256]{1,0:T(8,128)(2,1)S(1)} %get-tuple-element.206.refs_2_.refs_1_, bf16[2064,256]{1,0:T(8,128)(2,1)S(1)} %collective-permute-done.11.refs_3_.refs_2_, ...), custom_call_target="tpu_custom_call" | custom-call | flops 1024 | bytes 1024 | tf_op jit(solution)/shard_map/input_one_grad/pallas_call | solution.py:944
  73.4 3.1 %rgb_kernel.1 = (f32[2,3,32,32]{3,2,1,0:T(8,128)}, f32[2,3,16,16]{3,2,1,0:T(8,128)}, f32[8,128]{1,0:T(8,128)S(1)}, f32[8,128]{1,0:T(8,128)S(1)}) custom-call(f32[2,256]{1,0:T(2,128)S(1)} %broadcast_in_dim.2.refs_1_.refs_7_.refs_3_.refs_2_.refs_0_.refs_17_, f32[1,3]{1,0:T(1,128)} %bitcast.44, f32[2,4,8,256]{3,2,1,0:T(8,128)S(1)} %get-tuple-element.205.refs_2_, ...), custom_call_target="tpu_custom_call" | custom-call | flops 1024 | bytes 1024 | tf_op jit(solution)/shard_map/rgb_kernel/pallas_call | solution.py:944
  76.6 3.3 %style_grads_kernel.1 = (f32[16,256]{1,0:T(8,128)S(1)}, f32[8,256]{1,0:T(8,128)S(1)}, f32[8,128]{1,0:T(8,128)S(1)}) custom-call(s32[5]{0:T(128)S(1)} %stack.23.refs_0_, bf16[2064,256]{1,0:T(8,128)(2,1)S(1)} %get-tuple-element.206.refs_2_.refs_1_, bf16[2064,256]{1,0:T(8,128)(2,1)S(1)} %collective-permute-done.11.refs_3_.refs_2_, ...), custom_call_target="tpu_custom_call" | custom-call | flops 1024 | bytes 1024 | tf_op jit(solution)/shard_map/style_grads_kernel/pallas_call | solution.py:944
  80.3 1.0 collective-permute-done.20.refs_6_
  81.2 0.8 fold_kernel.6
  82.0 1.7 %collective-permute-start.21 = (bf16[3,64,512]{2,1,0:T(8,128)(2,1)S(1)}, bf16[3,64,512]{2,1,0:T(8,128)(2,1)S(1)}, u32[]{:S(2)}, u32[]{:S(2)}) collective-permute-start(bf16[3,64,512]{2,1,0:T(8,128)(2,1)S(1)} %get-tuple-element.244), channel_id=1, source_target_pairs={{0,4},{4,0},{1,5},{5,1},{2,6},{6,2},{3,7},{7,3},{8,12},{12,8},{9,1... | collective-permute-start | bytes 589832 | tf_op jit(solution)/shard_map/ppermute | solution.py:985
  83.7 1.5 %collective-permute-start.23 = (bf16[3,64,512]{2,1,0:T(8,128)(2,1)S(1)}, bf16[3,64,512]{2,1,0:T(8,128)(2,1)S(1)}, u32[]{:S(2)}, u32[]{:S(2)}) collective-permute-start(bf16[3,64,512]{2,1,0:T(8,128)(2,1)S(1)} %get-tuple-element.248), channel_id=1, source_target_pairs={{0,2},{2,0},{1,3},{3,1},{4,6},{6,4},{5,7},{7,5},{8,10},{10,8},{9,1... | collective-permute-start | bytes 589832 | tf_op jit(solution)/shard_map/ppermute | solution.py:985
  85.2 0.7 total_kernel.2
  85.9 1.1 collective-permute-start.30
  87.0 1.5 %collective-permute-start.31 = (bf16[3,32,512]{2,1,0:T(8,128)(2,1)S(1)}, bf16[3,32,512]{2,1,0:T(8,128)(2,1)S(1)}, u32[]{:S(2)}, u32[]{:S(2)}) collective-permute-start(bf16[3,32,512]{2,1,0:T(8,128)(2,1)S(1)} %get-tuple-element.261.refs_5_), channel_id=1, source_target_pairs={{0,4},{4,0},{1,5},{5,1},{2,6},{6,2},{3,7},{7,3},{8,12},{12,8},{9,1... | collective-permute-start | bytes 294920 | tf_op jit(solution)/shard_map/ppermute | solution.py:985
  89.4 0.6 collective-permute-done.23.refs_6_
  90.0 0.7 fold_kernel.7
  90.7 1.5 collective-permute-start.26
  92.2 1.6 %collective-permute-start.27 = (bf16[3,32,512]{2,1,0:T(8,128)(2,1)S(1)}, bf16[3,32,512]{2,1,0:T(8,128)(2,1)S(1)}, u32[]{:S(2)}, u32[]{:S(2)}) collective-permute-start(bf16[3,32,512]{2,1,0:T(8,128)(2,1)S(1)} %get-tuple-element.256), channel_id=1, source_target_pairs={{0,2},{2,0},{1,3},{3,1},{4,6},{6,4},{5,7},{7,5},{8,10},{10,8},{9,1... | collective-permute-start | bytes 294920 | tf_op jit(solution)/shard_map/ppermute | solution.py:985
  95.0 1.0 collective-permute-start.34
  96.5 1.8 %collective-permute-start.33 = (bf16[4,64,512]{2,1,0:T(8,128)(2,1)S(1)}, bf16[4,64,512]{2,1,0:T(8,128)(2,1)S(1)}, u32[]{:S(2)}, u32[]{:S(2)}) collective-permute-start(bf16[4,64,512]{2,1,0:T(8,128)(2,1)S(1)} %get-tuple-element.266.refs_1_), channel_id=1, source_target_pairs={{0,4},{4,0},{1,5},{5,1},{2,6},{6,2},{3,7},{7,3},{8,12},{12,8},{9,1... | collective-permute-start | bytes 786440 | tf_op jit(solution)/shard_map/ppermute | solution.py:985
  98.3 1.1 collective-permute-done.28.refs_6_
  100.1 3.4 %collective-permute-start.39 = (bf16[9,32,512]{2,1,0:T(8,128)(2,1)S(1)}, bf16[9,32,512]{2,1,0:T(8,128)(2,1)S(1)}, u32[]{:S(2)}, u32[]{:S(2)}) collective-permute-start(bf16[9,32,512]{2,1,0:T(8,128)(2,1)S(1)} %get-tuple-element.277.refs_1_), channel_id=1, source_target_pairs={{0,16},{16,0},{1,17},{17,1},{2,18},{18,2},{3,19},{19,3},{4,20},{20... | collective-permute-start | bytes 884744 | tf_op jit(solution)/shard_map/ppermute | solution.py:985
  103.5 0.7 join_kernel.5
  104.2 1.2 collective-permute-start.37
  105.4 1.1 collective-permute-start.38
  106.4 1.3 collective-permute-start.36
  108.3 2.0 %finish_kernel.3 = (f32[9,256,512]{2,1,0:T(8,128)}, f32[8,128]{1,0:T(8,128)S(1)}) custom-call(s32[5]{0:T(128)S(1)} %stack.23.refs_0_, bf16[4,128,512]{2,1,0:T(8,128)(2,1)S(1)} %get-tuple-element.272.refs_1_, bf16[3,128,512]{2,1,0:T(8,128)(2,1)S(1)} %get-tuple-element.273.refs_2_, bf16[3,128,512]{2,1,0:T(8,128)(2,1)S(1)} %get-tuple-element.274.refs_3_, ...), custom_call_target="tpu_custom_call" | custom-call | flops 1024 | bytes 1024 | tf_op jit(solution)/shard_map/finish_kernel/pallas_call | solution.py:944
  110.3 7.2 %collective-permute-done.39.refs_2_ = bf16[9,32,512]{2,1,0:T(8,128)(2,1)S(1)} collective-permute-done((bf16[9,32,512]{2,1,0:T(8,128)(2,1)S(1)}, bf16[9,32,512]{2,1,0:T(8,128)(2,1)S(1)}, u32[]{:S(2)}, u32[]{:S(2)}) %collective-permute-start.39) | collective-permute-done | bytes 294944 | tf_op jit(solution)/shard_map/ppermute | solution.py:985
  117.6 0.6 total_kernel.3
  118.3 1.1 collective-permute-start.41
  119.9 3.5 %collective-permute-done.38.refs_4_.refs_3_ = bf16[3,128,512]{2,1,0:T(8,128)(2,1)S(1)} collective-permute-done((bf16[3,128,512]{2,1,0:T(8,128)(2,1)S(1)}, bf16[3,128,512]{2,1,0:T(8,128)(2,1)S(1)}, u32[]{:S(2)}, u32[]{:S(2)}) %collective-permute-start.38) | collective-permute-done | bytes 393248 | tf_op jit(solution)/shard_map/ppermute | solution.py:985
  125.0 1.2 collective-permute-start.43
  126.2 0.9 collective-permute-start.44
  127.1 1.4 collective-permute-start.45
  128.5 2.0 %finish_kernel.4 = (f32[9,256,512]{2,1,0:T(8,128)}, f32[8,128]{1,0:T(8,128)S(1)}) custom-call(s32[5]{0:T(128)S(1)} %stack.23.refs_0_, bf16[4,128,512]{2,1,0:T(8,128)(2,1)S(1)} %collective-permute-done.36.refs_2_.refs_1_, bf16[3,128,512]{2,1,0:T(8,128)(2,1)S(1)} %collective-permute-done.37.refs_3_.refs_2_, ...), custom_call_target="tpu_custom_call", output_to_operand_aliasing={{0}: (4, {})} | custom-call | flops 1024 | bytes 1024 | tf_op jit(solution)/shard_map/finish_kernel/pallas_call | solution.py:944
  130.6 3.1 %spread_kernel.1 = (f32[512,256]{1,0:T(8,128)}, f32[512,256]{1,0:T(8,128)}, f32[512,256]{1,0:T(8,128)}, f32[1,256]{1,0:T(1,128)}, f32[1,256]{1,0:T(1,128)}, /*in...) custom-call(s32[5]{0:T(128)S(1)} %stack.23.refs_0_, ...), custom_call_target="tpu_custom_call" | custom-call | flops 1024 | bytes 1024 | tf_op jit(solution)/shard_map/spread_kernel/pallas_call | solution.py:944
  133.7 0.7 join_kernel.7
  134.4 0.7 collective-permute-start.46
  135.1 1.0 collective-permute-start.47
  136.1 1.0 collective-permute-start.48
  137.1 2.0 %finish_kernel.5 = (f32[9,256,512]{2,1,0:T(8,128)}, f32[8,128]{1,0:T(8,128)S(1)}) custom-call(s32[5]{0:T(128)S(1)} %stack.23.refs_0_, bf16[3,128,512]{2,1,0:T(8,128)(2,1)S(1)} %get-tuple-element.296.refs_1_, bf16[3,128,512]{2,1,0:T(8,128)(2,1)S(1)} %get-tuple-element.297.refs_2_, bf16[3,128,512]{2,1,0:T(8,128)(2,1)S(1)} %get-tuple-element.298.refs_3_, ...), custom_call_target="tpu_custom_call" | custom-call | flops 1024 | bytes 1024 | tf_op jit(solution)/shard_map/finish_kernel/pallas_call | solution.py:944
  139.1 4.0 %collective-permute-done.46.refs_1_ = bf16[3,128,512]{2,1,0:T(8,128)(2,1)S(1)} collective-permute-done((bf16[3,128,512]{2,1,0:T(8,128)(2,1)S(1)}, bf16[3,128,512]{2,1,0:T(8,128)(2,1)S(1)}, u32[]{:S(2)}, u32[]{:S(2)}) %collective-permute-start.46) | collective-permute-done | bytes 393248 | tf_op jit(solution)/shard_map/ppermute | solution.py:985
  143.5 0.7 collective-permute-done.48.refs_3_
  144.1 2.6 %finish_scalars_kernel.1 = (f32[9,256,512]{2,1,0:T(8,128)}, f32[2]{0:T(128)}, f32[3]{0:T(128)}, f32[3]{0:T(128)}, f32[8,128]{1,0:T(8,128)}) custom-call(s32[5]{0:T(128)S(1)} %stack.23.refs_0_, bf16[3,128,512]{2,1,0:T(8,128)(2,1)S(1)} %collective-permute-done.46.refs_1_, ...), custom_call_target="tpu_custom_call", output_to_operand_aliasing={{0}: (4, {})} | custom-call | flops 1024 | bytes 1024 | tf_op jit(solution)/shard_map/finish_scalars_kernel/pallas_call | solution.py:944
  (85 shorter events, 12.7 us)
Async XLA Ops:
  0.7 3.4 %copy-start.1 = (bf16[3,3,256,512]{3,2,1,0:T(8,128)(2,1)S(1)}, bf16[3,3,256,512]{3,2,1,0:T(8,128)(2,1)}, u32[]{:S(2)}) copy-start(bf16[3,3,256,512]{3,2,1,0:T(8,128)(2,1)} %param.31) | copy-start | bytes 7077892
  3.5 6.6 %collective-permute-start.1 = (bf16[9,256,256]{2,1,0:T(8,128)(2,1)S(1)}, bf16[9,256,256]{2,1,0:T(8,128)(2,1)S(1)}, u32[]{:S(2)}, u32[]{:S(2)}) collective-permute-start(bf16[9,256,256]{2,1,0:T(8,128)(2,1)S(1)} %get-tuple-element.166), channel_id=1, source_target_pairs={{0,1},{1,0},{2,3},{3,2},{4,5},{5,4},{6,7},{7,6},{8,9},{9,8},{10,11... | collective-permute-start | bytes 3538952 | tf_op jit(solution)/shard_map/ppermute | solution.py:985
  4.0 6.1 %collective-permute-start = (bf16[2,256,256]{2,1,0:T(8,128)(2,1)S(1)}, bf16[2,256,256]{2,1,0:T(8,128)(2,1)S(1)}, u32[]{:S(2)}, u32[]{:S(2)}) collective-permute-start(bf16[2,256,256]{2,1,0:T(8,128)(2,1)S(1)} %get-tuple-element.165.refs_1_), channel_id=1, source_target_pairs={{0,1},{1,0},{2,3},{3,2},{4,5},{5,4},{6,7},{7,6},{8,9},{9,8},{10,11... | collective-permute-start | bytes 786440 | tf_op jit(solution)/shard_map/ppermute | solution.py:985
  6.1 4.0 %collective-permute-start.2 = (f32[2,256]{1,0:T(2,128)S(1)}, f32[2,256]{1,0:T(2,128)S(1)}, u32[]{:S(2)}, u32[]{:S(2)}) collective-permute-start(f32[2,256]{1,0:T(2,128)S(1)} %get-tuple-element.170), channel_id=1, source_target_pairs={{0,1},{1,0},{2,3},{3,2},{4,5},{5,4},{6,7},{7,6},{8,9},{9,8},{10,11... | collective-permute-start | bytes 6152 | tf_op jit(solution)/shard_map/ppermute | solution.py:985
  9.9 5.1 %collective-permute-start.4 = (bf16[9,256,256]{2,1,0:T(8,128)(2,1)S(1)}, bf16[9,256,256]{2,1,0:T(8,128)(2,1)S(1)}, u32[]{:S(2)}, u32[]{:S(2)}) collective-permute-start(bf16[9,256,256]{2,1,0:T(8,128)(2,1)S(1)} %get-tuple-element.176), channel_id=1, source_target_pairs={{0,1},{1,0},{2,3},{3,2},{4,5},{5,4},{6,7},{7,6},{8,9},{9,8},{10,11... | collective-permute-start | bytes 3538952 | tf_op jit(solution)/shard_map/ppermute | solution.py:985
  10.1 3.3 %copy-start = (bf16[3,3,256,512]{3,2,1,0:T(8,128)(2,1)S(1)}, bf16[3,3,256,512]{3,2,1,0:T(8,128)(2,1)}, u32[]{:S(2)}) copy-start(bf16[3,3,256,512]{3,2,1,0:T(8,128)(2,1)} %param.33) | copy-start | bytes 7077892
  12.9 3.2 %copy-start.2 = (bf16[2,32,32,256]{3,2,1,0:T(8,128)(2,1)S(1)}, bf16[2,32,32,256]{3,2,1,0:T(8,128)(2,1)}, u32[]{:S(2)}) copy-start(bf16[2,32,32,256]{3,2,1,0:T(8,128)(2,1)} %refs_6_.3) | copy-start | bytes 3145732
  12.9 3.2 %collective-permute-start.3 = (bf16[2,4,256,256]{3,2,1,0:T(8,128)(2,1)S(1)}, bf16[2,4,256,256]{3,2,1,0:T(8,128)(2,1)S(1)}, u32[]{:S(2)}, u32[]{:S(2)}) collective-permute-start(bf16[2,4,256,256]{3,2,1,0:T(8,128)(2,1)S(1)} %get-tuple-element.175.refs_1_.refs_0_), channel_id=1, source_target_pairs={{0,1},{1,0},{2,3},{3,2},{4,5},{5,4},{6,7},{7,6},{8,9},{9,8},{10,11... | collective-permute-start | bytes 3145736 | tf_op jit(solution)/shard_map/ppermute | solution.py:985
  14.9 1.2 collective-permute-start.5
  23.1 2.7 %collective-permute-start.6 = (bf16[2064,256]{1,0:T(8,128)(2,1)S(1)}, bf16[2064,256]{1,0:T(8,128)(2,1)S(1)}, u32[]{:S(2)}, u32[]{:S(2)}) collective-permute-start(bf16[2064,256]{1,0:T(8,128)(2,1)S(1)} %get-tuple-element.189.refs_3_.refs_1_), channel_id=1, source_target_pairs={{0,1},{1,0},{2,3},{3,2},{4,5},{5,4},{6,7},{7,6},{8,9},{9,8},{10,11... | collective-permute-start | bytes 3170312 | tf_op jit(solution)/shard_map/ppermute | solution.py:985
  32.3 14.6 %collective-permute-start.7 = (bf16[3,128,512]{2,1,0:T(8,128)(2,1)S(1)}, bf16[3,128,512]{2,1,0:T(8,128)(2,1)S(1)}, u32[]{:S(2)}, u32[]{:S(2)}) collective-permute-start(bf16[3,128,512]{2,1,0:T(8,128)(2,1)S(1)} %get-tuple-element.192), channel_id=1, source_target_pairs={{0,2},{2,0},{1,3},{3,1},{4,6},{6,4},{5,7},{7,5},{8,10},{10,8},{9,1... | collective-permute-start | bytes 1179656 | tf_op jit(solution)/shard_map/ppermute | solution.py:985
  35.0 11.9 %collective-permute-start.8 = (bf16[3,128,512]{2,1,0:T(8,128)(2,1)S(1)}, bf16[3,128,512]{2,1,0:T(8,128)(2,1)S(1)}, u32[]{:S(2)}, u32[]{:S(2)}) collective-permute-start(bf16[3,128,512]{2,1,0:T(8,128)(2,1)S(1)} %get-tuple-element.194), channel_id=1, source_target_pairs={{0,4},{4,0},{1,5},{5,1},{2,6},{6,2},{3,7},{7,3},{8,12},{12,8},{9,1... | collective-permute-start | bytes 1179656 | tf_op jit(solution)/shard_map/ppermute | solution.py:985
  36.5 10.8 %collective-permute-start.9 = (bf16[3,128,512]{2,1,0:T(8,128)(2,1)S(1)}, bf16[3,128,512]{2,1,0:T(8,128)(2,1)S(1)}, u32[]{:S(2)}, u32[]{:S(2)}) collective-permute-start(bf16[3,128,512]{2,1,0:T(8,128)(2,1)S(1)} %get-tuple-element.196), channel_id=1, source_target_pairs={{0,8},{8,0},{1,9},{9,1},{2,10},{10,2},{3,11},{11,3},{4,12},{12,4},... | collective-permute-start | bytes 1179656 | tf_op jit(solution)/shard_map/ppermute | solution.py:985
  47.3 3.7 %copy-start.4 = (bf16[3,256]{1,0:T(4,128)(2,1)S(1)}, bf16[3,256]{1,0:T(4,128)(2,1)}, u32[]{:S(2)}) copy-start(bf16[3,256]{1,0:T(4,128)(2,1)} %refs_4_.6) | copy-start | bytes 4612
  48.3 8.8 %collective-permute-start.12 = (bf16[3,64,512]{2,1,0:T(8,128)(2,1)S(1)}, bf16[3,64,512]{2,1,0:T(8,128)(2,1)S(1)}, u32[]{:S(2)}, u32[]{:S(2)}) collective-permute-start(bf16[3,64,512]{2,1,0:T(8,128)(2,1)S(1)} %get-tuple-element.208), channel_id=1, source_target_pairs={{0,4},{4,0},{1,5},{5,1},{2,6},{6,2},{3,7},{7,3},{8,12},{12,8},{9,1... | collective-permute-start | bytes 589832 | tf_op jit(solution)/shard_map/ppermute | solution.py:985
  48.9 8.3 %collective-permute-start.13 = (bf16[3,64,512]{2,1,0:T(8,128)(2,1)S(1)}, bf16[3,64,512]{2,1,0:T(8,128)(2,1)S(1)}, u32[]{:S(2)}, u32[]{:S(2)}) collective-permute-start(bf16[3,64,512]{2,1,0:T(8,128)(2,1)S(1)} %get-tuple-element.210), channel_id=1, source_target_pairs={{0,8},{8,0},{1,9},{9,1},{2,10},{10,2},{3,11},{11,3},{4,12},{12,4},... | collective-permute-start | bytes 589832 | tf_op jit(solution)/shard_map/ppermute | solution.py:985
  50.4 6.7 %collective-permute-start.14 = (bf16[3,64,512]{2,1,0:T(8,128)(2,1)S(1)}, bf16[3,64,512]{2,1,0:T(8,128)(2,1)S(1)}, u32[]{:S(2)}, u32[]{:S(2)}) collective-permute-start(bf16[3,64,512]{2,1,0:T(8,128)(2,1)S(1)} %get-tuple-element.212), channel_id=1, source_target_pairs={{0,2},{2,0},{1,3},{3,1},{4,6},{6,4},{5,7},{7,5},{8,10},{10,8},{9,1... | collective-permute-start | bytes 589832 | tf_op jit(solution)/shard_map/ppermute | solution.py:985
  51.0 10.4 %collective-permute-start.11 = (bf16[2064,256]{1,0:T(8,128)(2,1)S(1)}, bf16[2064,256]{1,0:T(8,128)(2,1)S(1)}, u32[]{:S(2)}, u32[]{:S(2)}) collective-permute-start(bf16[2064,256]{1,0:T(8,128)(2,1)S(1)} %get-tuple-element.206.refs_2_.refs_1_), channel_id=1, source_target_pairs={{0,1},{1,0},{2,3},{3,2},{4,5},{5,4},{6,7},{7,6},{8,9},{9,8},{10,11... | collective-permute-start | bytes 3170312 | tf_op jit(solution)/shard_map/ppermute | solution.py:985
  56.7 4.8 %collective-permute-start.10 = (f32[2,4,8,256]{3,2,1,0:T(8,128)S(1)}, f32[2,4,8,256]{3,2,1,0:T(8,128)S(1)}, u32[]{:S(2)}, u32[]{:S(2)}) collective-permute-start(f32[2,4,8,256]{3,2,1,0:T(8,128)S(1)} %get-tuple-element.205.refs_2_), channel_id=1, source_target_pairs={{0,1},{1,0},{2,3},{3,2},{4,5},{5,4},{6,7},{7,6},{8,9},{9,8},{10,11... | collective-permute-start | bytes 196616 | tf_op jit(solution)/shard_map/ppermute | solution.py:985
  57.9 7.3 %collective-permute-start.15 = (bf16[3,32,512]{2,1,0:T(8,128)(2,1)S(1)}, bf16[3,32,512]{2,1,0:T(8,128)(2,1)S(1)}, u32[]{:S(2)}, u32[]{:S(2)}) collective-permute-start(bf16[3,32,512]{2,1,0:T(8,128)(2,1)S(1)} %get-tuple-element.215), channel_id=1, source_target_pairs={{0,8},{8,0},{1,9},{9,1},{2,10},{10,2},{3,11},{11,3},{4,12},{12,4},... | collective-permute-start | bytes 294920 | tf_op jit(solution)/shard_map/ppermute | solution.py:985
  58.2 8.7 %collective-permute-start.16 = (bf16[3,32,512]{2,1,0:T(8,128)(2,1)S(1)}, bf16[3,32,512]{2,1,0:T(8,128)(2,1)S(1)}, u32[]{:S(2)}, u32[]{:S(2)}) collective-permute-start(bf16[3,32,512]{2,1,0:T(8,128)(2,1)S(1)} %get-tuple-element.217), channel_id=1, source_target_pairs={{0,2},{2,0},{1,3},{3,1},{4,6},{6,4},{5,7},{7,5},{8,10},{10,8},{9,1... | collective-permute-start | bytes 294920 | tf_op jit(solution)/shard_map/ppermute | solution.py:985
  59.9 7.1 %collective-permute-start.17 = (bf16[3,32,512]{2,1,0:T(8,128)(2,1)S(1)}, bf16[3,32,512]{2,1,0:T(8,128)(2,1)S(1)}, u32[]{:S(2)}, u32[]{:S(2)}) collective-permute-start(bf16[3,32,512]{2,1,0:T(8,128)(2,1)S(1)} %get-tuple-element.219), channel_id=1, source_target_pairs={{0,4},{4,0},{1,5},{5,1},{2,6},{6,2},{3,7},{7,3},{8,12},{12,8},{9,1... | collective-permute-start | bytes 294920 | tf_op jit(solution)/shard_map/ppermute | solution.py:985
  64.3 16.0 %collective-permute-start.18 = (bf16[3,128,512]{2,1,0:T(8,128)(2,1)S(1)}, bf16[3,128,512]{2,1,0:T(8,128)(2,1)S(1)}, u32[]{:S(2)}, u32[]{:S(2)}) collective-permute-start(bf16[3,128,512]{2,1,0:T(8,128)(2,1)S(1)} %get-tuple-element.237), channel_id=1, source_target_pairs={{0,2},{2,0},{1,3},{3,1},{4,6},{6,4},{5,7},{7,5},{8,10},{10,8},{9,1... | collective-permute-start | bytes 1179656 | tf_op jit(solution)/shard_map/ppermute | solution.py:985
  64.9 15.4 %collective-permute-start.19 = (bf16[3,128,512]{2,1,0:T(8,128)(2,1)S(1)}, bf16[3,128,512]{2,1,0:T(8,128)(2,1)S(1)}, u32[]{:S(2)}, u32[]{:S(2)}) collective-permute-start(bf16[3,128,512]{2,1,0:T(8,128)(2,1)S(1)} %get-tuple-element.239), channel_id=1, source_target_pairs={{0,4},{4,0},{1,5},{5,1},{2,6},{6,2},{3,7},{7,3},{8,12},{12,8},{9,1... | collective-permute-start | bytes 1179656 | tf_op jit(solution)/shard_map/ppermute | solution.py:985
  65.2 16.0 %collective-permute-start.20 = (bf16[3,128,512]{2,1,0:T(8,128)(2,1)S(1)}, bf16[3,128,512]{2,1,0:T(8,128)(2,1)S(1)}, u32[]{:S(2)}, u32[]{:S(2)}) collective-permute-start(bf16[3,128,512]{2,1,0:T(8,128)(2,1)S(1)} %get-tuple-element.241), channel_id=1, source_target_pairs={{0,8},{8,0},{1,9},{9,1},{2,10},{10,2},{3,11},{11,3},{4,12},{12,4},... | collective-permute-start | bytes 1179656 | tf_op jit(solution)/shard_map/ppermute | solution.py:985
  67.6 17.6 %collective-permute-start.24 = (bf16[9,32,512]{2,1,0:T(8,128)(2,1)S(1)}, bf16[9,32,512]{2,1,0:T(8,128)(2,1)S(1)}, u32[]{:S(2)}, u32[]{:S(2)}) collective-permute-start(bf16[9,32,512]{2,1,0:T(8,128)(2,1)S(1)} %get-tuple-element.249.refs_1_), channel_id=1, source_target_pairs={{0,16},{16,0},{1,17},{17,1},{2,18},{18,2},{3,19},{19,3},{4,20},{20... | collective-permute-start | bytes 884744 | tf_op jit(solution)/shard_map/ppermute | solution.py:985
  70.2 6.3 %copy-start.3 = (bf16[2,512]{1,0:T(2,128)(2,1)S(1)}, bf16[2,512]{1,0:T(2,128)(2,1)}, u32[]{:S(2)}) copy-start(bf16[2,512]{1,0:T(2,128)(2,1)} %refs_14_.1) | copy-start | bytes 6148
  79.9 5.3 %collective-permute-start.25 = (f32[16,256]{1,0:T(8,128)S(1)}, f32[16,256]{1,0:T(8,128)S(1)}, u32[]{:S(2)}, u32[]{:S(2)}) collective-permute-start(f32[16,256]{1,0:T(8,128)S(1)} %get-tuple-element.250.refs_3_), channel_id=1, source_target_pairs={{0,16},{16,0},{1,17},{17,1},{2,18},{18,2},{3,19},{19,3},{4,20},{20... | collective-permute-start | bytes 49160 | tf_op jit(solution)/shard_map/ppermute | solution.py:985
  82.0 6.5 %collective-permute-start.21 = (bf16[3,64,512]{2,1,0:T(8,128)(2,1)S(1)}, bf16[3,64,512]{2,1,0:T(8,128)(2,1)S(1)}, u32[]{:S(2)}, u32[]{:S(2)}) collective-permute-start(bf16[3,64,512]{2,1,0:T(8,128)(2,1)S(1)} %get-tuple-element.244), channel_id=1, source_target_pairs={{0,4},{4,0},{1,5},{5,1},{2,6},{6,2},{3,7},{7,3},{8,12},{12,8},{9,1... | collective-permute-start | bytes 589832 | tf_op jit(solution)/shard_map/ppermute | solution.py:985
  83.7 5.7 %collective-permute-start.22 = (bf16[3,64,512]{2,1,0:T(8,128)(2,1)S(1)}, bf16[3,64,512]{2,1,0:T(8,128)(2,1)S(1)}, u32[]{:S(2)}, u32[]{:S(2)}) collective-permute-start(bf16[3,64,512]{2,1,0:T(8,128)(2,1)S(1)} %get-tuple-element.246), channel_id=1, source_target_pairs={{0,8},{8,0},{1,9},{9,1},{2,10},{10,2},{3,11},{11,3},{4,12},{12,4},... | collective-permute-start | bytes 589832 | tf_op jit(solution)/shard_map/ppermute | solution.py:985
  83.7 6.3 %collective-permute-start.23 = (bf16[3,64,512]{2,1,0:T(8,128)(2,1)S(1)}, bf16[3,64,512]{2,1,0:T(8,128)(2,1)S(1)}, u32[]{:S(2)}, u32[]{:S(2)}) collective-permute-start(bf16[3,64,512]{2,1,0:T(8,128)(2,1)S(1)} %get-tuple-element.248), channel_id=1, source_target_pairs={{0,2},{2,0},{1,3},{3,1},{4,6},{6,4},{5,7},{7,5},{8,10},{10,8},{9,1... | collective-permute-start | bytes 589832 | tf_op jit(solution)/shard_map/ppermute | solution.py:985
  85.9 7.9 %collective-permute-start.30 = (bf16[3,32,512]{2,1,0:T(8,128)(2,1)S(1)}, bf16[3,32,512]{2,1,0:T(8,128)(2,1)S(1)}, u32[]{:S(2)}, u32[]{:S(2)}) collective-permute-start(bf16[3,32,512]{2,1,0:T(8,128)(2,1)S(1)} %get-tuple-element.260.refs_3_), channel_id=1, source_target_pairs={{0,2},{2,0},{1,3},{3,1},{4,6},{6,4},{5,7},{7,5},{8,10},{10,8},{9,1... | collective-permute-start | bytes 294920 | tf_op jit(solution)/shard_map/ppermute | solution.py:985
  87.0 7.4 %collective-permute-start.31 = (bf16[3,32,512]{2,1,0:T(8,128)(2,1)S(1)}, bf16[3,32,512]{2,1,0:T(8,128)(2,1)S(1)}, u32[]{:S(2)}, u32[]{:S(2)}) collective-permute-start(bf16[3,32,512]{2,1,0:T(8,128)(2,1)S(1)} %get-tuple-element.261.refs_5_), channel_id=1, source_target_pairs={{0,4},{4,0},{1,5},{5,1},{2,6},{6,2},{3,7},{7,3},{8,12},{12,8},{9,1... | collective-permute-start | bytes 294920 | tf_op jit(solution)/shard_map/ppermute | solution.py:985
  88.5 5.8 %collective-permute-start.29 = (bf16[4,32,512]{2,1,0:T(8,128)(2,1)S(1)}, bf16[4,32,512]{2,1,0:T(8,128)(2,1)S(1)}, u32[]{:S(2)}, u32[]{:S(2)}) collective-permute-start(bf16[4,32,512]{2,1,0:T(8,128)(2,1)S(1)} %get-tuple-element.259.refs_1_), channel_id=1, source_target_pairs={{0,8},{8,0},{1,9},{9,1},{2,10},{10,2},{3,11},{11,3},{4,12},{12,4},... | collective-permute-start | bytes 393224 | tf_op jit(solution)/shard_map/ppermute | solution.py:985
  90.7 5.7 %collective-permute-start.26 = (bf16[3,32,512]{2,1,0:T(8,128)(2,1)S(1)}, bf16[3,32,512]{2,1,0:T(8,128)(2,1)S(1)}, u32[]{:S(2)}, u32[]{:S(2)}) collective-permute-start(bf16[3,32,512]{2,1,0:T(8,128)(2,1)S(1)} %get-tuple-element.254), channel_id=1, source_target_pairs={{0,8},{8,0},{1,9},{9,1},{2,10},{10,2},{3,11},{11,3},{4,12},{12,4},... | collective-permute-start | bytes 294920 | tf_op jit(solution)/shard_map/ppermute | solution.py:985
  92.2 6.1 %collective-permute-start.27 = (bf16[3,32,512]{2,1,0:T(8,128)(2,1)S(1)}, bf16[3,32,512]{2,1,0:T(8,128)(2,1)S(1)}, u32[]{:S(2)}, u32[]{:S(2)}) collective-permute-start(bf16[3,32,512]{2,1,0:T(8,128)(2,1)S(1)} %get-tuple-element.256), channel_id=1, source_target_pairs={{0,2},{2,0},{1,3},{3,1},{4,6},{6,4},{5,7},{7,5},{8,10},{10,8},{9,1... | collective-permute-start | bytes 294920 | tf_op jit(solution)/shard_map/ppermute | solution.py:985
  93.8 5.6 %collective-permute-start.28 = (bf16[3,32,512]{2,1,0:T(8,128)(2,1)S(1)}, bf16[3,32,512]{2,1,0:T(8,128)(2,1)S(1)}, u32[]{:S(2)}, u32[]{:S(2)}) collective-permute-start(bf16[3,32,512]{2,1,0:T(8,128)(2,1)S(1)} %get-tuple-element.258), channel_id=1, source_target_pairs={{0,4},{4,0},{1,5},{5,1},{2,6},{6,2},{3,7},{7,3},{8,12},{12,8},{9,1... | collective-permute-start | bytes 294920 | tf_op jit(solution)/shard_map/ppermute | solution.py:985
  95.0 8.6 %collective-permute-start.34 = (bf16[3,64,512]{2,1,0:T(8,128)(2,1)S(1)}, bf16[3,64,512]{2,1,0:T(8,128)(2,1)S(1)}, u32[]{:S(2)}, u32[]{:S(2)}) collective-permute-start(bf16[3,64,512]{2,1,0:T(8,128)(2,1)S(1)} %get-tuple-element.267.refs_3_), channel_id=1, source_target_pairs={{0,8},{8,0},{1,9},{9,1},{2,10},{10,2},{3,11},{11,3},{4,12},{12,4},... | collective-permute-start | bytes 589832 | tf_op jit(solution)/shard_map/ppermute | solution.py:985
  95.9 7.6 %collective-permute-start.35 = (bf16[3,64,512]{2,1,0:T(8,128)(2,1)S(1)}, bf16[3,64,512]{2,1,0:T(8,128)(2,1)S(1)}, u32[]{:S(2)}, u32[]{:S(2)}) collective-permute-start(bf16[3,64,512]{2,1,0:T(8,128)(2,1)S(1)} %get-tuple-element.268.refs_5_), channel_id=1, source_target_pairs={{0,2},{2,0},{1,3},{3,1},{4,6},{6,4},{5,7},{7,5},{8,10},{10,8},{9,1... | collective-permute-start | bytes 589832 | tf_op jit(solution)/shard_map/ppermute | solution.py:985
  96.5 7.1 %collective-permute-start.33 = (bf16[4,64,512]{2,1,0:T(8,128)(2,1)S(1)}, bf16[4,64,512]{2,1,0:T(8,128)(2,1)S(1)}, u32[]{:S(2)}, u32[]{:S(2)}) collective-permute-start(bf16[4,64,512]{2,1,0:T(8,128)(2,1)S(1)} %get-tuple-element.266.refs_1_), channel_id=1, source_target_pairs={{0,4},{4,0},{1,5},{5,1},{2,6},{6,2},{3,7},{7,3},{8,12},{12,8},{9,1... | collective-permute-start | bytes 786440 | tf_op jit(solution)/shard_map/ppermute | solution.py:985
  100.0 7.7 %collective-permute-start.32 = (f32[8,256]{1,0:T(8,128)S(1)}, f32[8,256]{1,0:T(8,128)S(1)}, u32[]{:S(2)}, u32[]{:S(2)}) collective-permute-start(f32[8,256]{1,0:T(8,128)S(1)} %get-tuple-element.265), channel_id=1, source_target_pairs={{0,1},{1,0},{2,3},{3,2},{4,5},{5,4},{6,7},{7,6},{8,9},{9,8},{10,11... | collective-permute-start | bytes 24584 | tf_op jit(solution)/shard_map/ppermute | solution.py:985
  100.1 17.5 %collective-permute-start.39 = (bf16[9,32,512]{2,1,0:T(8,128)(2,1)S(1)}, bf16[9,32,512]{2,1,0:T(8,128)(2,1)S(1)}, u32[]{:S(2)}, u32[]{:S(2)}) collective-permute-start(bf16[9,32,512]{2,1,0:T(8,128)(2,1)S(1)} %get-tuple-element.277.refs_1_), channel_id=1, source_target_pairs={{0,16},{16,0},{1,17},{17,1},{2,18},{18,2},{3,19},{19,3},{4,20},{20... | collective-permute-start | bytes 884744 | tf_op jit(solution)/shard_map/ppermute | solution.py:985
  104.2 15.2 %collective-permute-start.37 = (bf16[3,128,512]{2,1,0:T(8,128)(2,1)S(1)}, bf16[3,128,512]{2,1,0:T(8,128)(2,1)S(1)}, u32[]{:S(2)}, u32[]{:S(2)}) collective-permute-start(bf16[3,128,512]{2,1,0:T(8,128)(2,1)S(1)} %get-tuple-element.273.refs_2_), channel_id=1, source_target_pairs={{0,4},{4,0},{1,5},{5,1},{2,6},{6,2},{3,7},{7,3},{8,12},{12,8},{9,1... | collective-permute-start | bytes 1179656 | tf_op jit(solution)/shard_map/ppermute | solution.py:985
  105.4 18.0 %collective-permute-start.38 = (bf16[3,128,512]{2,1,0:T(8,128)(2,1)S(1)}, bf16[3,128,512]{2,1,0:T(8,128)(2,1)S(1)}, u32[]{:S(2)}, u32[]{:S(2)}) collective-permute-start(bf16[3,128,512]{2,1,0:T(8,128)(2,1)S(1)} %get-tuple-element.274.refs_3_), channel_id=1, source_target_pairs={{0,8},{8,0},{1,9},{9,1},{2,10},{10,2},{3,11},{11,3},{4,12},{12,4},... | collective-permute-start | bytes 1179656 | tf_op jit(solution)/shard_map/ppermute | solution.py:985
  106.4 16.9 %collective-permute-start.36 = (bf16[4,128,512]{2,1,0:T(8,128)(2,1)S(1)}, bf16[4,128,512]{2,1,0:T(8,128)(2,1)S(1)}, u32[]{:S(2)}, u32[]{:S(2)}) collective-permute-start(bf16[4,128,512]{2,1,0:T(8,128)(2,1)S(1)} %get-tuple-element.272.refs_1_), channel_id=1, source_target_pairs={{0,2},{2,0},{1,3},{3,1},{4,6},{6,4},{5,7},{7,5},{8,10},{10,8},{9,1... | collective-permute-start | bytes 1572872 | tf_op jit(solution)/shard_map/ppermute | solution.py:985
  118.2 6.2 %collective-permute-start.40 = (bf16[3,32,512]{2,1,0:T(8,128)(2,1)S(1)}, bf16[3,32,512]{2,1,0:T(8,128)(2,1)S(1)}, u32[]{:S(2)}, u32[]{:S(2)}) collective-permute-start(bf16[3,32,512]{2,1,0:T(8,128)(2,1)S(1)} %get-tuple-element.279.refs_1_), channel_id=1, source_target_pairs={{0,8},{8,0},{1,9},{9,1},{2,10},{10,2},{3,11},{11,3},{4,12},{12,4},... | collective-permute-start | bytes 294920 | tf_op jit(solution)/shard_map/ppermute | solution.py:985
  118.3 6.1 %collective-permute-start.41 = (bf16[3,32,512]{2,1,0:T(8,128)(2,1)S(1)}, bf16[3,32,512]{2,1,0:T(8,128)(2,1)S(1)}, u32[]{:S(2)}, u32[]{:S(2)}) collective-permute-start(bf16[3,32,512]{2,1,0:T(8,128)(2,1)S(1)} %get-tuple-element.280.refs_3_), channel_id=1, source_target_pairs={{0,2},{2,0},{1,3},{3,1},{4,6},{6,4},{5,7},{7,5},{8,10},{10,8},{9,1... | collective-permute-start | bytes 294920 | tf_op jit(solution)/shard_map/ppermute | solution.py:985
  119.4 5.0 %collective-permute-start.42 = (bf16[3,32,512]{2,1,0:T(8,128)(2,1)S(1)}, bf16[3,32,512]{2,1,0:T(8,128)(2,1)S(1)}, u32[]{:S(2)}, u32[]{:S(2)}) collective-permute-start(bf16[3,32,512]{2,1,0:T(8,128)(2,1)S(1)} %get-tuple-element.281.refs_5_), channel_id=1, source_target_pairs={{0,4},{4,0},{1,5},{5,1},{2,6},{6,2},{3,7},{7,3},{8,12},{12,8},{9,1... | collective-permute-start | bytes 294920 | tf_op jit(solution)/shard_map/ppermute | solution.py:985
  125.0 8.6 %collective-permute-start.43 = (bf16[3,64,512]{2,1,0:T(8,128)(2,1)S(1)}, bf16[3,64,512]{2,1,0:T(8,128)(2,1)S(1)}, u32[]{:S(2)}, u32[]{:S(2)}) collective-permute-start(bf16[3,64,512]{2,1,0:T(8,128)(2,1)S(1)} %get-tuple-element.292.refs_1_), channel_id=1, source_target_pairs={{0,4},{4,0},{1,5},{5,1},{2,6},{6,2},{3,7},{7,3},{8,12},{12,8},{9,1... | collective-permute-start | bytes 589832 | tf_op jit(solution)/shard_map/ppermute | solution.py:985
  126.2 7.5 %collective-permute-start.44 = (bf16[3,64,512]{2,1,0:T(8,128)(2,1)S(1)}, bf16[3,64,512]{2,1,0:T(8,128)(2,1)S(1)}, u32[]{:S(2)}, u32[]{:S(2)}) collective-permute-start(bf16[3,64,512]{2,1,0:T(8,128)(2,1)S(1)} %get-tuple-element.293.refs_3_), channel_id=1, source_target_pairs={{0,8},{8,0},{1,9},{9,1},{2,10},{10,2},{3,11},{11,3},{4,12},{12,4},... | collective-permute-start | bytes 589832 | tf_op jit(solution)/shard_map/ppermute | solution.py:985
  127.1 6.5 %collective-permute-start.45 = (bf16[3,64,512]{2,1,0:T(8,128)(2,1)S(1)}, bf16[3,64,512]{2,1,0:T(8,128)(2,1)S(1)}, u32[]{:S(2)}, u32[]{:S(2)}) collective-permute-start(bf16[3,64,512]{2,1,0:T(8,128)(2,1)S(1)} %get-tuple-element.294.refs_5_), channel_id=1, source_target_pairs={{0,2},{2,0},{1,3},{3,1},{4,6},{6,4},{5,7},{7,5},{8,10},{10,8},{9,1... | collective-permute-start | bytes 589832 | tf_op jit(solution)/shard_map/ppermute | solution.py:985
  134.4 8.8 %collective-permute-start.46 = (bf16[3,128,512]{2,1,0:T(8,128)(2,1)S(1)}, bf16[3,128,512]{2,1,0:T(8,128)(2,1)S(1)}, u32[]{:S(2)}, u32[]{:S(2)}) collective-permute-start(bf16[3,128,512]{2,1,0:T(8,128)(2,1)S(1)} %get-tuple-element.296.refs_1_), channel_id=1, source_target_pairs={{0,2},{2,0},{1,3},{3,1},{4,6},{6,4},{5,7},{7,5},{8,10},{10,8},{9,1... | collective-permute-start | bytes 1179656 | tf_op jit(solution)/shard_map/ppermute | solution.py:985
  135.1 8.4 %collective-permute-start.47 = (bf16[3,128,512]{2,1,0:T(8,128)(2,1)S(1)}, bf16[3,128,512]{2,1,0:T(8,128)(2,1)S(1)}, u32[]{:S(2)}, u32[]{:S(2)}) collective-permute-start(bf16[3,128,512]{2,1,0:T(8,128)(2,1)S(1)} %get-tuple-element.297.refs_2_), channel_id=1, source_target_pairs={{0,4},{4,0},{1,5},{5,1},{2,6},{6,2},{3,7},{7,3},{8,12},{12,8},{9,1... | collective-permute-start | bytes 1179656 | tf_op jit(solution)/shard_map/ppermute | solution.py:985
  136.1 8.1 %collective-permute-start.48 = (bf16[3,128,512]{2,1,0:T(8,128)(2,1)S(1)}, bf16[3,128,512]{2,1,0:T(8,128)(2,1)S(1)}, u32[]{:S(2)}, u32[]{:S(2)}) collective-permute-start(bf16[3,128,512]{2,1,0:T(8,128)(2,1)S(1)} %get-tuple-element.298.refs_3_), channel_id=1, source_target_pairs={{0,8},{8,0},{1,9},{9,1},{2,10},{10,2},{3,11},{11,3},{4,12},{12,4},... | collective-permute-start | bytes 1179656 | tf_op jit(solution)/shard_map/ppermute | solution.py:985
  137.1 2.0 %collective-permute-start.49 = (f32[1,256]{1,0:T(1,128)S(1)}, f32[1,256]{1,0:T(1,128)S(1)}, u32[]{:S(2)}, u32[]{:S(2)}) collective-permute-start(f32[1,256]{1,0:T(1,128)S(1)} %get-tuple-element.301.refs_5_), channel_id=1, source_target_pairs={{0,1},{1,0},{2,3},{3,2},{4,5},{5,4},{6,7},{7,6},{8,9},{9,8},{10,11... | collective-permute-start | bytes 3080 | tf_op jit(solution)/shard_map/ppermute | solution.py:985
